TPU v7x, 32 devices: a whole 2x2x4 slice. The times are simulated.
32 devices in a mesh: vocab: 8 (over z, x), tp: 4 (over y, core).
Axes of the slice: x: 2, y: 2, z: 4, core: 2. Of those that a mesh axis runs over, the one named last changes fastest.
Arguments:
- hidden: bfloat16 [4096, 2048], P('vocab'), may hold values from -28 to 28, as said below
- target_cluster: int32 [4096, 1], P('vocab'), may hold values from 0 to 63; in each aligned block of 512 rows (0 to 511, 512 to 1023, ...) at most 16 rows name the same one
- target_word: int32 [4096], P('vocab'), may hold values from 0 to 8191
- head_words: bfloat16 [2048, 8192], P(None, 'tp'), may hold values from -4 to 4
- head_clusters: bfloat16 [2048, 32], P(None, 'tp'), may hold values from -4 to 4
- proj_one: bfloat16 [8, 2048, 1024], P('vocab'), may hold values from -0.125 to 0.125
- proj_two: bfloat16 [8, 2048, 512], P('vocab'), may hold values from -0.125 to 0.125
- proj_three: bfloat16 [8, 2048, 256], P('vocab'), may hold values from -0.125 to 0.125
- proj_four: bfloat16 [8, 2048, 128], P('vocab'), may hold values from -0.125 to 0.125
- out_one: bfloat16 [8, 1024, 1024], P('vocab', None, 'tp'), may hold values from -4 to 4
- out_two: bfloat16 [8, 512, 2048], P('vocab', None, 'tp'), may hold values from -4 to 4
- out_three: bfloat16 [8, 256, 4096], P('vocab', None, 'tp'), may hold values from -4 to 4
- out_four: bfloat16 [8, 128, 8192], P('vocab', None, 'tp'), may hold values from -4 to 4
Outputs:
- grad_hidden: bfloat16 [4096, 2048], P('vocab', 'tp')
- grad_head_words: bfloat16 [2048, 8192], P('vocab', 'tp')
- grad_head_clusters: bfloat16 [2048, 32], P('vocab', 'tp')
- grad_proj_one: bfloat16 [8, 2048, 1024], P('vocab', 'tp')
- grad_proj_two: bfloat16 [8, 2048, 512], P('vocab', 'tp')
- grad_proj_three: bfloat16 [8, 2048, 256], P('vocab', 'tp')
- grad_proj_four: bfloat16 [8, 2048, 128], P('vocab', 'tp')
- grad_out_one: bfloat16 [8, 1024, 1024], P('vocab', None, 'tp')
- grad_out_two: bfloat16 [8, 512, 2048], P('vocab', None, 'tp')
- grad_out_three: bfloat16 [8, 256, 4096], P('vocab', None, 'tp')
- grad_out_four: bfloat16 [8, 128, 8192], P('vocab', None, 'tp')
Inputs may be any that keep to these rules, and one draw needn't show every extreme that they name: `hidden`: real values of order one, up to a factor that differs between tokens. `target_cluster`: A value below 32 names the tail cluster of the token's word; 32 or more marks a word of the head. Among the 512 tokens of one index of vocab no tail cluster is named more than 16 times. `target_word`: for a tail token only the value modulo its cluster's vocabulary counts.
All inputs are finite; a program needn't handle non-finite values.
Results may differ from a plain program's by a relative error of at most 0.017.
Values may be sent and summed in bfloat16 or wider, within the bound.
No kernel may reach another device: no remote copies, remote signals or barrier semaphores. Data moves between devices by JAX's collectives and lax.ppermute only.
A program may use at most 128 MiB of HBM per device.

v0:
```python
import jax
import jax.numpy as jnp
from jax import lax
from jax.sharding import PartitionSpec as P


def combined_all(value, axis, join):
    pieces = jax.tree.map(lambda part: lax.all_gather(part, axis), value)
    head = jax.tree.map(lambda part: part[0], pieces)
    tail = jax.tree.map(lambda part: part[1:], pieces)
    so_far, _ = lax.scan(lambda so_far, share: (join(so_far, share), None), head, tail)
    return so_far


def online_pair(first, second):
    head_peak = jnp.maximum(first[0], second[0])
    head_total = first[1] * jnp.exp(first[0] - head_peak) + second[1] * jnp.exp(
        second[0] - head_peak
    )
    tail_peak = jnp.maximum(first[2], second[2])
    tail_total = first[3] * jnp.exp(first[2] - tail_peak) + second[3] * jnp.exp(
        second[2] - tail_peak
    )
    return (head_peak, head_total, tail_peak, tail_total)


def body(
    hidden,
    target_cluster,
    target_word,
    head_words,
    head_clusters,
    proj_one,
    proj_two,
    proj_three,
    proj_four,
    out_one,
    out_two,
    out_three,
    out_four,
):
    groups = lax.axis_size("vocab")
    splits = lax.axis_size("tp")
    tp_index = lax.axis_index("tp")
    tok_rows, width = hidden.shape
    capacity = tok_rows // (4 * groups)
    clusters = 4 * groups
    slots = groups * capacity
    word_cols = head_words.shape[1]
    clus_cols = head_clusters.shape[1]
    own_width = width // splits
    logit_words = jnp.dot(hidden, head_words, preferred_element_type=jnp.float32)
    logit_clus = jnp.dot(hidden, head_clusters, preferred_element_type=jnp.float32)
    head_peak = jnp.maximum(jnp.max(logit_words, axis=1), jnp.max(logit_clus, axis=1))
    head_total = jnp.sum(jnp.exp(logit_words - head_peak[:, None]), axis=1) + jnp.sum(
        jnp.exp(logit_clus - head_peak[:, None]), axis=1
    )
    cluster_ids = target_cluster[:, 0]
    tail_mask = cluster_ids < clusters
    band_ids = cluster_ids // groups
    owner_ids = cluster_ids % groups
    member = (cluster_ids[:, None] == jnp.arange(clusters, dtype=jnp.int32)[None, :]).astype(
        jnp.int32
    )
    rank = jnp.sum((jnp.cumsum(member, axis=0) - 1) * member, axis=1)
    flat = jnp.where(tail_mask, owner_ids * 4 * capacity + band_ids * capacity + rank, -1)
    dispatch = jnp.arange(tok_rows, dtype=jnp.int32)[:, None] == flat[None, :]
    dispatch_bf = dispatch.astype(jnp.bfloat16)
    send_rows = jnp.dot(dispatch_bf, hidden, preferred_element_type=jnp.float32).astype(
        jnp.bfloat16
    )
    send_words = jnp.sum(dispatch.astype(jnp.int32) * (target_word + 1)[None, :], axis=1) - 1
    recv_rows, recv_words = (
        lax.all_to_all(
            send_rows.reshape(groups, 4 * capacity, width),
            "vocab",
            split_axis=0,
            concat_axis=0,
            tiled=True,
        ),
        lax.all_to_all(
            send_words.reshape(groups, 4 * capacity),
            "vocab",
            split_axis=0,
            concat_axis=0,
            tiled=True,
        ),
    )
    projections = (proj_one, proj_two, proj_three, proj_four)
    outputs = (out_one, out_two, out_three, out_four)
    band_rows = []
    band_valid = []
    band_local = []
    band_reduced = []
    band_logits = []
    for band in range(4):
        rows = recv_rows[:, band * capacity : (band + 1) * capacity, :].reshape(slots, width)
        words = recv_words[:, band * capacity : (band + 1) * capacity].reshape(slots)
        weight_out = outputs[band][0]
        vcols = weight_out.shape[1]
        valid = words >= 0
        local = jnp.where(valid, words % (vcols * splits) - tp_index * vcols, -1)
        reduced = jnp.dot(rows, projections[band][0], preferred_element_type=jnp.float32).astype(
            jnp.bfloat16
        )
        logits = jnp.dot(reduced, weight_out, preferred_element_type=jnp.float32)
        band_rows.append(rows)
        band_valid.append(valid)
        band_local.append(local)
        band_reduced.append(reduced)
        band_logits.append(logits)
    tail_peak = jnp.stack([jnp.max(logits, axis=1) for logits in band_logits])
    tail_total = jnp.stack(
        [
            jnp.sum(jnp.exp(band_logits[band] - tail_peak[band][:, None]), axis=1)
            for band in range(4)
        ]
    )
    head_peak, head_total, tail_peak, tail_total = combined_all(
        (head_peak, head_total, tail_peak, tail_total), "tp", online_pair
    )
    word_target = jnp.where(tail_mask, -1, target_word - tp_index * word_cols)
    clus_target = jnp.where(tail_mask, cluster_ids - tp_index * clus_cols, -1)
    inverse = 1.0 / head_total
    probs_words = jnp.exp(logit_words - head_peak[:, None]) * inverse[:, None]
    probs_clus = jnp.exp(logit_clus - head_peak[:, None]) * inverse[:, None]
    hit_words = (jnp.arange(word_cols, dtype=jnp.int32)[None, :] == word_target[:, None]).astype(
        jnp.float32
    )
    hit_clus = (jnp.arange(clus_cols, dtype=jnp.int32)[None, :] == clus_target[:, None]).astype(
        jnp.float32
    )
    grad_words = (probs_words - hit_words).astype(jnp.bfloat16)
    grad_clus = (probs_clus - hit_clus).astype(jnp.bfloat16)
    head_part = jnp.dot(grad_words, head_words.T, preferred_element_type=jnp.float32) + jnp.dot(
        grad_clus, head_clusters.T, preferred_element_type=jnp.float32
    )
    head_mine = lax.psum_scatter(
        head_part.astype(jnp.bfloat16), "tp", scatter_dimension=1, tiled=True
    ).astype(jnp.float32)
    band_dlog = []
    partials = []
    for band in range(4):
        weight_out = outputs[band][0]
        vcols = weight_out.shape[1]
        probs = jnp.exp(band_logits[band] - tail_peak[band][:, None]) / tail_total[band][:, None]
        hit = (jnp.arange(vcols, dtype=jnp.int32)[None, :] == band_local[band][:, None]).astype(
            jnp.float32
        )
        dlog = ((probs - hit) * band_valid[band][:, None].astype(jnp.float32)).astype(jnp.bfloat16)
        band_dlog.append(dlog)
        partials.append(jnp.dot(dlog, weight_out.T, preferred_element_type=jnp.float32))
    summed = (
        lax.psum(partials[0].astype(jnp.bfloat16), "tp").astype(jnp.float32),
        lax.psum(partials[1].astype(jnp.bfloat16), "tp").astype(jnp.float32),
        lax.psum(partials[2].astype(jnp.bfloat16), "tp").astype(jnp.float32),
        lax.psum(partials[3].astype(jnp.bfloat16), "tp").astype(jnp.float32),
    )
    grads_out = []
    grads_proj = []
    backs = []
    for band in range(4):
        dred = summed[band].astype(jnp.bfloat16)
        weight_in = projections[band][0]
        grads_out.append(
            jnp.dot(
                band_reduced[band].T, band_dlog[band], preferred_element_type=jnp.float32
            ).astype(jnp.bfloat16)[None]
        )
        rows_mine = lax.dynamic_slice_in_dim(band_rows[band], tp_index * own_width, own_width, 1)
        grads_proj.append(
            jnp.dot(rows_mine.T, dred, preferred_element_type=jnp.float32).astype(jnp.bfloat16)[
                None
            ]
        )
        weight_mine = lax.dynamic_slice_in_dim(weight_in, tp_index * own_width, own_width, 0)
        back = jnp.dot(dred, weight_mine.T, preferred_element_type=jnp.float32).astype(jnp.bfloat16)
        backs.append(back.reshape(groups, capacity, back.shape[1]))
    back_all = jnp.concatenate(backs, axis=1)
    returned = lax.all_to_all(back_all, "vocab", split_axis=0, concat_axis=0, tiled=True).reshape(
        tok_rows, back_all.shape[2]
    )
    tail_part = jnp.dot(dispatch_bf.T, returned, preferred_element_type=jnp.float32)
    grad_hidden = (head_mine + tail_part).astype(jnp.bfloat16)
    grads_cat = jnp.concatenate([grad_words, grad_clus], axis=1)
    head_sum = lax.psum_scatter(
        jnp.dot(hidden.T, grads_cat, preferred_element_type=jnp.float32).astype(jnp.bfloat16),
        "vocab",
        scatter_dimension=0,
        tiled=True,
    ).astype(jnp.float32)
    grad_head_words = head_sum[:, :word_cols].astype(jnp.bfloat16)
    grad_head_clusters = head_sum[:, word_cols:].astype(jnp.bfloat16)
    return (
        grad_hidden,
        grad_head_words,
        grad_head_clusters,
        grads_proj[0],
        grads_proj[1],
        grads_proj[2],
        grads_proj[3],
        grads_out[0],
        grads_out[1],
        grads_out[2],
        grads_out[3],
    )


def solution(mesh):
    return jax.shard_map(
        body,
        mesh=mesh,
        in_specs=(
            P("vocab", None),
            P("vocab", None),
            P("vocab"),
            P(None, "tp"),
            P(None, "tp"),
            P("vocab", None, None),
            P("vocab", None, None),
            P("vocab", None, None),
            P("vocab", None, None),
            P("vocab", None, "tp"),
            P("vocab", None, "tp"),
            P("vocab", None, "tp"),
            P("vocab", None, "tp"),
        ),
        out_specs=(
            P("vocab", "tp"),
            P("vocab", "tp"),
            P("vocab", "tp"),
            P("vocab", "tp", None),
            P("vocab", "tp", None),
            P("vocab", "tp", None),
            P("vocab", "tp", None),
            P("vocab", None, "tp"),
            P("vocab", None, "tp"),
            P("vocab", None, "tp"),
            P("vocab", None, "tp"),
        ),
        check_vma=False,
    )
```

profile of v0, /device:TPU:0, one launch (start us, length us, event | category | flops | bytes accessed | tf_op | source)
XLA Modules:
  0.0 344.2 jit_solution(16571865175138998294)
XLA Ops:
  7.2 0.8 fusion.55
  8.0 1.2 reduce-window.6
  9.5 0.8 fusion.54
  10.2 0.7 subtract_select_fusion
  11.2 0.7 sub.236
  11.8 7.3 %all-to-all-start.1 = ((s32[8,1,64]{2,1,0:T(1,128)}), s32[8,1,64]{2,1,0:T(1,128)S(1)}, u32[]{:S(2)}, u32[]{:S(2)}) async-start(s32[8,1,64]{2,1,0:T(1,128)} %sub.236), calls=%async_computation.2 | async-start | bytes 8192 | tf_op jit(solution)/shard_map/all_to_all | solution.py:81
  19.1 2.6 convolution_convert_fusion.1
  21.7 3.7 %all-to-all-done.1 = s32[8,1,64]{2,1,0:T(1,128)S(1)} async-done(((s32[8,1,64]{2,1,0:T(1,128)}), s32[8,1,64]{2,1,0:T(1,128)S(1)}, u32[]{:S(2)}, u32[]{:S(2)}) %all-to-all-start.1) | async-done | bytes 2080 | tf_op jit(solution)/shard_map/all_to_all | solution.py:81
  25.5 4.4 %all-to-all-start = ((bf16[8,64,2048]{2,1,0:T(8,128)(2,1)}), bf16[8,64,2048]{2,1,0:T(8,128)(2,1)}, u32[]{:S(2)}, u32[]{:S(2)}) async-start(bf16[8,64,2048]{2,1,0:T(8,128)(2,1)} %bitcast.208), calls=%async_computation | async-start | bytes 4194304 | tf_op jit(solution)/shard_map/all_to_all | solution.py:74
  29.9 0.7 fusion.83
  30.6 7.0 %fusion.82 = (f32[512]{0:T(512)S(1)}, f32[512,2048]{1,0:T(8,128)S(1)}) fusion(bf16[512,2048]{1,0:T(8,128)(2,1)S(1)} %copy-done, bf16[2048,2048]{1,0:T(8,128)(2,1)} %param.18), kind=kOutput, calls=%fused_computation.178 | convolution fusion | flops 4296015360 | bytes 14682112 | tf_op jit(solution)/shard_map/dot_general | solution.py:52
  37.7 1.9 copy-done.1
  39.6 0.7 exponential_reduce_fusion
  40.3 5.2 %all-gather.5 = f32[4,1,512]{2,1,0:T(1,128)S(1)} all-gather(f32[1,1,512]{2,1,0:T(1,128)S(1)} %bitcast.224), channel_id=3, replica_groups=mesh['vocab'=8,'tp'=4] {'tp'}, dimensions={0}, use_global_device_ids=true | all-gather | bytes 10240 | tf_op jit(solution)/shard_map/all_gather | solution.py:8
  45.5 5.1 %all-gather.4 = f32[4,1,512]{2,1,0:T(1,128)S(1)} all-gather(f32[1,1,512]{2,1,0:T(1,128)S(1)} %bitcast.220), channel_id=2, replica_groups=mesh['vocab'=8,'tp'=4] {'tp'}, dimensions={0}, use_global_device_ids=true | all-gather | bytes 10240 | tf_op jit(solution)/shard_map/all_gather | solution.py:8
  51.1 0.6 compare_convert_fusion.2
  51.6 0.6 compare_select_fusion.11
  52.2 24.7 %all-to-all-done = bf16[8,64,2048]{2,1,0:T(8,128)(2,1)} async-done(((bf16[8,64,2048]{2,1,0:T(8,128)(2,1)}), bf16[8,64,2048]{2,1,0:T(8,128)(2,1)}, u32[]{:S(2)}, u32[]{:S(2)}) %all-to-all-start) | async-done | bytes 2097184 | tf_op jit(solution)/shard_map/all_to_all | solution.py:74
  76.9 1.8 fusion.80
  78.8 2.7 convolution_convert_fusion.19
  81.5 0.3 convolution_convert_fusion.17
  81.9 0.4 fusion.21
  82.4 0.7 fusion.17
  83.2 0.3 fusion.87
  83.5 0.6 copy-done.23
  84.4 0.3 fusion.86
  84.9 0.3 fusion.85
  85.4 0.8 copy-done.3
  86.5 0.4 fusion.84
  86.8 0.3 exponential_reduce_fusion.1
  87.1 5.2 %all-gather.7 = f32[4,4,128]{2,1,0:T(4,128)S(1)} all-gather(f32[1,4,128]{2,1,0:T(4,128)S(1)} %maximum_bitcast_fusion.1), channel_id=5, replica_groups=mesh['vocab'=8,'tp'=4] {'tp'}, dimensions={0}, use_global_device_ids=true | all-gather | bytes 10240 | tf_op jit(solution)/shard_map/all_gather | solution.py:8
  92.3 5.3 %all-gather.6 = f32[4,4,128]{2,1,0:T(4,128)S(1)} all-gather(f32[1,4,128]{2,1,0:T(4,128)S(1)} %maximum_bitcast_fusion), channel_id=4, replica_groups=mesh['vocab'=8,'tp'=4] {'tp'}, dimensions={0}, use_global_device_ids=true | all-gather | bytes 10240 | tf_op jit(solution)/shard_map/all_gather | solution.py:8
  98.0 3.5 %subtract_convert_fusion = bf16[512,2048]{1,0:T(8,128)(2,1)S(1)} fusion(f32[512,2048]{1,0:T(8,128)} %copy-done.1, s32[512]{0:T(512)S(1)} %get-tuple-element.155, f32[512]{0:T(512)S(1)} %broadcast_divide_fusion, f32[512]{0:T(512)S(1)} %get-tuple-element.61), kind=kLoop, calls=%fused_computation.13 | loop fusion | flops 6291456 | bytes 6297600 | tf_op jit(solution)/shard_map/convert_element_type | solution.py:133
  101.8 1.0 convolution_convert_fusion.16
  102.8 9.5 %fusion.88 = f32[512,2048]{1,0:T(8,128)} fusion(bf16[512,2048]{1,0:T(8,128)(2,1)S(1)} %subtract_convert_fusion, bf16[2048,2048]{1,0:T(8,128)(2,1)} %param.18), kind=kOutput, calls=%fused_computation.184 | convolution fusion | flops 4294967296 | bytes 14680064 | tf_op jit(solution)/shard_map/dot_general | solution.py:135
  112.4 1.0 convolution_convert_fusion.11
  113.4 1.0 convolution_convert_fusion.9
  114.5 4.3 %add_convert_fusion = bf16[512,2048]{1,0:T(8,128)(2,1)} fusion(f32[512,2048]{1,0:T(8,128)} %fusion.88, bf16[512,8]{0,1:T(8,128)(2,1)S(1)} %subtract_convert_fusion.1, bf16[2048,8]{0,1:T(8,128)(2,1)S(1)} %copy-done.34), kind=kOutput, calls=%fused_computation.12 | convolution fusion | flops 18874368 | bytes 6332416 | tf_op jit(solution)/shard_map/dot_general | solution.py:135
  118.9 0.8 copy.36
  119.7 8.6 %fusion.2 = bf16[2048,2056]{0,1:T(8,128)(2,1)} fusion(bf16[512,2048]{1,0:T(8,128)(2,1)S(1)} %copy-done, bf16[512,8]{1,0:T(8,128)(2,1)} %copy.36, bf16[512,2048]{1,0:T(8,128)(2,1)} %copy-done.12), kind=kOutput, calls=%fused_computation.9 | convolution fusion | flops 4320165888 | bytes 12623872 | tf_op jit(solution)/shard_map/dot_general | solution.py:187
  128.3 0.6 multiply_convert_fusion
  128.9 0.8 copy-done.5
  129.7 1.4 convolution_convert_fusion.18
  131.1 12.4 %psum.31 = bf16[128,128]{1,0:T(8,128)(2,1)} all-reduce(bf16[128,128]{1,0:T(8,128)(2,1)S(1)} %convolution_convert_fusion.18), channel_id=1, replica_groups=mesh['vocab'=8,'tp'=4] {'tp'}, use_global_device_ids=true, to_apply=%region_22.23 | all-reduce | flops 16384 | bytes 65536 | tf_op jit(solution)/shard_map/psum | solution.py:157
  143.5 1.1 fusion.16
  144.6 1.8 convolution_convert_fusion.13
  146.7 1.2 convolution_convert_fusion.14
  147.9 1.4 convolution_convert_fusion.10
  149.4 1.8 convolution_convert_fusion.15
  151.2 1.7 pad_maximum_fusion
  152.9 5.5 %all-to-all-start.2 = ((bf16[8,64,512]{2,1,0:T(8,128)(2,1)}), bf16[8,64,512]{2,1,0:T(8,128)(2,1)}, u32[]{:S(2)}, u32[]{:S(2)}) async-start(bf16[8,64,512]{2,1,0:T(8,128)(2,1)} %pad_maximum_fusion), calls=%async_computation.3 | async-start | bytes 1048576 | tf_op jit(solution)/shard_map/all_to_all | solution.py:180
  158.5 1.8 fusion.24
  160.3 1.9 fusion.5
  162.2 1.9 fusion.14
  164.1 2.1 fusion.15
  166.2 1.9 fusion.20
  168.1 2.0 fusion.13
  170.1 2.3 fusion.11
  172.5 8.6 %reduce-scatter.3.cloned.1.call-done = bf16[512,512]{1,0:T(8,128)(2,1)} async-done(((bf16[512,2048]{1,0:T(8,128)(2,1)}), bf16[512,512]{1,0:T(8,128)(2,1)}) %reduce-scatter.3.cloned.1.call-update) | async-done | bytes 524304 | tf_op jit(solution)/shard_map/reduce_scatter | solution.py:138
  181.0 2.5 fusion.12
  183.5 150.2 %reduce-scatter.5.cloned.1.call-done = bf16[256,2056]{0,1:T(8,128)(2,1)} async-done(((bf16[2048,2056]{0,1:T(8,128)(2,1)}), bf16[256,2056]{0,1:T(8,128)(2,1)}) %reduce-scatter.5.cloned.1.call-update) | async-done | bytes 1052688 | tf_op jit(solution)/shard_map/reduce_scatter | solution.py:186
  333.7 1.3 slice.143
  335.0 1.4 copy.37
  336.4 1.3 slice.144
  (144 shorter events, 3.1 us)
Async XLA Ops:
  7.2 11.9 %copy-start = (bf16[512,2048]{1,0:T(8,128)(2,1)S(1)}, bf16[512,2048]{1,0:T(8,128)(2,1)}, u32[]{:S(2)}) copy-start(bf16[512,2048]{1,0:T(8,128)(2,1)} %param.15) | copy-start | bytes 6291460
  11.8 13.6 %all-to-all-start.1 = ((s32[8,1,64]{2,1,0:T(1,128)}), s32[8,1,64]{2,1,0:T(1,128)S(1)}, u32[]{:S(2)}, u32[]{:S(2)}) async-start(s32[8,1,64]{2,1,0:T(1,128)} %sub.236), calls=%async_computation.2 | async-start | bytes 8192 | tf_op jit(solution)/shard_map/all_to_all | solution.py:81
  21.7 8.2 %copy-start.34 = (bf16[2048,8]{0,1:T(8,128)(2,1)S(1)}, bf16[2048,8]{0,1:T(8,128)(2,1)}, u32[]{:S(2)}) copy-start(bf16[2048,8]{0,1:T(8,128)(2,1)} %param.19) | copy-start | bytes 98308
  25.5 51.5 %all-to-all-start = ((bf16[8,64,2048]{2,1,0:T(8,128)(2,1)}), bf16[8,64,2048]{2,1,0:T(8,128)(2,1)}, u32[]{:S(2)}, u32[]{:S(2)}) async-start(bf16[8,64,2048]{2,1,0:T(8,128)(2,1)} %bitcast.208), calls=%async_computation | async-start | bytes 4194304 | tf_op jit(solution)/shard_map/all_to_all | solution.py:74
  29.9 116.8 %all-reduce.3.cloned.1.call-start = ((), (), s32[]{:S(2)}) async-start(), calls=%async_computation.7 | async-start | bytes 917504 | tf_op jit(solution)/shard_map/psum | solution.py:156
  37.6 1.9 copy-start.1
  37.6 13.0 %copy-start.36 = (s32[512,1]{0,1:T(1,128)S(1)}, s32[512,1]{0,1:T(1,128)}, u32[]{:S(2)}) copy-start(s32[512,1]{0,1:T(1,128)} %param.16) | copy-start | bytes 6148
  39.6 41.9 %copy-start.16 = (bf16[1,2048,256]{2,1,0:T(8,128)(2,1)S(1)}, bf16[1,2048,256]{2,1,0:T(8,128)(2,1)}, u32[]{:S(2)}) copy-start(bf16[1,2048,256]{2,1,0:T(8,128)(2,1)} %param.22) | copy-start | bytes 3145732
  45.4 36.9 %copy-start.35 = (f32[4,1,512]{2,1,0:T(1,128)}, f32[4,1,512]{2,1,0:T(1,128)S(1)}, u32[]{:S(2)}) copy-start(f32[4,1,512]{2,1,0:T(1,128)S(1)} %all-gather.5) | copy-start | bytes 24580
  50.6 31.7 %copy-start.33 = (f32[4,1,512]{2,1,0:T(1,128)}, f32[4,1,512]{2,1,0:T(1,128)S(1)}, u32[]{:S(2)}) copy-start(f32[4,1,512]{2,1,0:T(1,128)S(1)} %all-gather.4) | copy-start | bytes 24580
  76.9 4.9 %copy-start.7 = (bf16[1,2048,512]{2,1,0:T(8,128)(2,1)S(1)}, bf16[1,2048,512]{2,1,0:T(8,128)(2,1)}, u32[]{:S(2)}) copy-start(bf16[1,2048,512]{2,1,0:T(8,128)(2,1)} %param.21) | copy-start | bytes 6291460
  76.9 5.4 %copy-start.2 = (bf16[1,2048,1024]{2,1,0:T(8,128)(2,1)S(1)}, bf16[1,2048,1024]{2,1,0:T(8,128)(2,1)}, u32[]{:S(2)}) copy-start(bf16[1,2048,1024]{2,1,0:T(8,128)(2,1)} %param.20) | copy-start | bytes 12582916
  78.7 4.4 %copy-start.8 = (bf16[8,16,2048]{2,1,0:T(8,128)(2,1)}, bf16[8,16,2048]{2,1,0:T(8,128)(2,1)S(1)}, u32[]{:S(2)}) copy-start(bf16[8,16,2048]{2,1,0:T(8,128)(2,1)S(1)} %get-tuple-element.149) | copy-start | bytes 1572868
  78.8 4.4 %copy-start.9 = (bf16[8,16,2048]{2,1,0:T(8,128)(2,1)}, bf16[8,16,2048]{2,1,0:T(8,128)(2,1)S(1)}, u32[]{:S(2)}) copy-start(bf16[8,16,2048]{2,1,0:T(8,128)(2,1)S(1)} %get-tuple-element.147) | copy-start | bytes 1572868
  78.8 4.4 %copy-start.10 = (bf16[8,16,2048]{2,1,0:T(8,128)(2,1)}, bf16[8,16,2048]{2,1,0:T(8,128)(2,1)S(1)}, u32[]{:S(2)}) copy-start(bf16[8,16,2048]{2,1,0:T(8,128)(2,1)S(1)} %get-tuple-element.148) | copy-start | bytes 1572868
  78.8 4.4 %copy-start.11 = (bf16[8,16,2048]{2,1,0:T(8,128)(2,1)}, bf16[8,16,2048]{2,1,0:T(8,128)(2,1)S(1)}, u32[]{:S(2)}) copy-start(bf16[8,16,2048]{2,1,0:T(8,128)(2,1)S(1)} %get-tuple-element.150) | copy-start | bytes 1572868
  81.5 4.9 %copy-start.32 = (bf16[128,128]{1,0:T(8,128)(2,1)}, bf16[128,128]{1,0:T(8,128)(2,1)S(1)}, u32[]{:S(2)}) copy-start(bf16[128,128]{1,0:T(8,128)(2,1)S(1)} %convolution_convert_fusion.19) | copy-start | bytes 98308
  81.8 1.3 copy-start.28
  81.9 2.5 copy-start.26
  82.4 4.1 %copy-start.31 = (bf16[128,512]{1,0:T(8,128)(2,1)}, bf16[128,512]{1,0:T(8,128)(2,1)S(1)}, u32[]{:S(2)}) copy-start(bf16[128,512]{1,0:T(8,128)(2,1)S(1)} %fusion.21) | copy-start | bytes 393220
  82.4 2.5 copy-start.13
  82.4 4.1 %copy-start.15 = (bf16[1,128,2048]{2,1,0:T(8,128)(2,1)S(1)}, bf16[1,128,2048]{2,1,0:T(8,128)(2,1)}, u32[]{:S(2)}) copy-start(bf16[1,128,2048]{2,1,0:T(8,128)(2,1)} %param.27) | copy-start | bytes 1572868
  83.2 3.6 %copy-start.17 = (bf16[128,1024]{1,0:T(8,128)(2,1)}, bf16[128,1024]{1,0:T(8,128)(2,1)S(1)}, u32[]{:S(2)}) copy-start(bf16[128,1024]{1,0:T(8,128)(2,1)S(1)} %fusion.17) | copy-start | bytes 786436
  83.2 14.5 %slice-start = ((f32[4,1,512]{2,1,0:T(1,128)}), f32[1,1,512]{2,1,0:T(1,128)S(1)}, s32[]{:S(2)}) async-start(f32[4,1,512]{2,1,0:T(1,128)} %copy-done.33), calls=%async_computation.8 | async-start | bytes 4096 | tf_op jit(solution)/shard_map/slice | solution.py:9
  83.2 14.5 %slice-start.1 = ((f32[4,1,512]{2,1,0:T(1,128)}), f32[1,1,512]{2,1,0:T(1,128)S(1)}, s32[]{:S(2)}) async-start(f32[4,1,512]{2,1,0:T(1,128)} %copy-done.35), calls=%async_computation.9 | async-start | bytes 4096 | tf_op jit(solution)/shard_map/slice | solution.py:9
  83.5 0.7 copy-start.23
  84.7 0.7 copy-start.19
  85.4 0.8 copy-start.3
  97.9 3.6 %copy-start.4 = (f32[128,1024]{1,0:T(8,128)S(1)}, f32[128,1024]{1,0:T(8,128)}, u32[]{:S(2)}) copy-start(f32[128,1024]{1,0:T(8,128)} %copy-done.3) | copy-start | bytes 1572868
  97.9 3.8 %copy-start.14 = (bf16[1,256,1024]{2,1,0:T(8,128)(2,1)S(1)}, bf16[1,256,1024]{2,1,0:T(8,128)(2,1)}, u32[]{:S(2)}) copy-start(bf16[1,256,1024]{2,1,0:T(8,128)(2,1)} %param.26) | copy-start | bytes 1572868
  101.4 10.9 %copy-start.12 = (bf16[512,2048]{1,0:T(8,128)(2,1)}, bf16[512,2048]{1,0:T(8,128)(2,1)S(1)}, u32[]{:S(2)}) copy-start(bf16[512,2048]{1,0:T(8,128)(2,1)S(1)} %subtract_convert_fusion) | copy-start | bytes 6291460
  101.5 10.9 %copy-start.37 = (f32[128]{0:T(128)}, f32[128]{0:T(128)S(1)}, u32[]{:S(2)}) copy-start(f32[128]{0:T(128)S(1)} %get-tuple-element.184) | copy-start | bytes 1540
  101.5 11.9 %copy-start.39 = (f32[128]{0:T(128)}, f32[128]{0:T(128)S(1)}, u32[]{:S(2)}) copy-start(f32[128]{0:T(128)S(1)} %get-tuple-element.162) | copy-start | bytes 1540
  101.5 11.9 %copy-start.41 = (f32[128]{0:T(128)}, f32[128]{0:T(128)S(1)}, u32[]{:S(2)}) copy-start(f32[128]{0:T(128)S(1)} %get-tuple-element.187) | copy-start | bytes 1540
  102.8 9.6 %copy-start.20 = (f32[128,512]{1,0:T(8,128)S(1)}, f32[128,512]{1,0:T(8,128)}, u32[]{:S(2)}) copy-start(f32[128,512]{1,0:T(8,128)} %copy-done.19) | copy-start | bytes 786436
  102.8 9.6 %copy-start.27 = (bf16[1,512,512]{2,1,0:T(8,128)(2,1)S(1)}, bf16[1,512,512]{2,1,0:T(8,128)(2,1)}, u32[]{:S(2)}) copy-start(bf16[1,512,512]{2,1,0:T(8,128)(2,1)} %param.25) | copy-start | bytes 1572868
  102.8 9.6 %copy-start.42 = (f32[128]{0:T(128)S(1)}, f32[128]{0:T(128)}, u32[]{:S(2)}) copy-start(f32[128]{0:T(128)} %get-tuple-element.180) | copy-start | bytes 1540
  102.8 9.6 %copy-start.43 = (s32[128]{0:T(128)S(1)}, s32[128]{0:T(128)}, u32[]{:S(2)}) copy-start(s32[128]{0:T(128)} %get-tuple-element.182) | copy-start | bytes 1540
  102.8 10.6 %copy-start.24 = (f32[128,256]{1,0:T(8,128)S(1)}, f32[128,256]{1,0:T(8,128)}, u32[]{:S(2)}) copy-start(f32[128,256]{1,0:T(8,128)} %copy-done.23) | copy-start | bytes 393220
  102.8 10.6 %copy-start.29 = (bf16[1,1024,256]{2,1,0:T(8,128)(2,1)S(1)}, bf16[1,1024,256]{2,1,0:T(8,128)(2,1)}, u32[]{:S(2)}) copy-start(bf16[1,1024,256]{2,1,0:T(8,128)(2,1)} %param.24) | copy-start | bytes 1572868
  102.8 10.6 %copy-start.44 = (f32[128]{0:T(128)S(1)}, f32[128]{0:T(128)}, u32[]{:S(2)}) copy-start(f32[128]{0:T(128)} %get-tuple-element.181) | copy-start | bytes 1540
  102.8 10.6 %copy-start.45 = (s32[128]{0:T(128)S(1)}, s32[128]{0:T(128)}, u32[]{:S(2)}) copy-start(s32[128]{0:T(128)} %get-tuple-element.183) | copy-start | bytes 1540
  114.5 66.6 %reduce-scatter.3.cloned.1.call-start = ((), (), s32[]{:S(2)}) async-start(), calls=%async_computation.5 | async-start | bytes 2621440 | tf_op jit(solution)/shard_map/reduce_scatter | solution.py:138
  118.9 214.9 %reduce-scatter.5.cloned.1.call-start = ((), (), s32[]{:S(2)}) async-start(), calls=%async_computation.6 | async-start | bytes 9474048 | tf_op jit(solution)/shard_map/reduce_scatter | solution.py:186
  128.9 0.8 copy-start.5
  129.7 32.5 %copy-start.18 = (bf16[128,1024]{1,0:T(8,128)(2,1)S(1)}, bf16[128,1024]{1,0:T(8,128)(2,1)}, u32[]{:S(2)}) copy-start(bf16[128,1024]{1,0:T(8,128)(2,1)} %copy-done.17) | copy-start | bytes 786436
  129.7 32.5 %copy-start.40 = (f32[128]{0:T(128)S(1)}, f32[128]{0:T(128)}, u32[]{:S(2)}) copy-start(f32[128]{0:T(128)} %copy-done.39) | copy-start | bytes 1540
  131.1 29.2 %copy-start.6 = (bf16[128,2048]{1,0:T(8,128)(2,1)S(1)}, bf16[128,2048]{1,0:T(8,128)(2,1)}, u32[]{:S(2)}) copy-start(bf16[128,2048]{1,0:T(8,128)(2,1)} %copy-done.5) | copy-start | bytes 1572868
  131.1 33.0 %copy-start.21 = (f32[128,512]{1,0:T(8,128)S(1)}, f32[128,512]{1,0:T(8,128)}, u32[]{:S(2)}) copy-start(f32[128,512]{1,0:T(8,128)} %copy-done.19) | copy-start | bytes 786436
  131.1 33.0 %copy-start.38 = (f32[128]{0:T(128)S(1)}, f32[128]{0:T(128)}, u32[]{:S(2)}) copy-start(f32[128]{0:T(128)} %copy-done.37) | copy-start | bytes 1540
  144.6 17.6 %copy-start.25 = (f32[128,256]{1,0:T(8,128)S(1)}, f32[128,256]{1,0:T(8,128)}, u32[]{:S(2)}) copy-start(f32[128,256]{1,0:T(8,128)} %copy-done.23) | copy-start | bytes 393220
  149.3 20.8 %copy-start.22 = (bf16[128,1024]{1,0:T(8,128)(2,1)S(1)}, bf16[128,1024]{1,0:T(8,128)(2,1)}, u32[]{:S(2)}) copy-start(bf16[128,1024]{1,0:T(8,128)(2,1)} %get-tuple-element.140) | copy-start | bytes 786436
  152.9 19.5 %all-to-all-start.2 = ((bf16[8,64,512]{2,1,0:T(8,128)(2,1)}), bf16[8,64,512]{2,1,0:T(8,128)(2,1)}, u32[]{:S(2)}, u32[]{:S(2)}) async-start(bf16[8,64,512]{2,1,0:T(8,128)(2,1)} %pad_maximum_fusion), calls=%async_computation.3 | async-start | bytes 1048576 | tf_op jit(solution)/shard_map/all_to_all | solution.py:180
  158.5 9.7 %copy-start.30 = (bf16[128,512]{1,0:T(8,128)(2,1)S(1)}, bf16[128,512]{1,0:T(8,128)(2,1)}, u32[]{:S(2)}) copy-start(bf16[128,512]{1,0:T(8,128)(2,1)} %get-tuple-element.139) | copy-start | bytes 393220
Sparse Core Ops, SparseCore 0:
  114.6 32.0 all-reduce.2
  149.4 31.5 reduce-scatter.2
  184.5 149.1 reduce-scatter.4
where the time goes:
time: 345 us; the launch traced here: 344 us
  waiting for transfers between devices  188 us (54%)
  matrix products  66.5 us (19%)
  blocking collectives  33.2 us (10%)
  starting transfers between devices  17.3 us (5%)
  between operations  14.5 us (4%)
  other arithmetic  12.7 us (4%)
  local copies, waits for them, and re-layouts  12.4 us (4%)
    reduce_scatter x1, waiting for transfers between devices, body(): lax.psum_scatter(jnp.dot(hidden.T, grads_cat, preferred_element_type=jnp....  150 us
    all_to_all x1, waiting for transfers between devices, body(): lax.all_to_all(send_rows.reshape(groups, 4 * capacity, width), 'vocab', s...  24.7 us
    all_gather x4, blocking collectives, combined_all(): pieces = jax.tree.map(lambda part: lax.all_gather(part, axis), value)  20.8 us
    psum x1, blocking collectives, body(): lax.psum(partials[3].astype(jnp.bfloat16), 'tp').astype(jnp.float32)  12.4 us
    dot_general x1, matrix products, body(): jnp.dot(grad_words, head_words.T, preferred_element_type=jnp.float32)  9.54 us
    dot_general x1, matrix products, body(): jnp.dot(hidden.T, grads_cat, preferred_element_type=jnp.float32)  8.57 us
    reduce_scatter x1, waiting for transfers between devices, body(): lax.psum_scatter(head_part.astype(jnp.bfloat16), 'tp', scatter_dimension=...  8.56 us
    dot_general x4, matrix products, body(): jnp.dot(rows_mine.T, dred, preferred_element_type=jnp.float32)  8.09 us
  transfers between devices with their start and end apart: 6, of which 5 were waited for; matrix products, arithmetic and copies ran while one was open for 16% of the time, Pallas kernels for 0%

commit v1 on v0

v1 whole, which is shorter than its diff:
```python
import functools

import jax
import jax.numpy as jnp
from jax import lax
from jax.experimental import pallas as pl
from jax.experimental.pallas import tpu as pltpu
from jax.sharding import PartitionSpec as P

F32 = jnp.float32
BF16 = jnp.bfloat16
I32 = jnp.int32
LANES = 128


def xor_pairs(size, step):
    return [(i, i ^ step) for i in range(size)]


def tp_swap(value, step):
    return lax.ppermute(value, "tp", xor_pairs(lax.axis_size("tp"), step))


def dot_nn(a, b):
    return lax.dot_general(a, b, (((1,), (0,)), ((), ())), preferred_element_type=F32)


def dot_nt(a, b):
    return lax.dot_general(a, b, (((1,), (1,)), ((), ())), preferred_element_type=F32)


def dot_tn(a, b):
    return lax.dot_general(a, b, (((0,), (0,)), ((), ())), preferred_element_type=F32)


def struct(shape, dtype):
    return jax.ShapeDtypeStruct(shape, dtype)


def whole(array):
    rank = len(array.shape)
    return pl.BlockSpec(array.shape, lambda *_: (0,) * rank)


COST_SCALE = 1.0
MICROSECONDS = {
    "send_rows": 3,
    "head_logits": 9,
    "line_logits": 20,
    "head_back": 9,
    "head_weights": 8,
    "turned_rows": 2,
    "tail_logits": 5,
    "tail_grads": 3,
    "tail_back": 3,
    "add": 1,
    "grad_hidden": 2,
}


SMALL = ("add",)


def kernel_call(kernel, name, scalars, operands, in_specs, outs, out_specs, scratch=(), grid=(1,)):
    return pl.pallas_call(
        kernel,
        name=name,
        out_shape=outs,
        grid_spec=pltpu.PrefetchScalarGridSpec(
            num_scalar_prefetch=1,
            grid=grid,
            in_specs=in_specs,
            out_specs=out_specs,
            scratch_shapes=list(scratch),
        ),
        compiler_params=pltpu.CompilerParams(vmem_limit_bytes=(16 if name in SMALL else 60) << 20),
        cost_estimate=pl.CostEstimate(
            flops=int(MICROSECONDS[name] * COST_SCALE * 1e9), bytes_accessed=1, transcendentals=0
        ),
    )(scalars, *operands)


class Order:
    def __init__(self, scalars):
        self.scalars = scalars
        self.last = None

    def hold(self, *values):
        spec = pl.BlockSpec(memory_space=pl.ANY)
        held = pl.pallas_call(
            lambda *refs: None,
            name="hold",
            out_shape=[struct(v.shape, v.dtype) for v in values],
            in_specs=[spec] * (len(values) + 1),
            out_specs=[spec] * len(values),
            input_output_aliases={i: i for i in range(len(values))},
            cost_estimate=pl.CostEstimate(flops=1, bytes_accessed=1, transcendentals=0),
        )(*values, self.last)
        self.last = held[-1]
        return held

    def call(self, kernel, cfg, name, operands, in_specs, outs, out_specs, scratch=(), grid=(1,), scalars=None):
        kernel = functools.partial(kernel, cfg)
        scalars = self.scalars if scalars is None else scalars
        if self.last is not None:
            n = len(operands)
            operands = (*operands, self.last)
            in_specs = [*in_specs, pl.BlockSpec(memory_space=pl.ANY)]
            inner = kernel

            def kernel(scal, *refs):
                inner(scal, *refs[:n], *refs[n + 1 :])

        done = kernel_call(kernel, name, scalars, operands, in_specs, outs, out_specs, scratch, grid)
        self.last = done[-1] if isinstance(done, (list, tuple)) else done
        return done


def lanes_of(shape):
    return lax.broadcasted_iota(I32, shape, len(shape) - 1)


def columns_of(rows):
    n = rows[0].shape[1]
    filler = jnp.zeros((LANES - len(rows), n), F32)
    return jnp.concatenate(list(rows) + [filler], axis=0).T


def merged_stats(shares, splits, quarter):
    rows = []
    for step, share in enumerate(shares):
        value = share
        if quarter:
            value = jnp.concatenate(
                [value[:, (m ^ step) * quarter : ((m ^ step) + 1) * quarter] for m in range(splits)],
                axis=1,
            )
        rows.append((value[0:1], value[1:2]))
    top = rows[0][0]
    for peak, _ in rows[1:]:
        top = jnp.maximum(top, peak)
    total = rows[0][1] * jnp.exp(rows[0][0] - top)
    for peak, part in rows[1:]:
        total = total + part * jnp.exp(peak - top)
    return top, total


def target_columns(ids_ref):
    return columns_of([ids_ref[i : i + 1, :] for i in range(3)])


def send_kernel(cfg, scal, ids_ref, hid_ref, dt_ref, send_ref):
    groups, capacity = cfg
    tok = hid_ref.shape[0]
    width = max(LANES, 4 * groups)
    targets = target_columns(ids_ref)
    clus = targets[:, 1:2].astype(I32)
    word = targets[:, 2:3].astype(I32)
    member = (lanes_of((tok, width)) == clus).astype(F32).astype(BF16)
    row = lax.broadcasted_iota(I32, (tok, tok), 0)
    before = (lanes_of((tok, tok)) < row).astype(F32).astype(BF16)
    ranks = dot_nn(before, member)
    rank = jnp.sum(ranks * member.astype(F32), axis=1, keepdims=True).astype(I32)
    flat = lax.rem(clus, groups) * (4 * capacity) + lax.div(clus, groups) * capacity + rank
    flat = jnp.where(clus >= 0, flat, -1)
    place = (lanes_of((tok, tok)) == flat).astype(F32).astype(BF16)
    dt_ref[...] = place
    lane = lanes_of((tok, LANES))
    digits = jnp.where(
        lane == 0, lax.div(word, 256), jnp.where(lane == 1, lax.rem(word, 256), (lane == 2).astype(I32))
    )
    own = hid_ref.shape[1]
    send_ref[:, :own] = dot_tn(place, hid_ref[...]).astype(BF16)
    send_ref[:, own:] = dot_tn(place, digits.astype(F32).astype(BF16)).astype(BF16)


def logits_kernel(cfg, scal, *refs):
    n, clus_cols = cfg
    pieces, (w_ref, wc_ref, e_ref, ec_ref, st_ref, ex_ref) = refs[:n], refs[n : n + 6]
    peak_ref, sum_ref = refs[n + 6 :]
    j = pl.program_id(0)
    blocks = pl.num_programs(0)
    parts = []
    at = 0
    for piece in pieces:
        size = piece.shape[0]
        step = min(size, 256)
        parts += [(piece, i, at + i, step) for i in range(0, size, step)]
        at += size

    @pl.when(j == 0)
    def _():
        for piece, i, at, size in parts:
            out = slice(at, at + size)
            logits = dot_nn(piece[i : i + size, :], wc_ref[...])
            logits = jnp.where(lanes_of(logits.shape) < clus_cols, logits, -jnp.inf)
            peak = jnp.max(logits, axis=1, keepdims=True)
            expd = jnp.exp(logits - peak)
            ec_ref[out, :] = expd.astype(BF16)
            peak_ref[out, :] = peak
            sum_ref[out, :] = jnp.sum(expd, axis=1, keepdims=True)
            st_ref[out, :] = jnp.where(lanes_of((size, LANES)) == blocks, peak, 0.0)

    for piece, i, at, size in parts:
        out = slice(at, at + size)
        logits = dot_nn(piece[i : i + size, :], w_ref[...])
        before = peak_ref[out, :]
        peak = jnp.maximum(before, jnp.max(logits, axis=1, keepdims=True))
        expd = jnp.exp(logits - peak)
        e_ref[out, :] = expd.astype(BF16)
        total = sum_ref[out, :] * jnp.exp(before - peak) + jnp.sum(expd, axis=1, keepdims=True)
        peak_ref[out, :] = peak
        sum_ref[out, :] = total
        st_ref[out, :] = jnp.where(lanes_of((size, LANES)) == j, peak, st_ref[out, :])

    @pl.when(j == blocks - 1)
    def _():
        lane = lanes_of(st_ref.shape)
        both = jnp.where(lane == 0, peak_ref[...], jnp.where(lane == 1, sum_ref[...], 0.0))
        ex_ref[...] = both.T[:8]


def head_columns(cfg, shares, ids, permuted):
    splits, quarter = cfg
    top, total = merged_stats(shares, splits, quarter if permuted else 0)
    return columns_of([top, 1.0 / total, ids[0:1], ids[1:2]])


def head_block(expd, stats, lane, cols, target, first, limit):
    peak = jnp.sum(jnp.where(lanes_of(stats.shape) == lane, stats, 0.0), axis=1, keepdims=True)
    probs = expd.astype(F32) * (jnp.exp(peak - cols[:, 0:1]) * cols[:, 1:2])
    local = cols[:, target : target + 1].astype(I32) - first
    local = jnp.where(local < limit, local, -1)
    return jnp.where(lanes_of(probs.shape) == local, probs - 1.0, probs).astype(BF16)


def back_kernel(cfg, scal, e_ref, ec_ref, st_ref, ids_ref, *refs):
    splits, block, clus_cols = cfg
    shares, refs = refs[:splits], refs[splits:]
    w_ref, wc_ref, give_ref, keep_ref, g_ref, gc_ref, col_ref = refs
    i = pl.program_id(0)
    tok, word_cols = e_ref.shape
    blocks = word_cols // block

    @pl.when(i == 0)
    def _():
        col_ref[...] = head_columns((splits, 0), [share[...] for share in shares], ids_ref[...], False)
        for at in range(0, tok, LANES):
            rows = slice(at, at + LANES)
            cols, stats = col_ref[rows, :], st_ref[rows, :]
            for j in range(blocks):
                part = slice(j * block, (j + 1) * block)
                first = scal[0] * word_cols + j * block
                g_ref[rows, part] = head_block(e_ref[rows, part], stats, j, cols, 2, first, block)
            first = scal[0] * clus_cols
            gc_ref[rows, :] = head_block(ec_ref[rows, :], stats, blocks, cols, 3, first, clus_cols)

    out = dot_nt(g_ref[...], w_ref[...]) + dot_nt(gc_ref[...], wc_ref[...])

    @pl.when(i < splits // 2)
    def _():
        give_ref[0] = out.astype(BF16)

    @pl.when(i >= splits // 2)
    def _():
        keep_ref[0] = out.astype(BF16)


def turn_kernel(cfg, scal, *refs):
    near, n = cfg
    pieces, (out_ref,) = refs[:n], refs[n:]
    out_rows = out_ref.shape[0] // near
    at = 0
    for piece in pieces:
        size = piece.shape[0]
        turned = piece[...].T
        for i in range(near):
            to = pl.multiple_of((scal[2] ^ i) * out_rows, out_rows)
            out_ref[pl.ds(to, out_rows), at : at + size] = turned[i * out_rows : (i + 1) * out_rows]
        at += size


def weights_kernel(cfg, scal, t_ref, e0, e1, st0, st1, *refs):
    splits, quarter, clus_cols, word_cols, line, offset, last = cfg
    tok = e0.shape[0]
    block = e0.shape[1]
    i = pl.program_id(0)
    if last:
        col_ref, ec0, ec1, own_ref, near_ref, ownc_ref, nearc_ref, g_ref = refs
    else:
        ids0, ids1, *refs = refs
        shares0, shares1, refs = refs[:splits], refs[splits : 2 * splits], refs[2 * splits :]
        own_ref, near_ref, col_ref, g_ref = refs
    out_rows = own_ref.shape[0]

    def fill(first_ref, others_ref, lane, target, first, limit):
        for at in range(0, line * tok, LANES):
            source, stats, here = (first_ref, st0, at) if at < tok else (others_ref, st1, at - tok)
            rows = slice(here, here + LANES)
            g_ref[at : at + LANES, : source.shape[1]] = head_block(
                source[rows, :], stats[rows, :], lane, col_ref[at : at + LANES, :], target, first, limit
            )

    if not last:

        @pl.when(i == 0)
        def _():
            col_ref[:tok, :] = head_columns(
                (splits, quarter), [share[...] for share in shares0], ids0[...], False
            )
            for k in range(line - 1):
                part = slice(k * tok, (k + 1) * tok)
                col_ref[(k + 1) * tok : (k + 2) * tok, :] = head_columns(
                    (splits, quarter), [share[:, part] for share in shares1], ids1[:, part], True
                )

    j = i + offset
    fill(e0, e1, j, 2, scal[0] * word_cols + j * block, block)
    both = dot_nn(t_ref[...], g_ref[...]).astype(BF16)
    own_ref[...] = both[:out_rows]
    near_ref[...] = both[out_rows:]
    if last:

        @pl.when(i == pl.num_programs(0) - 1)
        def _():
            fill(ec0, ec1, word_cols // block, 3, scal[0] * clus_cols, clus_cols)
            both = dot_nn(t_ref[...], g_ref[:, :LANES]).astype(BF16)
            ownc_ref[...] = both[:out_rows]
            nearc_ref[...] = both[out_rows:]


def tail_logits_kernel(cfg, scal, *refs):
    splits = cfg
    pieces, refs = refs[:splits], refs[splits:]
    projections, outs, (red_ref, e_ref, ex_ref, acc_ref) = refs[:4], refs[4:8], refs[8:]
    i = pl.program_id(0)
    for m in range(splits):

        @pl.when(i == m)
        def _():
            at = 0
            for band, proj in enumerate(projections):
                part = slice(at, at + proj.shape[2])
                product = dot_nn(pieces[m][band], proj[0])
                acc_ref[:, part] = acc_ref[:, part] + product if m else product
                at += proj.shape[2]

    @pl.when(i == splits - 1)
    def _():
        tail_softmax(acc_ref, outs, red_ref, e_ref, ex_ref)


def tail_softmax(acc_ref, outs, red_ref, e_ref, ex_ref):
    red_ref[...] = acc_ref[...].astype(BF16)
    slots = red_ref.shape[0]
    at = to = 0
    ones = []
    for band, outw in enumerate(outs):
        size, cols = outw.shape[1:]
        logits = dot_nn(red_ref[:, at : at + size], outw[0])
        peak = jnp.max(logits, axis=1, keepdims=True)
        expd = jnp.exp(logits - peak)
        e_ref[:, to : to + cols] = expd.astype(BF16)
        ones += [peak, jnp.sum(expd, axis=1, keepdims=True)]
        at += size
        to += cols
    lane = lanes_of((slots, LANES))
    both = jnp.zeros((slots, LANES), F32)
    for i, one in enumerate(ones):
        both = jnp.where(lane == i, one, both)
    both = both.T
    for band in range(4):
        ex_ref[0:1, band * slots : (band + 1) * slots] = both[2 * band : 2 * band + 1]
        ex_ref[1:2, band * slots : (band + 1) * slots] = both[2 * band + 1 : 2 * band + 2]
    ex_ref[2:8, :] = jnp.zeros((6, ex_ref.shape[1]), F32)


def tail_grads_kernel(cfg, scal, red_ref, e_ref, digit_ref, *refs):
    splits = cfg
    shares, refs = refs[:splits], refs[splits:]
    outs, (go1, go2, go3, go4, out_ref) = refs[:4], refs[4:]
    slots = red_ref.shape[0]
    top, total = merged_stats([share[...] for share in shares], splits, 0)
    scale = jnp.exp(shares[0][0:1, :] - top) / total
    cols = columns_of([scale[:, b * slots : (b + 1) * slots] for b in range(4)])
    at = to = 0
    for band, (outw, go) in enumerate(zip(outs, (go1, go2, go3, go4))):
        size, vcols = outw.shape[1:]
        digits = digit_ref[band].astype(F32).astype(I32)
        word = digits[:, 0:1] * 256 + digits[:, 1:2]
        valid = digits[:, 2:3] > 0
        local = lax.rem(word, vcols * splits) - scal[0] * vcols
        probs = e_ref[:, to : to + vcols].astype(F32) * cols[:, band : band + 1]
        probs = jnp.where(lanes_of(probs.shape) == local, probs - 1.0, probs)
        dlog = jnp.where(valid, probs, 0.0).astype(BF16)
        out_ref[:, at : at + size] = dot_nt(dlog, outw[0])
        go[0] = dot_tn(red_ref[:, at : at + size], dlog).astype(BF16)
        at += size
        to += vcols


def tail_back_kernel(cfg, scal, part, far, rows_ref, p1, p2, p3, p4, g1, g2, g3, g4, back_ref):
    dred = (part[...].astype(F32) + far[...].astype(F32)).astype(BF16)
    at = 0
    for band, (proj, grad) in enumerate(zip((p1, p2, p3, p4), (g1, g2, g3, g4))):
        size = proj.shape[2]
        mine = dred[:, at : at + size]
        back_ref[band] = dot_nt(mine, proj[0]).astype(BF16)
        grad[0] = dot_tn(rows_ref[band], mine).astype(BF16)
        at += size


def add_kernel(cfg, scal, first_ref, second_ref, out_ref):
    total = first_ref[...].astype(F32) + second_ref[...].astype(F32)
    out_ref[...] = total.reshape(out_ref.shape).astype(BF16)


def final_kernel(cfg, scal, dt_ref, ret_ref, keep_ref, beside_ref, far_ref, out_ref):
    tail = dot_nn(dt_ref[...], ret_ref[...])
    head = keep_ref[0].astype(F32) + beside_ref[0].astype(F32) + far_ref[...].astype(F32)
    out_ref[...] = (head + tail).astype(BF16)


def body(
    hidden,
    target_cluster,
    target_word,
    head_words,
    head_clusters,
    proj_one,
    proj_two,
    proj_three,
    proj_four,
    out_one,
    out_two,
    out_three,
    out_four,
):
    groups = lax.axis_size("vocab")
    splits = lax.axis_size("tp")
    v_index = lax.axis_index("vocab")
    tp_index = lax.axis_index("tp")
    tok_rows, width = hidden.shape
    capacity = tok_rows // (4 * groups)
    clusters = 4 * groups
    slots = groups * capacity
    word_cols = head_words.shape[1]
    clus_cols = head_clusters.shape[1]
    own_width = width // splits
    line = 4
    near = groups // line
    line_index = v_index // near
    near_index = v_index % near
    quarter = tok_rows // splits
    out_rows = width // groups
    block = 512
    blocks = word_cols // block
    scalars = jnp.stack([tp_index, line_index, near_index]).astype(I32)
    order = Order(scalars)
    bits = [1 << i for i in range(splits.bit_length() - 1)]

    cluster_row = target_cluster.reshape(1, tok_rows)
    word_row = target_word.reshape(1, tok_rows)
    kind = lax.broadcasted_iota(I32, (8, tok_rows), 0)
    in_tail = cluster_row < clusters
    ids = jnp.where(
        kind == 0,
        jnp.where(in_tail, -1, word_row),
        jnp.where(kind == 1, jnp.where(in_tail, cluster_row, -1), word_row),
    ).astype(F32)
    moved_ids = [
        lax.ppermute(ids, "vocab", [(i, (i + step * near) % groups) for i in range(groups)])
        for step in range(1, line)
    ]

    def line_ids():
        moved = jnp.stack(moved_ids, axis=1)
        for bit in bits:
            parts = moved.reshape(8, line - 1, splits // (2 * bit), 2, bit * quarter)
            moved = jnp.where((tp_index // bit) % 2 == 1, parts[:, :, :, ::-1], parts)
        return moved.reshape(8, (line - 1) * tok_rows)

    ring = [(i, (i + near) % groups) for i in range(groups)]
    piece = lax.dynamic_slice_in_dim(hidden, tp_index * quarter, quarter, 0)
    from_line = {1: lax.ppermute(piece, "vocab", ring)}
    across = {}
    chunks = {0: [hidden]}

    def move_rows(stage):
        values = []
        if stage < line:
            values.append(from_line[stage])
        if stage > 1:
            values.append(across[stage - 1])
        values = order.hold(*values)
        if stage < line:
            held = values[0]
            if stage + 1 < line:
                from_line[stage + 1] = lax.ppermute(held, "vocab", ring)
            across[stage] = tp_swap(held, 2)
            chunks[stage] = [held, tp_swap(held, 1)]
        if stage > 1:
            chunks[stage - 1] += [values[-1], tp_swap(values[-1], 1)]

    clus_padded = jnp.pad(head_clusters, ((0, 0), (0, LANES - clus_cols)))
    row_block = pl.BlockSpec((tok_rows, block), lambda i, s: (0, i))
    lane_block = pl.BlockSpec((tok_rows, LANES), lambda i, s: (0, 0))
    stat_block = pl.BlockSpec((8, tok_rows), lambda i, s: (0, 0))

    def head_logits(pieces):
        tok = sum(p.shape[0] for p in pieces)
        return order.call(
            logits_kernel,
            (len(pieces), clus_cols),
            "head_logits" if len(pieces) == 1 else "line_logits",
            (*pieces, head_words, clus_padded),
            [whole(p) for p in pieces]
            + [pl.BlockSpec((width, block), lambda i, s: (0, i)), whole(clus_padded)],
            [
                struct((tok, word_cols), BF16),
                struct((tok, LANES), BF16),
                struct((tok, LANES), F32),
                struct((8, tok), F32),
            ],
            [
                pl.BlockSpec((tok, block), lambda i, s: (0, i)),
                pl.BlockSpec((tok, LANES), lambda i, s: (0, 0)),
                pl.BlockSpec((tok, LANES), lambda i, s: (0, 0)),
                pl.BlockSpec((8, tok), lambda i, s: (0, 0)),
            ],
            [pltpu.VMEM((tok, 1), F32)] * 2,
            (blocks,),
        )

    def shared(stats):
        return [tp_swap(stats, step) for step in range(1, splits)]

    def added(first, second, step, specs=None):
        out = struct(first.shape[-2:], BF16)
        total = order.call(
            add_kernel,
            None,
            "add",
            (first, second),
            specs or [whole(first), whole(second)],
            out,
            whole(out),
        )
        return total, tp_swap(total, step)

    projections = (proj_one, proj_two, proj_three, proj_four)
    outputs = (out_one, out_two, out_three, out_four)
    reduced_width = sum(p.shape[2] for p in projections)
    vocab_cols = sum(o.shape[2] for o in outputs)
    proj_specs = [
        pl.BlockSpec((1, own_width, p.shape[2]), lambda i, s: (0, s[0], 0)) for p in projections
    ]
    out_specs = [whole(o) for o in outputs]
    band_sums = struct((slots, reduced_width), F32)

    def tail_send():
        sent = struct((tok_rows, own_width + LANES), BF16)
        place = struct((tok_rows, tok_rows), BF16)
        dispatch, send = order.call(
            send_kernel,
            (groups, capacity),
            "send_rows",
            (ids, hidden),
            [whole(ids), pl.BlockSpec((tok_rows, own_width), lambda i, s: (0, s[0]))],
            [place, sent],
            [whole(place), whole(sent)],
        )
        recv = lax.all_to_all(
            send.reshape(groups, 4 * capacity, own_width + LANES),
            "vocab",
            split_axis=0,
            concat_axis=0,
            tiled=True,
        )
        rows = recv.reshape(groups, 4, capacity, own_width + LANES).transpose(1, 0, 2, 3)
        rows = rows.reshape(4, slots, own_width + LANES)
        return dispatch, rows[:, :, :own_width], rows[:, :, own_width:]

    def tail_logits():
        outs = [
            struct((slots, reduced_width), BF16),
            struct((slots, vocab_cols), BF16),
            struct((8, 4 * slots), F32),
        ]
        proj_parts = [
            pl.BlockSpec((1, own_width, p.shape[2]), lambda i, s: (0, s[0] ^ i, 0)) for p in projections
        ]
        return order.call(
            tail_logits_kernel,
            splits,
            "tail_logits",
            (*all_rows, *projections, *outputs),
            [whole(r) for r in all_rows] + proj_parts + out_specs,
            outs,
            [whole(o) for o in outs],
            [pltpu.VMEM((slots, reduced_width), F32)],
            (splits,),
        )

    def tail_grads():
        *grads_out, partial = order.call(
            tail_grads_kernel,
            splits,
            "tail_grads",
            (reduced, tail_expd, digits, tail_stats, *tail_shares, *outputs),
            [whole(reduced), whole(tail_expd), whole(digits)] + [whole(tail_stats)] * splits + out_specs,
            [struct(o.shape, BF16) for o in outputs] + [band_sums],
            out_specs + [whole(band_sums)],
        )
        return grads_out, partial, tp_swap(partial, 1)

    def tail_back():
        outs = [struct((1, own_width, p.shape[2]), BF16) for p in projections]
        outs.append(struct((4, slots, own_width), BF16))
        *grads_proj, back = order.call(
            tail_back_kernel,
            None,
            "tail_back",
            (part, far, rows, *projections),
            [whole(part), whole(far), whole(rows)] + proj_specs,
            outs,
            [whole(o) for o in outs],
        )
        back = back.reshape(4, groups, capacity, own_width).transpose(1, 0, 2, 3)
        returned = lax.all_to_all(
            back.reshape(groups, 4 * capacity, own_width),
            "vocab",
            split_axis=0,
            concat_axis=0,
            tiled=True,
        )
        return grads_proj, returned.reshape(tok_rows, own_width)

    def head_back():
        count = splits // 2

        def part_of(i):
            return jnp.where(i < count, 2 * i + 1, 2 * (i - count))

        pair = struct((count, tok_rows, own_width), BF16)
        give, keep = order.call(
            back_kernel,
            (splits, block, clus_cols),
            "head_back",
            (*own_expd, ids, own_stats, *early, head_words, clus_padded),
            [whole(v) for v in own_expd]
            + [stat_block] * (1 + splits)
            + [
                pl.BlockSpec((own_width, word_cols), lambda i, s: (s[0] ^ part_of(i), 0)),
                pl.BlockSpec((own_width, LANES), lambda i, s: (s[0] ^ part_of(i), 0)),
            ],
            [pair, pair],
            [
                pl.BlockSpec((1, tok_rows, own_width), lambda i, s: (jnp.minimum(i, count - 1), 0, 0)),
                pl.BlockSpec((1, tok_rows, own_width), lambda i, s: (jnp.maximum(i - count, 0), 0, 0)),
            ],
            [
                pltpu.VMEM((tok_rows, word_cols), BF16),
                pltpu.VMEM((tok_rows, LANES), BF16),
                pltpu.VMEM((tok_rows, LANES), F32),
            ],
            (splits,),
        )
        return keep, tp_swap(give, 1)

    def grad_hidden_step():
        out = struct((tok_rows, own_width), BF16)
        pair = pl.BlockSpec((1, tok_rows, own_width), lambda i, s: (0, 0, 0))
        return order.call(
            final_kernel,
            None,
            "grad_hidden",
            (dispatch, returned, back_keep, back_beside, back_far),
            [whole(dispatch), whole(returned), pair, pair, whole(back_far)],
            out,
            whole(out),
        )

    def turned_rows():
        pieces = [piece for step in range(line) for piece in chunks[step]]
        out = struct((near * out_rows, line * tok_rows), BF16)
        return order.call(
            turn_kernel,
            (near, len(pieces)),
            "turned_rows",
            pieces,
            [pl.BlockSpec((p.shape[0], near * out_rows), lambda i, s: (0, s[1])) for p in pieces],
            out,
            whole(out),
        )

    def weight_grads(half, count, columns):
        steps = blocks // count
        rest = (near - 1) * out_rows
        outs = [struct((out_rows, steps * block), BF16), struct((rest, steps * block), BF16)]
        specs = [pl.BlockSpec((o.shape[0], block), lambda i, s: (0, i)) for o in outs]
        operands = [turned, own_expd[0], line_expd[0], own_expd[2], line_expd[2]]
        in_specs = [
            whole(turned),
            pl.BlockSpec((tok_rows, block), lambda i, s: (0, i + half * steps)),
            pl.BlockSpec(((line - 1) * tok_rows, block), lambda i, s: (0, i + half * steps)),
            whole(own_expd[2]),
            whole(line_expd[2]),
        ]
        if columns is None:
            extra = [ids, line_ids(), own_stats, *early, *late]
            more = [struct((line * tok_rows, LANES), F32)]
        else:
            extra = [columns, own_expd[1], line_expd[1]]
            more = [struct((out_rows, LANES), BF16), struct((rest, LANES), BF16)]
        return order.call(
            weights_kernel,
            (splits, quarter, clus_cols, word_cols, line, half * steps, columns is not None),
            "head_weights",
            operands + extra,
            in_specs + [whole(v) for v in extra],
            outs + more,
            specs + [whole(o) for o in more],
            [pltpu.VMEM((line * tok_rows, block), BF16)],
            (steps,),
        )

    def near_sum(own, rest):
        total = own.astype(F32)
        for step in range(1, near):
            part = rest[(step - 1) * out_rows : step * out_rows]
            total = total + lax.ppermute(part, "vocab", xor_pairs(groups, step)).astype(F32)
        return total.astype(BF16)

    dispatch, rows, digits = tail_send()
    move_rows(1)
    *own_expd, own_stats = head_logits(chunks[0])
    early = shared(own_stats)
    move_rows(2)
    across_rows, beside_rows = tp_swap(rows, 2), tp_swap(rows, 1)
    back_keep, back_beside = head_back()
    (across_rows,) = order.hold(across_rows)
    all_rows = [rows, beside_rows, across_rows, tp_swap(across_rows, 1)]
    move_rows(3)
    reduced, tail_expd, tail_stats = tail_logits()
    tail_shares = shared(tail_stats)
    second = pl.BlockSpec((1, tok_rows, own_width), lambda i, s: (1, 0, 0))
    _, back_far = added(back_keep, back_beside, 2, [second, second])
    move_rows(4)
    turned = turned_rows()
    grads_out, part, beside = tail_grads()
    part, far = added(part, beside, 2)
    *line_expd, line_stats = head_logits([p for step in range(1, line) for p in chunks[step]])
    late = [line_stats] + shared(line_stats)
    grads_proj, returned = tail_back()
    own, rest, columns = weight_grads(0, 2, None)
    sums = [near_sum(own, rest)]
    own, rest, own_clus, rest_clus = weight_grads(1, 2, columns)
    sums.append(near_sum(own, rest))
    clus_sum = near_sum(own_clus, rest_clus)[:, :clus_cols]
    grad_hidden = grad_hidden_step()
    return (
        grad_hidden,
        jnp.concatenate(sums, axis=1),
        clus_sum,
        *grads_proj,
        *grads_out,
    )


def solution(mesh):
    return jax.shard_map(
        body,
        mesh=mesh,
        in_specs=(
            P("vocab", None),
            P("vocab", None),
            P("vocab"),
            P(None, "tp"),
            P(None, "tp"),
            P("vocab", None, None),
            P("vocab", None, None),
            P("vocab", None, None),
            P("vocab", None, None),
            P("vocab", None, "tp"),
            P("vocab", None, "tp"),
            P("vocab", None, "tp"),
            P("vocab", None, "tp"),
        ),
        out_specs=(
            P("vocab", "tp"),
            P("vocab", "tp"),
            P("vocab", "tp"),
            P("vocab", "tp", None),
            P("vocab", "tp", None),
            P("vocab", "tp", None),
            P("vocab", "tp", None),
            P("vocab", None, "tp"),
            P("vocab", None, "tp"),
            P("vocab", None, "tp"),
            P("vocab", None, "tp"),
        ),
        check_vma=False,
    )
```

time: 345 us -> 203 us (0.59)
  waiting for transfers between devices: 188 us -> 40.7 us
  Pallas kernels: 0 us -> 104 us
  matrix products: 66.5 us -> 0 us
  blocking collectives: 33.2 us -> 0 us
  starting transfers between devices: 17.3 us -> 36.3 us
  between operations: 14.5 us -> 1.01 us
  other arithmetic: 12.7 us -> 4.77 us
    reduce_scatter x2 -> x0, waiting for transfers between devices: 159 us -> none  [the longest x1 150 us: body(): lax.psum_scatter(jnp.dot(hidden.T, grads_cat, preferred_element_type=jnp....]
    pallas_call x0 -> x18, Pallas kernels: none -> 104 us  [the longest x13 104 us: kernel_call(): pl.pallas_call(kernel, name=name, out_shape=outs, grid_spec=pltpu.Prefetc...]
    dot_general x31 -> x0, matrix products: 66.5 us -> none  [the longest x1 9.54 us: body(): jnp.dot(grad_words, head_words.T, preferred_element_type=jnp.float32)]
    ppermute x0 -> x34, waiting for transfers between devices: none -> 37.6 us  [the longest x25 14 us: tp_swap(): return lax.ppermute(value, 'tp', xor_pairs(lax.axis_size('tp'), step))]
    ppermute x0 -> x34, starting transfers between devices: none -> 27 us  [the longest x25 14.8 us: tp_swap(): return lax.ppermute(value, 'tp', xor_pairs(lax.axis_size('tp'), step))]
    all_to_all x3 -> x2, waiting for transfers between devices: 28.5 us -> 3.1 us  [the longest x1 2.45 us: tail_send(): lax.all_to_all(send.reshape(groups, 4 * capacity, own_width + LANES), 'vo...]
    all_gather x4 -> x0, blocking collectives: 20.8 us -> none  [combined_all(): pieces = jax.tree.map(lambda part: lax.all_gather(part, axis), value)]
    psum x1 -> x0, blocking collectives: 12.4 us -> none  [body(): lax.psum(partials[3].astype(jnp.bfloat16), 'tp').astype(jnp.float32)]
  transfers between devices with their start and end apart: 6 -> 36, of which waited for: 5 -> 10; matrix products, arithmetic and copies ran while one was open for 16% -> 4% of each run, Pallas kernels for 0% -> 41%
where the time goes in v1:
time: 203 us; the launch traced here: 202 us
  Pallas kernels  104 us (51%)
  waiting for transfers between devices  40.7 us (20%)
  starting transfers between devices  36.3 us (18%)
  local copies, waits for them, and re-layouts  15.5 us (8%)
  other arithmetic  4.77 us (2%)
    pallas_call x13, Pallas kernels, kernel_call(): pl.pallas_call(kernel, name=name, out_shape=outs, grid_spec=pltpu.Prefetc...  104 us
    ppermute x25, starting transfers between devices, tp_swap(): return lax.ppermute(value, 'tp', xor_pairs(lax.axis_size('tp'), step))  14.8 us
    ppermute x25, waiting for transfers between devices, tp_swap(): return lax.ppermute(value, 'tp', xor_pairs(lax.axis_size('tp'), step))  14 us
    unnamed x70, local copies, waits for them, and re-layouts  11.9 us
    ppermute x3, waiting for transfers between devices, near_sum(): lax.ppermute(part, 'vocab', xor_pairs(groups, step)).astype(F32)  11.1 us
    ppermute x2, waiting for transfers between devices, move_rows(): from_line[stage + 1] = lax.ppermute(held, 'vocab', ring)  9.4 us
    all_to_all x1, starting transfers between devices, tail_send(): lax.all_to_all(send.reshape(groups, 4 * capacity, own_width + LANES), 'vo...  4.79 us
    all_to_all x1, starting transfers between devices, tail_back(): lax.all_to_all(back.reshape(groups, 4 * capacity, own_width), 'vocab', sp...  4.54 us
  transfers between devices with their start and end apart: 36, of which 10 were waited for; matrix products, arithmetic and copies ran while one was open for 4% of the time, Pallas kernels for 41%

profile of v1, /device:TPU:0, one launch (start us, length us, event | category | flops | bytes accessed | tf_op | source)
XLA Modules:
  0.0 202.3 jit_solution(11738225522412509937)
XLA Ops:
  0.6 1.1 constant_dynamic-slice_fusion
  1.7 3.1 %collective-permute-start.2 = (bf16[128,2048]{1,0:T(8,128)(2,1)S(1)}, bf16[128,2048]{1,0:T(8,128)(2,1)}, u32[]{:S(2)}, u32[]{:S(2)}) collective-permute-start(bf16[128,2048]{1,0:T(8,128)(2,1)S(1)} %constant_dynamic-slice_fusion), channel_id=1, source_target_pairs={{0,8},{4,12},{8,16},{12,20},{16,24},{20,28},{24,0},{28,4},{1,9},{5... | collective-permute-start | bytes 1572872 | tf_op jit(solution)/shard_map/ppermute | solution.py:485
  4.8 0.7 compare_select_fusion.1
  5.5 0.6 pad_add_fusion.scal
  6.1 1.4 select_convert_fusion.ids_ref.refs_3_.refs_5_
  7.5 4.5 %send_rows.1 = (bf16[512,512]{1,0:T(8,128)(2,1)}, bf16[512,640]{1,0:T(8,128)(2,1)}) custom-call(s32[3]{0:T(128)} %pad_add_fusion.scal, f32[8,512]{1,0:T(8,128)} %select_convert_fusion.ids_ref.refs_3_.refs_5_, bf16[512,2048]{1,0:T(8,128)(2,1)} %refs_0_.3), custom_call_target="tpu_custom_call" | custom-call | flops 3000000000 | bytes 1 | tf_op jit(solution)/shard_map/send_rows/pallas_call | solution.py:65
  12.0 4.8 %all-to-all-start = ((bf16[8,64,640]{2,1,0:T(8,128)(2,1)}), bf16[8,64,640]{2,1,0:T(8,128)(2,1)S(1)}, u32[]{:S(2)}, u32[]{:S(2)}) async-start(bf16[8,64,640]{2,1,0:T(8,128)(2,1)} %bitcast.23), calls=%async_computation | async-start | bytes 1310720 | tf_op jit(solution)/shard_map/all_to_all | solution.py:573
  17.0 0.9 pad.4.refs_2_.refs_9_.refs_13_
  17.9 0.9 collective-permute-done.2.refs_0_
  18.9 1.1 collective-permute-start.6
  20.0 1.5 collective-permute-start.7
  21.5 11.7 %head_logits.1 = (bf16[512,2048]{1,0:T(8,128)(2,1)}, bf16[512,128]{1,0:T(8,128)(2,1)}, f32[512,128]{1,0:T(8,128)}, f32[8,512]{1,0:T(8,128)}) custom-call(s32[3]{0:T(128)} %pad_add_fusion.scal, bf16[512,2048]{1,0:T(8,128)(2,1)} %refs_0_.3, bf16[2048,2048]{1,0:T(8,128)(2,1)} %refs_12_.1, bf16[2048,128]{1,0:T(8,128)(2,1)} %pad.4.refs_2_.refs_9_.refs_13_, ...), custom_call_target="tpu_custom_call" | custom-call | flops 8999999488 | bytes 1 | tf_op jit(solution)/shard_map/head_logits/pallas_call | solution.py:65
  33.2 0.6 collective-permute-start.4
  33.8 1.3 collective-permute-start.5
  35.1 7.5 %collective-permute-done.6.refs_0_ = bf16[128,2048]{1,0:T(8,128)(2,1)} collective-permute-done((bf16[128,2048]{1,0:T(8,128)(2,1)}, bf16[128,2048]{1,0:T(8,128)(2,1)}, u32[]{:S(2)}, u32[]{:S(2)}) %collective-permute-start.6) | collective-permute-done | bytes 524320 | tf_op jit(solution)/shard_map/ppermute | solution.py:499
  42.6 2.5 %all-to-all-done = bf16[8,64,640]{2,1,0:T(8,128)(2,1)S(1)} async-done(((bf16[8,64,640]{2,1,0:T(8,128)(2,1)}), bf16[8,64,640]{2,1,0:T(8,128)(2,1)S(1)}, u32[]{:S(2)}, u32[]{:S(2)}) %all-to-all-start) | async-done | bytes 655392 | tf_op jit(solution)/shard_map/all_to_all | solution.py:573
  45.1 1.6 collective-permute-start.1
  47.3 12.2 %head_back.1 = (bf16[2,512,512]{2,1,0:T(8,128)(2,1)}, bf16[2,512,512]{2,1,0:T(8,128)(2,1)}) custom-call(s32[3]{0:T(128)} %pad_add_fusion.scal, bf16[512,2048]{1,0:T(8,128)(2,1)} %get-tuple-element.49.refs_0_.refs_1_, bf16[512,128]{1,0:T(8,128)(2,1)} %get-tuple-element.50.refs_1_.refs_6_, f32[512,128]{1,0:T(8,128)} %get-tuple-element.51.refs_2_.refs_3_, ...), custom_call_target="tpu_custom_call" | custom-call | flops 8999999488 | bytes 1 | tf_op jit(solution)/shard_map/head_back/pallas_call | solution.py:65
  60.1 0.6 collective-permute-start.9
  60.7 0.8 copy-done.12
  62.0 12.2 %collective-permute-done.10.refs_1_ = bf16[128,2048]{1,0:T(8,128)(2,1)} collective-permute-done((bf16[128,2048]{1,0:T(8,128)(2,1)}, bf16[128,2048]{1,0:T(8,128)(2,1)}, u32[]{:S(2)}, u32[]{:S(2)}) %collective-permute-start.10) | collective-permute-done | bytes 524320 | tf_op jit(solution)/shard_map/ppermute | solution.py:21
  74.2 1.9 collective-permute-done.9.refs_0_
  76.1 0.8 copy-done.11
  77.0 0.8 copy-done.23
  77.7 1.5 collective-permute-start.19
  79.3 8.7 %tail_logits.1 = (bf16[128,1920]{1,0:T(8,128)(2,1)}, bf16[128,3840]{1,0:T(8,128)(2,1)}, f32[8,512]{1,0:T(8,128)}) custom-call(s32[3]{0:T(128)} %pad_add_fusion.scal, bf16[4,128,512]{2,1,0:T(8,128)(2,1)} %copy-done.17, bf16[4,128,512]{2,1,0:T(8,128)(2,1)} %collective-permute-done.refs_1_, bf16[4,128,512]{2,1,0:T(8,128)(2,1)} %hold.7.refs_2_, ...), custom_call_target="tpu_custom_call" | custom-call | flops 5000000000 | bytes 1 | tf_op jit(solution)/shard_map/tail_logits/pallas_call | solution.py:65
  88.3 0.8 copy-done.8
  89.1 0.7 add.43.refs_1_
  89.7 0.8 copy-done.1
  90.6 1.7 collective-permute-done.19.refs_0_
  92.3 0.8 copy-done.10
  93.1 0.7 slice.13.refs_2_
  94.3 1.5 collective-permute-start.12
  95.9 0.8 copy-done.13
  96.6 0.8 copy-done.14
  97.4 4.2 %turned_rows.1.refs_11_.refs_0_ = bf16[512,2048]{1,0:T(8,128)(2,1)} custom-call(s32[3]{0:T(128)} %pad_add_fusion.scal, bf16[512,2048]{1,0:T(8,128)(2,1)} %refs_0_.3, bf16[128,2048]{1,0:T(8,128)(2,1)} %hold.5.refs_3_.refs_1_.refs_0_, bf16[128,2048]{1,0:T(8,128)(2,1)} %collective-permute-done.14.refs_2_.refs_1_, ...), custom_call_target="tpu_custom_call" | custom-call | flops 2000000000 | bytes 1 | tf_op jit(solution)/shard_map/turned_rows/pallas_call | solution.py:65
  102.3 5.6 %tail_grads.1 = (bf16[1,1024,256]{2,1,0:T(8,128)(2,1)}, bf16[1,512,512]{2,1,0:T(8,128)(2,1)}, bf16[1,256,1024]{2,1,0:T(8,128)(2,1)}, bf16[1,128,2048]{2,1,0:T(8,128)(2,1)}, f32[128,1920]{1,0:T(8,128)}) custom-call(s32[3]{0:T(128)} %pad_add_fusion.scal, bf16[128,1920]{1,0:T(8,128)(2,1)} %get-tuple-element.57.refs_0_, ...), custom_call_target="tpu_custom_call" | custom-call | flops 3000000000 | bytes 1 | tf_op jit(solution)/shard_map/tail_grads/pallas_call | solution.py:65
  107.8 0.6 collective-permute-start.22
  108.7 3.6 %collective-permute-start.27 = (f32[8,512]{1,0:T(8,128)S(1)}, f32[8,512]{1,0:T(8,128)S(1)}, u32[]{:S(2)}, u32[]{:S(2)}) collective-permute-start(f32[8,512]{1,0:T(8,128)S(1)} %copy-done.22), channel_id=1, source_target_pairs={{0,24},{4,28},{8,0},{12,4},{16,8},{20,12},{24,16},{28,20},{1,25},{... | collective-permute-start | bytes 49160 | tf_op jit(solution)/shard_map/ppermute | solution.py:472
  112.3 1.7 collective-permute-done.25
  114.6 0.6 reverse_select_fusion
  115.2 1.2 copy-done.6
  116.4 0.7 add.44.refs_14_.refs_0_
  117.1 1.6 collective-permute-start.23
  118.7 23.7 %line_logits.1 = (bf16[1536,2048]{1,0:T(8,128)(2,1)}, bf16[1536,128]{1,0:T(8,128)(2,1)}, f32[1536,128]{1,0:T(8,128)}, f32[8,1536]{1,0:T(8,128)}) custom-call(s32[3]{0:T(128)} %pad_add_fusion.scal, bf16[128,2048]{1,0:T(8,128)(2,1)} %hold.5.refs_3_.refs_1_.refs_0_, bf16[128,2048]{1,0:T(8,128)(2,1)} %collective-permute-done.14.refs_2_.refs_1_, ...), custom_call_target="tpu_custom_call" | custom-call | flops 20000000000 | bytes 1 | tf_op jit(solution)/shard_map/line_logits/pallas_call | solution.py:65
  142.5 0.8 collective-permute-start.29
  143.3 1.1 collective-permute-start.30
  144.4 0.8 copy-done.24
  145.2 4.8 %tail_back.1 = (bf16[1,512,1024]{2,1,0:T(8,128)(2,1)}, bf16[1,512,512]{2,1,0:T(8,128)(2,1)}, bf16[1,512,256]{2,1,0:T(8,128)(2,1)}, bf16[1,512,128]{2,1,0:T(8,128)(2,1)}, bf16[4,128,512]{2,1,0:T(8,128)(2,1)}) custom-call(s32[3]{0:T(128)} %pad_add_fusion.scal, bf16[128,1920]{1,0:T(8,128)(2,1)} %copy-done.7, bf16[128,1920]{1,0:T(8,128)(2,1)} %copy-done.24, ...), custom_call_target="tpu_custom_call" | custom-call | flops 3000000000 | bytes 1 | tf_op jit(solution)/shard_map/tail_back/pallas_call | solution.py:65
  150.0 0.6 copy-done.25
  150.6 10.4 %head_weights.2 = (bf16[256,1024]{1,0:T(8,128)(2,1)}, bf16[256,1024]{1,0:T(8,128)(2,1)}, f32[2048,128]{1,0:T(8,128)}) custom-call(s32[3]{0:T(128)} %pad_add_fusion.scal, bf16[512,2048]{1,0:T(8,128)(2,1)} %turned_rows.1.refs_11_.refs_0_, bf16[512,2048]{1,0:T(8,128)(2,1)} %get-tuple-element.49.refs_0_.refs_1_, bf16[1536,2048]{1,0:T(8,128)(2,1)} %get-tuple-element.65.refs_2_, ...), custom_call_target="tpu_custom_call" | custom-call | flops 8000000000 | bytes 1 | tf_op jit(solution)/shard_map/head_weights/pallas_call | solution.py:65
  161.0 1.5 collective-permute-start.31
  162.6 13.2 %head_weights.3 = (bf16[256,1024]{1,0:T(8,128)(2,1)}, bf16[256,1024]{1,0:T(8,128)(2,1)}, bf16[256,128]{1,0:T(8,128)(2,1)}, bf16[256,128]{1,0:T(8,128)(2,1)}) custom-call(s32[3]{0:T(128)} %pad_add_fusion.scal, bf16[512,2048]{1,0:T(8,128)(2,1)} %turned_rows.1.refs_11_.refs_0_, bf16[512,2048]{1,0:T(8,128)(2,1)} %get-tuple-element.49.refs_0_.refs_1_, ...), custom_call_target="tpu_custom_call" | custom-call | flops 8000000000 | bytes 1 | tf_op jit(solution)/shard_map/head_weights/pallas_call | solution.py:65
  175.8 0.6 collective-permute-start.33
  176.5 1.5 collective-permute-start.32
  177.9 0.7 collective-permute-start.24
  178.6 0.8 copy.36
  179.5 4.5 %all-to-all-start.1 = ((bf16[8,64,512]{2,1,0:T(8,128)(2,1)}), bf16[8,64,512]{2,1,0:T(8,128)(2,1)S(1)}, u32[]{:S(2)}, u32[]{:S(2)}) async-start(bf16[8,64,512]{2,1,0:T(8,128)(2,1)} %bitcast.10), calls=%async_computation.1 | async-start | bytes 1048576 | tf_op jit(solution)/shard_map/all_to_all | solution.py:630
  184.1 0.7 copy.37
  184.9 11.1 %collective-permute-done.32 = bf16[256,1024]{1,0:T(8,128)(2,1)S(1)} collective-permute-done((bf16[256,1024]{1,0:T(8,128)(2,1)}, bf16[256,1024]{1,0:T(8,128)(2,1)S(1)}, u32[]{:S(2)}, u32[]{:S(2)}) %collective-permute-start.32) | collective-permute-done | bytes 524320 | tf_op jit(solution)/shard_map/ppermute | solution.py:732
  196.2 1.1 pad_maximum_fusion
  197.3 0.6 all-to-all-done.1
  197.9 0.8 copy-done.19
  198.7 3.6 %grad_hidden.1 = bf16[512,512]{1,0:T(8,128)(2,1)} custom-call(s32[3]{0:T(128)} %pad_add_fusion.scal, bf16[512,512]{1,0:T(8,128)(2,1)} %get-tuple-element.47.refs_0_, bf16[512,512]{1,0:T(8,128)(2,1)} %bitcast.25, bf16[2,512,512]{2,1,0:T(8,128)(2,1)} %get-tuple-element.54.refs_1_.refs_0_.refs_2_, bf16[2,512,512]{2,1,0:T(8,128)(2,1)} %copy-done.5, ...), custom_call_target="tpu_custom_call" | custom-call | flops 2000000000 | bytes 1 | tf_op jit(solution)/shard_map/grad_hidden/pallas_call | solution.py:65
  (113 shorter events, 4.9 us)
Async XLA Ops:
  1.7 17.1 %collective-permute-start.2 = (bf16[128,2048]{1,0:T(8,128)(2,1)S(1)}, bf16[128,2048]{1,0:T(8,128)(2,1)}, u32[]{:S(2)}, u32[]{:S(2)}) collective-permute-start(bf16[128,2048]{1,0:T(8,128)(2,1)S(1)} %constant_dynamic-slice_fusion), channel_id=1, source_target_pairs={{0,8},{4,12},{8,16},{12,20},{16,24},{20,28},{24,0},{28,4},{1,9},{5... | collective-permute-start | bytes 1572872 | tf_op jit(solution)/shard_map/ppermute | solution.py:485
  7.5 9.3 %copy-start.21 = (bf16[2048,8]{0,1:T(8,128)(2,1)S(1)}, bf16[2048,8]{0,1:T(8,128)(2,1)}, u32[]{:S(2)}) copy-start(bf16[2048,8]{0,1:T(8,128)(2,1)} %param.17) | copy-start | bytes 98308
  12.0 33.0 %all-to-all-start = ((bf16[8,64,640]{2,1,0:T(8,128)(2,1)}), bf16[8,64,640]{2,1,0:T(8,128)(2,1)S(1)}, u32[]{:S(2)}, u32[]{:S(2)}) async-start(bf16[8,64,640]{2,1,0:T(8,128)(2,1)} %bitcast.23), calls=%async_computation | async-start | bytes 1310720 | tf_op jit(solution)/shard_map/all_to_all | solution.py:573
  18.9 23.7 %collective-permute-start.6 = (bf16[128,2048]{1,0:T(8,128)(2,1)}, bf16[128,2048]{1,0:T(8,128)(2,1)}, u32[]{:S(2)}, u32[]{:S(2)}) collective-permute-start(bf16[128,2048]{1,0:T(8,128)(2,1)} %hold.5.refs_3_.refs_1_.refs_0_), channel_id=1, source_target_pairs={{0,8},{4,12},{8,16},{12,20},{16,24},{20,28},{24,0},{28,4},{1,9},{5... | collective-permute-start | bytes 1572872 | tf_op jit(solution)/shard_map/ppermute | solution.py:499
  20.0 22.6 %collective-permute-start.7 = (bf16[128,2048]{1,0:T(8,128)(2,1)}, bf16[128,2048]{1,0:T(8,128)(2,1)}, u32[]{:S(2)}, u32[]{:S(2)}) collective-permute-start(bf16[128,2048]{1,0:T(8,128)(2,1)} %hold.5.refs_3_.refs_1_.refs_0_), channel_id=1, source_target_pairs={{0,2},{1,3},{2,0},{3,1},{4,6},{5,7},{6,4},{7,5},{8,10},{9,11},{10,... | collective-permute-start | bytes 1572872 | tf_op jit(solution)/shard_map/ppermute | solution.py:21
  33.1 13.6 %collective-permute-start.3 = (f32[8,512]{1,0:T(8,128)}, f32[8,512]{1,0:T(8,128)S(1)}, u32[]{:S(2)}, u32[]{:S(2)}) collective-permute-start(f32[8,512]{1,0:T(8,128)} %get-tuple-element.52.refs_2_.refs_4_.refs_7_), channel_id=1, source_target_pairs={{0,1},{1,0},{2,3},{3,2},{4,5},{5,4},{6,7},{7,6},{8,9},{9,8},{10,11... | collective-permute-start | bytes 49160 | tf_op jit(solution)/shard_map/ppermute | solution.py:21
  33.2 13.5 %collective-permute-start.4 = (f32[8,512]{1,0:T(8,128)}, f32[8,512]{1,0:T(8,128)S(1)}, u32[]{:S(2)}, u32[]{:S(2)}) collective-permute-start(f32[8,512]{1,0:T(8,128)} %get-tuple-element.52.refs_2_.refs_4_.refs_7_), channel_id=1, source_target_pairs={{0,2},{1,3},{2,0},{3,1},{4,6},{5,7},{6,4},{7,5},{8,10},{9,11},{10,... | collective-permute-start | bytes 49160 | tf_op jit(solution)/shard_map/ppermute | solution.py:21
  33.8 13.0 %collective-permute-start.5 = (f32[8,512]{1,0:T(8,128)}, f32[8,512]{1,0:T(8,128)S(1)}, u32[]{:S(2)}, u32[]{:S(2)}) collective-permute-start(f32[8,512]{1,0:T(8,128)} %get-tuple-element.52.refs_2_.refs_4_.refs_7_), channel_id=1, source_target_pairs={{0,3},{1,2},{2,1},{3,0},{4,7},{5,6},{6,5},{7,4},{8,11},{9,10},{10,... | collective-permute-start | bytes 49160 | tf_op jit(solution)/shard_map/ppermute | solution.py:21
  45.1 15.6 %copy-start.17 = (bf16[4,128,512]{2,1,0:T(8,128)(2,1)}, bf16[4,128,512]{2,1,0:T(8,128)(2,1)S(1)}, u32[]{:S(2)}) copy-start(bf16[4,128,512]{2,1,0:T(8,128)(2,1)S(1)} %slice.12.refs_0_.refs_2_) | copy-start | bytes 1572868
  45.1 15.6 %collective-permute-start.1 = (bf16[4,128,512]{2,1,0:T(8,128)(2,1)S(1)}, bf16[4,128,512]{2,1,0:T(8,128)(2,1)S(1)}, u32[]{:S(2)}, u32[]{:S(2)}) collective-permute-start(bf16[4,128,512]{2,1,0:T(8,128)(2,1)S(1)} %slice.12.refs_0_.refs_2_), channel_id=1, source_target_pairs={{0,2},{1,3},{2,0},{3,1},{4,6},{5,7},{6,4},{7,5},{8,10},{9,11},{10,... | collective-permute-start | bytes 1572872 | tf_op jit(solution)/shard_map/ppermute | solution.py:21
  59.5 28.4 %collective-permute-start.20 = (bf16[2,512,512]{2,1,0:T(8,128)(2,1)}, bf16[2,512,512]{2,1,0:T(8,128)(2,1)S(1)}, u32[]{:S(2)}, u32[]{:S(2)}) collective-permute-start(bf16[2,512,512]{2,1,0:T(8,128)(2,1)} %get-tuple-element.61), channel_id=1, source_target_pairs={{0,1},{1,0},{2,3},{3,2},{4,5},{5,4},{6,7},{7,6},{8,9},{9,8},{10,11... | collective-permute-start | bytes 3145736 | tf_op jit(solution)/shard_map/ppermute | solution.py:21
  59.6 14.6 %collective-permute-start.10 = (bf16[128,2048]{1,0:T(8,128)(2,1)}, bf16[128,2048]{1,0:T(8,128)(2,1)}, u32[]{:S(2)}, u32[]{:S(2)}) collective-permute-start(bf16[128,2048]{1,0:T(8,128)(2,1)} %get-tuple-element.55.refs_5_.refs_4_), channel_id=1, source_target_pairs={{0,2},{1,3},{2,0},{3,1},{4,6},{5,7},{6,4},{7,5},{8,10},{9,11},{10,... | collective-permute-start | bytes 1572872 | tf_op jit(solution)/shard_map/ppermute | solution.py:21
  60.1 16.0 %collective-permute-start.9 = (bf16[128,2048]{1,0:T(8,128)(2,1)}, bf16[128,2048]{1,0:T(8,128)(2,1)S(1)}, u32[]{:S(2)}, u32[]{:S(2)}) collective-permute-start(bf16[128,2048]{1,0:T(8,128)(2,1)} %get-tuple-element.55.refs_5_.refs_4_), channel_id=1, source_target_pairs={{0,8},{4,12},{8,16},{12,20},{16,24},{20,28},{24,0},{28,4},{1,9},{5... | collective-permute-start | bytes 1572872 | tf_op jit(solution)/shard_map/ppermute | solution.py:499
  60.7 16.2 %collective-permute-start = (bf16[4,128,512]{2,1,0:T(8,128)(2,1)S(1)}, bf16[4,128,512]{2,1,0:T(8,128)(2,1)}, u32[]{:S(2)}, u32[]{:S(2)}) collective-permute-start(bf16[4,128,512]{2,1,0:T(8,128)(2,1)S(1)} %slice.12.refs_0_.refs_2_), channel_id=1, source_target_pairs={{0,1},{1,0},{2,3},{3,2},{4,5},{5,4},{6,7},{7,6},{8,9},{9,8},{10,11... | collective-permute-start | bytes 1572872 | tf_op jit(solution)/shard_map/ppermute | solution.py:21
  60.7 0.8 copy-start.12
  61.5 15.4 %collective-permute-start.8 = (bf16[4,128,512]{2,1,0:T(8,128)(2,1)}, bf16[4,128,512]{2,1,0:T(8,128)(2,1)S(1)}, u32[]{:S(2)}, u32[]{:S(2)}) collective-permute-start(bf16[4,128,512]{2,1,0:T(8,128)(2,1)} %hold.7.refs_2_), channel_id=1, source_target_pairs={{0,1},{1,0},{2,3},{3,2},{4,5},{5,4},{6,7},{7,6},{8,9},{9,8},{10,11... | collective-permute-start | bytes 1572872 | tf_op jit(solution)/shard_map/ppermute | solution.py:21
  74.2 18.9 %collective-permute-start.14 = (bf16[128,2048]{1,0:T(8,128)(2,1)}, bf16[128,2048]{1,0:T(8,128)(2,1)}, u32[]{:S(2)}, u32[]{:S(2)}) collective-permute-start(bf16[128,2048]{1,0:T(8,128)(2,1)} %hold.5.refs_3_.refs_1_.refs_0_), channel_id=1, source_target_pairs={{0,1},{1,0},{2,3},{3,2},{4,5},{5,4},{6,7},{7,6},{8,9},{9,8},{10,11... | collective-permute-start | bytes 1572872 | tf_op jit(solution)/shard_map/ppermute | solution.py:21
  76.1 0.8 copy-start.11
  76.1 17.7 %collective-permute-start.15 = (bf16[128,2048]{1,0:T(8,128)(2,1)}, bf16[128,2048]{1,0:T(8,128)(2,1)}, u32[]{:S(2)}, u32[]{:S(2)}) collective-permute-start(bf16[128,2048]{1,0:T(8,128)(2,1)} %get-tuple-element.53.refs_10_.refs_3_.refs_2_), channel_id=1, source_target_pairs={{0,1},{1,0},{2,3},{3,2},{4,5},{5,4},{6,7},{7,6},{8,9},{9,8},{10,11... | collective-permute-start | bytes 1572872 | tf_op jit(solution)/shard_map/ppermute | solution.py:21
  76.9 17.4 %collective-permute-start.16 = (bf16[128,2048]{1,0:T(8,128)(2,1)}, bf16[128,2048]{1,0:T(8,128)(2,1)}, u32[]{:S(2)}, u32[]{:S(2)}) collective-permute-start(bf16[128,2048]{1,0:T(8,128)(2,1)} %get-tuple-element.55.refs_5_.refs_4_), channel_id=1, source_target_pairs={{0,1},{1,0},{2,3},{3,2},{4,5},{5,4},{6,7},{7,6},{8,9},{9,8},{10,11... | collective-permute-start | bytes 1572872 | tf_op jit(solution)/shard_map/ppermute | solution.py:21
  76.9 0.8 copy-start.23
  77.7 14.5 %collective-permute-start.19 = (bf16[128,2048]{1,0:T(8,128)(2,1)}, bf16[128,2048]{1,0:T(8,128)(2,1)S(1)}, u32[]{:S(2)}, u32[]{:S(2)}) collective-permute-start(bf16[128,2048]{1,0:T(8,128)(2,1)} %get-tuple-element.60.refs_9_.refs_8_), channel_id=1, source_target_pairs={{0,2},{1,3},{2,0},{3,1},{4,6},{5,7},{6,4},{7,5},{8,10},{9,11},{10,... | collective-permute-start | bytes 1572872 | tf_op jit(solution)/shard_map/ppermute | solution.py:21
  79.3 9.0 %copy-start = (bf16[2,512,512]{2,1,0:T(8,128)(2,1)S(1)}, bf16[2,512,512]{2,1,0:T(8,128)(2,1)}, u32[]{:S(2)}) copy-start(bf16[2,512,512]{2,1,0:T(8,128)(2,1)} %get-tuple-element.54.refs_1_.refs_0_.refs_2_) | copy-start | bytes 3145732
  79.3 9.0 %copy-start.3 = (s32[3]{0:T(128)S(1)}, s32[3]{0:T(128)}, u32[]{:S(2)}) copy-start(s32[3]{0:T(128)} %pad_add_fusion.scal) | copy-start | bytes 40
  88.0 5.1 %copy-start.5 = (bf16[2,512,512]{2,1,0:T(8,128)(2,1)}, bf16[2,512,512]{2,1,0:T(8,128)(2,1)S(1)}, u32[]{:S(2)}) copy-start(bf16[2,512,512]{2,1,0:T(8,128)(2,1)S(1)} %collective-permute-done.20.refs_1_.refs_3_) | copy-start | bytes 3145732
  88.0 7.8 %collective-permute-start.17 = (bf16[128,2048]{1,0:T(8,128)(2,1)}, bf16[128,2048]{1,0:T(8,128)(2,1)}, u32[]{:S(2)}, u32[]{:S(2)}) collective-permute-start(bf16[128,2048]{1,0:T(8,128)(2,1)} %get-tuple-element.56.refs_12_.refs_7_.refs_6_), channel_id=1, source_target_pairs={{0,1},{1,0},{2,3},{3,2},{4,5},{5,4},{6,7},{7,6},{8,9},{9,8},{10,11... | collective-permute-start | bytes 1572872 | tf_op jit(solution)/shard_map/ppermute | solution.py:21
  88.3 0.8 copy-start.8
  89.1 4.7 %copy-start.9 = (f32[8,512]{1,0:T(8,128)S(1)}, f32[8,512]{1,0:T(8,128)}, u32[]{:S(2)}) copy-start(f32[8,512]{1,0:T(8,128)} %get-tuple-element.59.refs_2_.refs_3_) | copy-start | bytes 49156
  89.7 0.8 copy-start.1
  92.3 0.8 copy-start.10
  92.3 3.6 %collective-permute-start.18 = (bf16[128,2048]{1,0:T(8,128)(2,1)}, bf16[128,2048]{1,0:T(8,128)(2,1)S(1)}, u32[]{:S(2)}, u32[]{:S(2)}) collective-permute-start(bf16[128,2048]{1,0:T(8,128)(2,1)} %get-tuple-element.60.refs_9_.refs_8_), channel_id=1, source_target_pairs={{0,1},{1,0},{2,3},{3,2},{4,5},{5,4},{6,7},{7,6},{8,9},{9,8},{10,11... | collective-permute-start | bytes 1572872 | tf_op jit(solution)/shard_map/ppermute | solution.py:21
  93.1 2.8 %collective-permute-start.21 = (bf16[128,2048]{1,0:T(8,128)(2,1)}, bf16[128,2048]{1,0:T(8,128)(2,1)S(1)}, u32[]{:S(2)}, u32[]{:S(2)}) collective-permute-start(bf16[128,2048]{1,0:T(8,128)(2,1)} %hold.9.refs_11_.refs_13_.refs_10_), channel_id=1, source_target_pairs={{0,1},{1,0},{2,3},{3,2},{4,5},{5,4},{6,7},{7,6},{8,9},{9,8},{10,11... | collective-permute-start | bytes 1572872 | tf_op jit(solution)/shard_map/ppermute | solution.py:21
  93.8 7.8 %collective-permute-start.11 = (f32[8,512]{1,0:T(8,128)S(1)}, f32[8,512]{1,0:T(8,128)S(1)}, u32[]{:S(2)}, u32[]{:S(2)}) collective-permute-start(f32[8,512]{1,0:T(8,128)S(1)} %copy-done.9), channel_id=1, source_target_pairs={{0,1},{1,0},{2,3},{3,2},{4,5},{5,4},{6,7},{7,6},{8,9},{9,8},{10,11... | collective-permute-start | bytes 49160 | tf_op jit(solution)/shard_map/ppermute | solution.py:21
  94.3 7.3 %collective-permute-start.12 = (f32[8,512]{1,0:T(8,128)S(1)}, f32[8,512]{1,0:T(8,128)S(1)}, u32[]{:S(2)}, u32[]{:S(2)}) collective-permute-start(f32[8,512]{1,0:T(8,128)S(1)} %copy-done.9), channel_id=1, source_target_pairs={{0,2},{1,3},{2,0},{3,1},{4,6},{5,7},{6,4},{7,5},{8,10},{9,11},{10,... | collective-permute-start | bytes 49160 | tf_op jit(solution)/shard_map/ppermute | solution.py:21
  95.8 5.8 %collective-permute-start.13 = (f32[8,512]{1,0:T(8,128)S(1)}, f32[8,512]{1,0:T(8,128)S(1)}, u32[]{:S(2)}, u32[]{:S(2)}) collective-permute-start(f32[8,512]{1,0:T(8,128)S(1)} %copy-done.9), channel_id=1, source_target_pairs={{0,3},{1,2},{2,1},{3,0},{4,7},{5,6},{6,5},{7,4},{8,11},{9,10},{10,... | collective-permute-start | bytes 49160 | tf_op jit(solution)/shard_map/ppermute | solution.py:21
  95.8 0.8 copy-start.13
  96.6 0.8 copy-start.14
  102.3 6.2 %copy-start.22 = (f32[8,512]{1,0:T(8,128)S(1)}, f32[8,512]{1,0:T(8,128)}, u32[]{:S(2)}) copy-start(f32[8,512]{1,0:T(8,128)} %select_convert_fusion.ids_ref.refs_3_.refs_5_) | copy-start | bytes 49156
  102.3 12.9 %copy-start.4 = (s32[3]{0:T(128)S(1)}, s32[3]{0:T(128)}, u32[]{:S(2)}) copy-start(s32[3]{0:T(128)} %pad_add_fusion.scal) | copy-start | bytes 40
  107.8 7.4 %collective-permute-start.22 = (f32[128,1920]{1,0:T(8,128)}, f32[128,1920]{1,0:T(8,128)S(1)}, u32[]{:S(2)}, u32[]{:S(2)}) collective-permute-start(f32[128,1920]{1,0:T(8,128)} %get-tuple-element.62.refs_0_.refs_2_), channel_id=1, source_target_pairs={{0,1},{1,0},{2,3},{3,2},{4,5},{5,4},{6,7},{7,6},{8,9},{9,8},{10,11... | collective-permute-start | bytes 2949128 | tf_op jit(solution)/shard_map/ppermute | solution.py:21
  108.4 5.5 %collective-permute-start.25 = (f32[8,512]{1,0:T(8,128)S(1)}, f32[8,512]{1,0:T(8,128)S(1)}, u32[]{:S(2)}, u32[]{:S(2)}) collective-permute-start(f32[8,512]{1,0:T(8,128)S(1)} %copy-done.22), channel_id=1, source_target_pairs={{0,8},{4,12},{8,16},{12,20},{16,24},{20,28},{24,0},{28,4},{1,9},{5... | collective-permute-start | bytes 49160 | tf_op jit(solution)/shard_map/ppermute | solution.py:472
  108.5 5.5 %collective-permute-start.26 = (f32[8,512]{1,0:T(8,128)S(1)}, f32[8,512]{1,0:T(8,128)S(1)}, u32[]{:S(2)}, u32[]{:S(2)}) collective-permute-start(f32[8,512]{1,0:T(8,128)S(1)} %copy-done.22), channel_id=1, source_target_pairs={{0,16},{4,20},{8,24},{12,28},{16,0},{20,4},{24,8},{28,12},{1,17},{... | collective-permute-start | bytes 49160 | tf_op jit(solution)/shard_map/ppermute | solution.py:472
  108.7 5.9 %collective-permute-start.27 = (f32[8,512]{1,0:T(8,128)S(1)}, f32[8,512]{1,0:T(8,128)S(1)}, u32[]{:S(2)}, u32[]{:S(2)}) collective-permute-start(f32[8,512]{1,0:T(8,128)S(1)} %copy-done.22), channel_id=1, source_target_pairs={{0,24},{4,28},{8,0},{12,4},{16,8},{20,12},{24,16},{28,20},{1,25},{... | collective-permute-start | bytes 49160 | tf_op jit(solution)/shard_map/ppermute | solution.py:472
  115.2 1.2 copy-start.6
  117.1 1.6 copy-start.7
  117.1 27.3 %collective-permute-start.23 = (bf16[128,1920]{1,0:T(8,128)(2,1)S(1)}, bf16[128,1920]{1,0:T(8,128)(2,1)S(1)}, u32[]{:S(2)}, u32[]{:S(2)}) collective-permute-start(bf16[128,1920]{1,0:T(8,128)(2,1)S(1)} %add.44.refs_14_.refs_0_), channel_id=1, source_target_pairs={{0,2},{1,3},{2,0},{3,1},{4,6},{5,7},{6,4},{7,5},{8,10},{9,11},{10,... | collective-permute-start | bytes 1474568 | tf_op jit(solution)/shard_map/ppermute | solution.py:21
  142.4 7.6 %collective-permute-start.28 = (f32[8,1536]{1,0:T(8,128)}, f32[8,1536]{1,0:T(8,128)S(1)}, u32[]{:S(2)}, u32[]{:S(2)}) collective-permute-start(f32[8,1536]{1,0:T(8,128)} %get-tuple-element.63.refs_7_.refs_11_), channel_id=1, source_target_pairs={{0,1},{1,0},{2,3},{3,2},{4,5},{5,4},{6,7},{7,6},{8,9},{9,8},{10,11... | collective-permute-start | bytes 147464 | tf_op jit(solution)/shard_map/ppermute | solution.py:21
  142.5 7.5 %collective-permute-start.29 = (f32[8,1536]{1,0:T(8,128)}, f32[8,1536]{1,0:T(8,128)S(1)}, u32[]{:S(2)}, u32[]{:S(2)}) collective-permute-start(f32[8,1536]{1,0:T(8,128)} %get-tuple-element.63.refs_7_.refs_11_), channel_id=1, source_target_pairs={{0,2},{1,3},{2,0},{3,1},{4,6},{5,7},{6,4},{7,5},{8,10},{9,11},{10,... | collective-permute-start | bytes 147464 | tf_op jit(solution)/shard_map/ppermute | solution.py:21
  143.3 6.7 %collective-permute-start.30 = (f32[8,1536]{1,0:T(8,128)}, f32[8,1536]{1,0:T(8,128)S(1)}, u32[]{:S(2)}, u32[]{:S(2)}) collective-permute-start(f32[8,1536]{1,0:T(8,128)} %get-tuple-element.63.refs_7_.refs_11_), channel_id=1, source_target_pairs={{0,3},{1,2},{2,1},{3,0},{4,7},{5,6},{6,5},{7,4},{8,11},{9,10},{10,... | collective-permute-start | bytes 147464 | tf_op jit(solution)/shard_map/ppermute | solution.py:21
  144.4 0.8 copy-start.24
  150.0 0.6 copy-start.25
  150.0 0.6 copy-start.26
  150.0 0.6 copy-start.27
  161.0 23.7 %collective-permute-start.31 = (bf16[256,1024]{1,0:T(8,128)(2,1)}, bf16[256,1024]{1,0:T(8,128)(2,1)S(1)}, u32[]{:S(2)}, u32[]{:S(2)}) collective-permute-start(bf16[256,1024]{1,0:T(8,128)(2,1)} %get-tuple-element.71), channel_id=1, source_target_pairs={{0,4},{4,0},{8,12},{12,8},{16,20},{20,16},{24,28},{28,24},{1,5},{5... | collective-permute-start | bytes 1572872 | tf_op jit(solution)/shard_map/ppermute | solution.py:732
  162.6 15.4 %copy-start.2 = (bf16[512,512]{1,0:T(8,128)(2,1)S(1)}, bf16[512,512]{1,0:T(8,128)(2,1)}, u32[]{:S(2)}) copy-start(bf16[512,512]{1,0:T(8,128)(2,1)} %copy-done.1) | copy-start | bytes 1572868
  162.6 16.1 %copy-start.18 = (bf16[4,128,512]{2,1,0:T(8,128)(2,1)S(1)}, bf16[4,128,512]{2,1,0:T(8,128)(2,1)}, u32[]{:S(2)}) copy-start(bf16[4,128,512]{2,1,0:T(8,128)(2,1)} %get-tuple-element.64.refs_15_) | copy-start | bytes 1572868
  175.8 8.2 %copy-start.20 = (bf16[256,128]{1,0:T(8,128)(2,1)S(1)}, bf16[256,128]{1,0:T(8,128)(2,1)}, u32[]{:S(2)}) copy-start(bf16[256,128]{1,0:T(8,128)(2,1)} %get-tuple-element.74) | copy-start | bytes 196612
  175.8 8.9 %copy-start.15 = (bf16[256,1024]{1,0:T(8,128)(2,1)S(1)}, bf16[256,1024]{1,0:T(8,128)(2,1)}, u32[]{:S(2)}) copy-start(bf16[256,1024]{1,0:T(8,128)(2,1)} %get-tuple-element.70) | copy-start | bytes 1572868
  175.8 20.2 %copy-start.16 = (bf16[256,1024]{1,0:T(8,128)(2,1)S(1)}, bf16[256,1024]{1,0:T(8,128)(2,1)}, u32[]{:S(2)}) copy-start(bf16[256,1024]{1,0:T(8,128)(2,1)} %get-tuple-element.72) | copy-start | bytes 1572868
  175.8 8.2 %collective-permute-start.33 = (bf16[256,128]{1,0:T(8,128)(2,1)}, bf16[256,128]{1,0:T(8,128)(2,1)S(1)}, u32[]{:S(2)}, u32[]{:S(2)}) collective-permute-start(bf16[256,128]{1,0:T(8,128)(2,1)} %get-tuple-element.69.refs_5_), channel_id=1, source_target_pairs={{0,4},{4,0},{8,12},{12,8},{16,20},{20,16},{24,28},{28,24},{1,5},{5... | collective-permute-start | bytes 196616 | tf_op jit(solution)/shard_map/ppermute | solution.py:732
  176.5 19.6 %collective-permute-start.32 = (bf16[256,1024]{1,0:T(8,128)(2,1)}, bf16[256,1024]{1,0:T(8,128)(2,1)S(1)}, u32[]{:S(2)}, u32[]{:S(2)}) collective-permute-start(bf16[256,1024]{1,0:T(8,128)(2,1)} %get-tuple-element.73), channel_id=1, source_target_pairs={{0,4},{4,0},{8,12},{12,8},{16,20},{20,16},{24,28},{28,24},{1,5},{5... | collective-permute-start | bytes 1572872 | tf_op jit(solution)/shard_map/ppermute | solution.py:732
  177.9 19.3 %collective-permute-start.24 = (bf16[512,512]{1,0:T(8,128)(2,1)S(1)}, bf16[512,512]{1,0:T(8,128)(2,1)}, u32[]{:S(2)}, u32[]{:S(2)}) collective-permute-start(bf16[512,512]{1,0:T(8,128)(2,1)S(1)} %copy-done.2), channel_id=1, source_target_pairs={{0,2},{1,3},{2,0},{3,1},{4,6},{5,7},{6,4},{7,5},{8,10},{9,11},{10,... | collective-permute-start | bytes 1572872 | tf_op jit(solution)/shard_map/ppermute | solution.py:21
  179.5 18.4 %all-to-all-start.1 = ((bf16[8,64,512]{2,1,0:T(8,128)(2,1)}), bf16[8,64,512]{2,1,0:T(8,128)(2,1)S(1)}, u32[]{:S(2)}, u32[]{:S(2)}) async-start(bf16[8,64,512]{2,1,0:T(8,128)(2,1)} %bitcast.10), calls=%async_computation.1 | async-start | bytes 1048576 | tf_op jit(solution)/shard_map/all_to_all | solution.py:630
  197.9 0.8 copy-start.19
  (6 other events, 3.6 us)

commit v2 on v1

--- a/solution.py
+++ b/solution.py
@@ -49,7 +49,6 @@
     "line_logits": 20,
     "head_back": 9,
     "head_weights": 8,
-    "turned_rows": 2,
     "tail_logits": 5,
     "tail_grads": 3,
     "tail_back": 3,
@@ -73,7 +72,7 @@
             out_specs=out_specs,
             scratch_shapes=list(scratch),
         ),
-        compiler_params=pltpu.CompilerParams(vmem_limit_bytes=(16 if name in SMALL else 60) << 20),
+        compiler_params=pltpu.CompilerParams(vmem_limit_bytes=(16 if name in SMALL else 63) << 20),
         cost_estimate=pl.CostEstimate(
             flops=int(MICROSECONDS[name] * COST_SCALE * 1e9), bytes_accessed=1, transcendentals=0
         ),
@@ -175,9 +174,11 @@
 
 
 def logits_kernel(cfg, scal, *refs):
-    n, clus_cols = cfg
-    pieces, (w_ref, wc_ref, e_ref, ec_ref, st_ref, ex_ref) = refs[:n], refs[n : n + 6]
-    peak_ref, sum_ref = refs[n + 6 :]
+    n, clus_cols, earlier = cfg
+    pieces, refs = refs[:n], refs[n:]
+    if earlier:
+        earlier_ref, *refs = refs
+    w_ref, wc_ref, e_ref, ec_ref, st_ref, turn_ref, ex_ref, peak_ref, sum_ref = refs
     j = pl.program_id(0)
     blocks = pl.num_programs(0)
     parts = []
@@ -213,25 +214,43 @@
         sum_ref[out, :] = total
         st_ref[out, :] = jnp.where(lanes_of((size, LANES)) == j, peak, st_ref[out, :])
 
+    @pl.when(j == 1)
+    def _():
+        count = turn_ref.shape[0] * turn_ref.shape[1]
+        first = pl.multiple_of(scal[1] * count, count)
+        for piece, i, at, size in parts:
+            turned_into(turn_ref, piece[i : i + size, pl.ds(first, count)], scal[2], at)
+
     @pl.when(j == blocks - 1)
     def _():
         lane = lanes_of(st_ref.shape)
         both = jnp.where(lane == 0, peak_ref[...], jnp.where(lane == 1, sum_ref[...], 0.0))
-        ex_ref[...] = both.T[:8]
-
-
-def head_columns(cfg, shares, ids, permuted):
-    splits, quarter = cfg
+        if earlier:
+            ex_ref[:, :earlier] = earlier_ref[...]
+        ex_ref[:, earlier:] = both.T[:8]
+
+
+WORD_LANE, CLUS_LANE = LANES - 2, LANES - 1
+
+
+def head_columns(cfg, scal, shares, ids, stats, permuted):
+    splits, quarter, word_cols, clus_cols = cfg
     top, total = merged_stats(shares, splits, quarter if permuted else 0)
-    return columns_of([top, 1.0 / total, ids[0:1], ids[1:2]])
-
-
-def head_block(expd, stats, lane, cols, target, first, limit):
-    peak = jnp.sum(jnp.where(lanes_of(stats.shape) == lane, stats, 0.0), axis=1, keepdims=True)
-    probs = expd.astype(F32) * (jnp.exp(peak - cols[:, 0:1]) * cols[:, 1:2])
-    local = cols[:, target : target + 1].astype(I32) - first
-    local = jnp.where(local < limit, local, -1)
-    return jnp.where(lanes_of(probs.shape) == local, probs - 1.0, probs).astype(BF16)
+    tp_index = scal[0]
+    word = ids[0:1] - (tp_index * word_cols).astype(F32)
+    clus = ids[1:2] - (tp_index * clus_cols).astype(F32)
+    clus = jnp.where(clus < clus_cols, clus, -1.0)
+    cols = columns_of([top, 1.0 / total, word, clus])
+    scales = jnp.exp(stats - cols[:, 0:1]) * cols[:, 1:2]
+    lane = lanes_of(scales.shape)
+    return jnp.where(lane == WORD_LANE, cols[:, 2:3], jnp.where(lane == CLUS_LANE, cols[:, 3:4], scales))
+
+
+def head_block(expd, cols, lane, target, first):
+    scale = jnp.sum(jnp.where(lanes_of(cols.shape) == lane, cols, 0.0), axis=1, keepdims=True)
+    local = cols[:, target : target + 1] - first
+    probs = expd.astype(F32) * scale
+    return jnp.where(lanes_of(probs.shape).astype(F32) == local, probs - 1.0, probs).astype(BF16)
 
 
 def back_kernel(cfg, scal, e_ref, ec_ref, st_ref, ids_ref, *refs):
@@ -244,16 +263,17 @@
 
     @pl.when(i == 0)
     def _():
-        col_ref[...] = head_columns((splits, 0), [share[...] for share in shares], ids_ref[...], False)
+        cfg = (splits, 0, word_cols, clus_cols)
+        col_ref[...] = head_columns(
+            cfg, scal, [share[...] for share in shares], ids_ref[...], st_ref[...], False
+        )
         for at in range(0, tok, LANES):
             rows = slice(at, at + LANES)
-            cols, stats = col_ref[rows, :], st_ref[rows, :]
+            cols = col_ref[rows, :]
             for j in range(blocks):
                 part = slice(j * block, (j + 1) * block)
-                first = scal[0] * word_cols + j * block
-                g_ref[rows, part] = head_block(e_ref[rows, part], stats, j, cols, 2, first, block)
-            first = scal[0] * clus_cols
-            gc_ref[rows, :] = head_block(ec_ref[rows, :], stats, blocks, cols, 3, first, clus_cols)
+                g_ref[rows, part] = head_block(e_ref[rows, part], cols, j, WORD_LANE, float(j * block))
+            gc_ref[rows, :] = head_block(ec_ref[rows, :], cols, blocks, CLUS_LANE, 0.0)
 
     out = dot_nt(g_ref[...], w_ref[...]) + dot_nt(gc_ref[...], wc_ref[...])
 
@@ -266,67 +286,72 @@
         keep_ref[0] = out.astype(BF16)
 
 
-def turn_kernel(cfg, scal, *refs):
-    near, n = cfg
-    pieces, (out_ref,) = refs[:n], refs[n:]
-    out_rows = out_ref.shape[0] // near
-    at = 0
-    for piece in pieces:
-        size = piece.shape[0]
-        turned = piece[...].T
-        for i in range(near):
-            to = pl.multiple_of((scal[2] ^ i) * out_rows, out_rows)
-            out_ref[pl.ds(to, out_rows), at : at + size] = turned[i * out_rows : (i + 1) * out_rows]
-        at += size
-
-
-def weights_kernel(cfg, scal, t_ref, e0, e1, st0, st1, *refs):
-    splits, quarter, clus_cols, word_cols, line, offset, last = cfg
-    tok = e0.shape[0]
-    block = e0.shape[1]
+def turned_into(out_ref, value, near_index, at):
+    turned = value.T
+    near, out_rows, _ = out_ref.shape
+    for i in range(near):
+        out_ref[near_index ^ i, :, at : at + value.shape[0]] = turned[i * out_rows : (i + 1) * out_rows]
+
+
+def weights_kernel(cfg, scal, *refs):
+    splits, quarter, clus_cols, word_cols, sizes, offset, last = cfg
+    n = len(sizes)
+    turned, expds, refs = refs[:n], refs[n : 2 * n], refs[2 * n :]
+    block = expds[0].shape[1]
+    starts = [sum(sizes[:k]) for k in range(n)]
     i = pl.program_id(0)
     if last:
-        col_ref, ec0, ec1, own_ref, near_ref, ownc_ref, nearc_ref, g_ref = refs
+        col_ref, *clus, own_ref, near_ref, g_ref = refs
     else:
-        ids0, ids1, *refs = refs
-        shares0, shares1, refs = refs[:splits], refs[splits : 2 * splits], refs[2 * splits :]
+        stats, ids, refs = refs[:n], refs[n : 2 * n], refs[2 * n :]
+        shares, refs = [refs[k * splits : (k + 1) * splits] for k in range(n)], refs[n * splits :]
         own_ref, near_ref, col_ref, g_ref = refs
     out_rows = own_ref.shape[0]
 
-    def fill(first_ref, others_ref, lane, target, first, limit):
-        for at in range(0, line * tok, LANES):
-            source, stats, here = (first_ref, st0, at) if at < tok else (others_ref, st1, at - tok)
-            rows = slice(here, here + LANES)
-            g_ref[at : at + LANES, : source.shape[1]] = head_block(
-                source[rows, :], stats[rows, :], lane, col_ref[at : at + LANES, :], target, first, limit
-            )
+    def fill(sources, lane, target, first):
+        for source, start, size in zip(sources, starts, sizes):
+            for here in range(0, size, LANES):
+                to = slice(start + here, start + here + LANES)
+                g_ref[to, : source.shape[1]] = head_block(
+                    source[here : here + LANES, :], col_ref[to, :], lane, target, first
+                )
+
+    def product(cols):
+        total = None
+        for ref, start, size in zip(turned, starts, sizes):
+            rows = ref[...].reshape(ref.shape[0] * ref.shape[1], size)
+            part = dot_nn(rows, g_ref[start : start + size, :cols])
+            total = part if total is None else total + part
+        return total.astype(BF16)
 
     if not last:
 
         @pl.when(i == 0)
         def _():
-            col_ref[:tok, :] = head_columns(
-                (splits, quarter), [share[...] for share in shares0], ids0[...], False
-            )
-            for k in range(line - 1):
-                part = slice(k * tok, (k + 1) * tok)
-                col_ref[(k + 1) * tok : (k + 2) * tok, :] = head_columns(
-                    (splits, quarter), [share[:, part] for share in shares1], ids1[:, part], True
-                )
+            cfg = (splits, quarter, word_cols, clus_cols)
+            tok = sizes[0]
+            for k in range(n):
+                for here in range(0, sizes[k], tok):
+                    part = slice(here, here + tok)
+                    to = starts[k] + here
+                    col_ref[to : to + tok, :] = head_columns(
+                        cfg, scal, [share[:, part] for share in shares[k]], ids[k][:, part], stats[k][part, :], k > 0
+                    )
 
     j = i + offset
-    fill(e0, e1, j, 2, scal[0] * word_cols + j * block, block)
-    both = dot_nn(t_ref[...], g_ref[...]).astype(BF16)
-    own_ref[...] = both[:out_rows]
-    near_ref[...] = both[out_rows:]
+    fill(expds, j, WORD_LANE, (j * block).astype(F32))
+    both = product(block)
+    here = pl.ds(pl.multiple_of(i * block, block), block)
+    own_ref[:, here] = both[:out_rows]
+    near_ref[:, here] = both[out_rows:]
     if last:
 
         @pl.when(i == pl.num_programs(0) - 1)
         def _():
-            fill(ec0, ec1, word_cols // block, 3, scal[0] * clus_cols, clus_cols)
-            both = dot_nn(t_ref[...], g_ref[:, :LANES]).astype(BF16)
-            ownc_ref[...] = both[:out_rows]
-            nearc_ref[...] = both[out_rows:]
+            fill(clus, word_cols // block, CLUS_LANE, 0.0)
+            both = product(LANES)
+            own_ref[:, -LANES:] = both[:out_rows]
+            near_ref[:, -LANES:] = both[out_rows:]
 
 
 def tail_logits_kernel(cfg, scal, *refs):
@@ -507,26 +532,31 @@
     lane_block = pl.BlockSpec((tok_rows, LANES), lambda i, s: (0, 0))
     stat_block = pl.BlockSpec((8, tok_rows), lambda i, s: (0, 0))
 
-    def head_logits(pieces):
+    def head_logits(pieces, earlier):
         tok = sum(p.shape[0] for p in pieces)
+        turned = struct((near, out_rows, tok), BF16)
+        before = sum(e.shape[1] for e in earlier)
+        stats = struct((8, before + tok), F32)
         return order.call(
             logits_kernel,
-            (len(pieces), clus_cols),
+            (len(pieces), clus_cols, before),
             "head_logits" if len(pieces) == 1 else "line_logits",
-            (*pieces, head_words, clus_padded),
-            [whole(p) for p in pieces]
+            (*pieces, *earlier, head_words, clus_padded),
+            [whole(p) for p in (*pieces, *earlier)]
             + [pl.BlockSpec((width, block), lambda i, s: (0, i)), whole(clus_padded)],
             [
                 struct((tok, word_cols), BF16),
                 struct((tok, LANES), BF16),
                 struct((tok, LANES), F32),
-                struct((8, tok), F32),
+                turned,
+                stats,
             ],
             [
                 pl.BlockSpec((tok, block), lambda i, s: (0, i)),
                 pl.BlockSpec((tok, LANES), lambda i, s: (0, 0)),
                 pl.BlockSpec((tok, LANES), lambda i, s: (0, 0)),
-                pl.BlockSpec((8, tok), lambda i, s: (0, 0)),
+                whole(turned),
+                whole(stats),
             ],
             [pltpu.VMEM((tok, 1), F32)] * 2,
             (blocks,),
@@ -535,9 +565,9 @@
     def shared(stats):
         return [tp_swap(stats, step) for step in range(1, splits)]
 
-    def added(first, second, step, specs=None):
+    def added(first, second, specs=None):
         out = struct(first.shape[-2:], BF16)
-        total = order.call(
+        return order.call(
             add_kernel,
             None,
             "add",
@@ -546,7 +576,6 @@
             out,
             whole(out),
         )
-        return total, tp_swap(total, step)
 
     projections = (proj_one, proj_two, proj_three, proj_four)
     outputs = (out_one, out_two, out_three, out_four)
@@ -558,10 +587,10 @@
     out_specs = [whole(o) for o in outputs]
     band_sums = struct((slots, reduced_width), F32)
 
-    def tail_send():
+    def tail_rows():
         sent = struct((tok_rows, own_width + LANES), BF16)
         place = struct((tok_rows, tok_rows), BF16)
-        dispatch, send = order.call(
+        return order.call(
             send_kernel,
             (groups, capacity),
             "send_rows",
@@ -570,6 +599,7 @@
             [place, sent],
             [whole(place), whole(sent)],
         )
+    def tail_send(send):
         recv = lax.all_to_all(
             send.reshape(groups, 4 * capacity, own_width + LANES),
             "vocab",
@@ -579,7 +609,7 @@
         )
         rows = recv.reshape(groups, 4, capacity, own_width + LANES).transpose(1, 0, 2, 3)
         rows = rows.reshape(4, slots, own_width + LANES)
-        return dispatch, rows[:, :, :own_width], rows[:, :, own_width:]
+        return rows[:, :, :own_width], rows
 
     def tail_logits():
         outs = [
@@ -608,7 +638,12 @@
             splits,
             "tail_grads",
             (reduced, tail_expd, digits, tail_stats, *tail_shares, *outputs),
-            [whole(reduced), whole(tail_expd), whole(digits)] + [whole(tail_stats)] * splits + out_specs,
+            [
+                whole(reduced),
+                whole(tail_expd),
+                pl.BlockSpec((4, slots, LANES), lambda i, s: (0, 0, own_width // LANES)),
+            ]
+            + [whole(tail_stats)] * splits + out_specs,
             [struct(o.shape, BF16) for o in outputs] + [band_sums],
             out_specs + [whole(band_sums)],
         )
@@ -626,6 +661,9 @@
             outs,
             [whole(o) for o in outs],
         )
+        return grads_proj, back
+
+    def tail_return(back):
         back = back.reshape(4, groups, capacity, own_width).transpose(1, 0, 2, 3)
         returned = lax.all_to_all(
             back.reshape(groups, 4 * capacity, own_width),
@@ -634,10 +672,11 @@
             concat_axis=0,
             tiled=True,
         )
-        return grads_proj, returned.reshape(tok_rows, own_width)
+        return returned.reshape(tok_rows, own_width)
 
     def head_back():
         count = splits // 2
+        *own_expd, _ = head_groups[0]
 
         def part_of(i):
             return jnp.where(i < count, 2 * i + 1, 2 * (i - count))
@@ -647,7 +686,7 @@
             back_kernel,
             (splits, block, clus_cols),
             "head_back",
-            (*own_expd, ids, own_stats, *early, head_words, clus_padded),
+            (*own_expd, ids, *early, head_words, clus_padded),
             [whole(v) for v in own_expd]
             + [stat_block] * (1 + splits)
             + [
@@ -681,84 +720,97 @@
             whole(out),
         )
 
-    def turned_rows():
-        pieces = [piece for step in range(line) for piece in chunks[step]]
-        out = struct((near * out_rows, line * tok_rows), BF16)
-        return order.call(
-            turn_kernel,
-            (near, len(pieces)),
-            "turned_rows",
-            pieces,
-            [pl.BlockSpec((p.shape[0], near * out_rows), lambda i, s: (0, s[1])) for p in pieces],
-            out,
-            whole(out),
-        )
-
-    def weight_grads(half, count, columns):
-        steps = blocks // count
+    def weight_grads(first, steps, columns):
         rest = (near - 1) * out_rows
-        outs = [struct((out_rows, steps * block), BF16), struct((rest, steps * block), BF16)]
-        specs = [pl.BlockSpec((o.shape[0], block), lambda i, s: (0, i)) for o in outs]
-        operands = [turned, own_expd[0], line_expd[0], own_expd[2], line_expd[2]]
-        in_specs = [
-            whole(turned),
-            pl.BlockSpec((tok_rows, block), lambda i, s: (0, i + half * steps)),
-            pl.BlockSpec(((line - 1) * tok_rows, block), lambda i, s: (0, i + half * steps)),
-            whole(own_expd[2]),
-            whole(line_expd[2]),
-        ]
+        sizes = tuple(group[0].shape[0] for group in head_groups)
+        cols = steps * block + (LANES if columns is not None else 0)
+        outs = [struct((out_rows, cols), BF16), struct((rest, cols), BF16)]
+        expds, clus, stats, turned = zip(*head_groups)
+        operands = [*turned, *expds]
+        in_specs = [whole(t) for t in turned]
+        in_specs += [pl.BlockSpec((size, block), lambda i, s: (0, i + first)) for size in sizes]
         if columns is None:
-            extra = [ids, line_ids(), own_stats, *early, *late]
-            more = [struct((line * tok_rows, LANES), F32)]
+            others = line_ids()
+            extra = [*stats, ids]
+            in_specs += [whole(v) for v in extra]
+            lanes = []
+            at = 0
+            for size in sizes[1:]:
+                lanes.append(pl.BlockSpec((8, size), lambda i, s, place=at // size: (0, place)))
+                at += size
+            in_specs += lanes + [stat_block] * splits
+            in_specs += [spec for spec in lanes for _ in range(splits)]
+            extra += [others] * len(lanes) + early + late * len(lanes)
+            outs.append(struct((line * tok_rows, LANES), F32))
         else:
-            extra = [columns, own_expd[1], line_expd[1]]
-            more = [struct((out_rows, LANES), BF16), struct((rest, LANES), BF16)]
+            extra = [columns, *clus]
+            in_specs += [whole(v) for v in extra]
         return order.call(
             weights_kernel,
-            (splits, quarter, clus_cols, word_cols, line, half * steps, columns is not None),
+            (splits, quarter, clus_cols, word_cols, sizes, first, columns is not None),
             "head_weights",
             operands + extra,
-            in_specs + [whole(v) for v in extra],
-            outs + more,
-            specs + [whole(o) for o in more],
+            in_specs,
+            outs,
+            [whole(o) for o in outs],
             [pltpu.VMEM((line * tok_rows, block), BF16)],
             (steps,),
         )
 
-    def near_sum(own, rest):
-        total = own.astype(F32)
+    def near_parts(own, rest):
+        parts = [own]
         for step in range(1, near):
             part = rest[(step - 1) * out_rows : step * out_rows]
-            total = total + lax.ppermute(part, "vocab", xor_pairs(groups, step)).astype(F32)
-        return total.astype(BF16)
-
-    dispatch, rows, digits = tail_send()
+            parts.append(lax.ppermute(part, "vocab", xor_pairs(groups, step)))
+        return parts
+
+    def near_sum(parts):
+        return sum(part.astype(F32) for part in parts).astype(BF16)
+
+    head_groups = []
+
+    def head_group(*steps, earlier=()):
+        *group, mine = head_logits([p for step in steps for p in chunks[step]], earlier)
+        head_groups.append(group)
+        return mine
+
+    dispatch, send = tail_rows()
     move_rows(1)
-    *own_expd, own_stats = head_logits(chunks[0])
-    early = shared(own_stats)
+    early = head_group(0)
+    early = [early] + shared(early)
     move_rows(2)
+    rows, digits = tail_send(*order.hold(send))
+    back_keep, back_beside = head_back()
+    moved_ids = order.hold(*moved_ids)
+    move_rows(3)
+    late = head_group(1, 2)
+    (rows,) = order.hold(rows)
     across_rows, beside_rows = tp_swap(rows, 2), tp_swap(rows, 1)
-    back_keep, back_beside = head_back()
+    move_rows(4)
+    second = pl.BlockSpec((1, tok_rows, own_width), lambda i, s: (1, 0, 0))
+    back_far = added(back_keep, back_beside, [second, second])
+    late = head_group(3, earlier=(late,))
+    late = [late] + shared(late)
     (across_rows,) = order.hold(across_rows)
+    back_far = tp_swap(back_far, 2)
     all_rows = [rows, beside_rows, across_rows, tp_swap(across_rows, 1)]
-    move_rows(3)
     reduced, tail_expd, tail_stats = tail_logits()
     tail_shares = shared(tail_stats)
-    second = pl.BlockSpec((1, tok_rows, own_width), lambda i, s: (1, 0, 0))
-    _, back_far = added(back_keep, back_beside, 2, [second, second])
-    move_rows(4)
-    turned = turned_rows()
+    (back_far,) = order.hold(back_far)
     grads_out, part, beside = tail_grads()
-    part, far = added(part, beside, 2)
-    *line_expd, line_stats = head_logits([p for step in range(1, line) for p in chunks[step]])
-    late = [line_stats] + shared(line_stats)
-    grads_proj, returned = tail_back()
-    own, rest, columns = weight_grads(0, 2, None)
-    sums = [near_sum(own, rest)]
-    own, rest, own_clus, rest_clus = weight_grads(1, 2, columns)
-    sums.append(near_sum(own, rest))
-    clus_sum = near_sum(own_clus, rest_clus)[:, :clus_cols]
+    part = added(part, beside)
+    far = tp_swap(part, 2)
+    ahead = blocks - 1
+    *first_parts, columns = weight_grads(0, ahead, None)
+    first_sum = near_parts(*first_parts)
+    grads_proj, back = tail_back()
+    returned = tail_return(back)
+    second_sum = near_parts(*weight_grads(ahead, blocks - ahead, columns))
     grad_hidden = grad_hidden_step()
+    second_sum = near_sum(order.hold(*second_sum))
+    at = (blocks - ahead) * block
+    sums = [near_sum(first_sum), second_sum[:, :at]]
+    clus_sum = second_sum[:, at : at + clus_cols]
     return (
         grad_hidden,
         jnp.concatenate(sums, axis=1),

time: 203 us -> 180 us (0.89)
  waiting for transfers between devices: 40.7 us -> 16 us
    ppermute x25, waiting for transfers between devices: 14 us -> 4.37 us  [tp_swap(): return lax.ppermute(value, 'tp', xor_pairs(lax.axis_size('tp'), step))]
    ppermute x2, waiting for transfers between devices: 9.4 us -> 0.01 us  [move_rows(): from_line[stage + 1] = lax.ppermute(held, 'vocab', ring)]
    ppermute x3 -> x2, waiting for transfers between devices: 11.1 us -> 4.67 us  [near_parts(): parts.append(lax.ppermute(part, 'vocab', xor_pairs(groups, step)))]
    ppermute x1, waiting for transfers between devices: 0.92 us -> 5.87 us  [body(): from_line = {1: lax.ppermute(piece, 'vocab', ring)}]
    all_to_all x1, waiting for transfers between devices: 2.45 us -> 0.01 us  [tail_send(): lax.all_to_all(send.reshape(groups, 4 * capacity, own_width + LANES), 'vo...]
    convert_element_type x3 -> x2, other arithmetic: 0.4 us -> 2.71 us  [near_sum(): return sum((part.astype(F32) for part in parts)).astype(BF16)]
    ppermute x3, waiting for transfers between devices: 2.28 us -> 0.01 us  [body(): lax.ppermute(ids, 'vocab', [(i, (i + step * near) % groups) for i in rang...]
    unnamed x70 -> x66, local copies, waits for them, and re-layouts: 11.9 us -> 9.69 us
  transfers between devices with their start and end apart: 36 -> 35, of which waited for: 10 -> 8; matrix products, arithmetic and copies ran while one was open for 4% -> 6% of each run, Pallas kernels for 41% -> 54%
where the time goes in v2:
time: 180 us; the launch traced here: 178 us
  Pallas kernels  102 us (57%)
  starting transfers between devices  36.6 us (20%)
  local copies, waits for them, and re-layouts  16.4 us (9%)
  waiting for transfers between devices  16 us (9%)
  other arithmetic  6.45 us (4%)
    pallas_call x13, Pallas kernels, kernel_call(): pl.pallas_call(kernel, name=name, out_shape=outs, grid_spec=pltpu.Prefetc...  102 us
    ppermute x25, starting transfers between devices, tp_swap(): return lax.ppermute(value, 'tp', xor_pairs(lax.axis_size('tp'), step))  14.6 us
    unnamed x66, local copies, waits for them, and re-layouts  9.69 us
    ppermute x1, waiting for transfers between devices, body(): from_line = {1: lax.ppermute(piece, 'vocab', ring)}  5.87 us
    ppermute x2, waiting for transfers between devices, near_parts(): parts.append(lax.ppermute(part, 'vocab', xor_pairs(groups, step)))  4.67 us
    all_to_all x1, starting transfers between devices, tail_return(): lax.all_to_all(back.reshape(groups, 4 * capacity, own_width), 'vocab', sp...  4.54 us
    all_to_all x1, starting transfers between devices, tail_send(): lax.all_to_all(send.reshape(groups, 4 * capacity, own_width + LANES), 'vo...  4.38 us
    ppermute x25, waiting for transfers between devices, tp_swap(): return lax.ppermute(value, 'tp', xor_pairs(lax.axis_size('tp'), step))  4.37 us
  transfers between devices with their start and end apart: 35, of which 8 were waited for; matrix products, arithmetic and copies ran while one was open for 6% of the time, Pallas kernels for 54%

profile of v2, /device:TPU:0, one launch (start us, length us, event | category | flops | bytes accessed | tf_op | source)
XLA Modules:
  0.0 178.4 jit_solution(11664675736091586850)
XLA Ops:
  0.7 1.9 %constant_dynamic-slice_fusion = bf16[128,2048]{1,0:T(8,128)(2,1)} fusion(bf16[512,2048]{1,0:T(8,128)(2,1)} %refs_0_.1, s32[]{:T(128)S(6)} %select_n.70), kind=kLoop, calls=%fused_computation.13 | loop fusion | bytes 1048580 | tf_op jit(solution)/shard_map/dynamic_slice | solution.py:509
  2.5 3.0 %collective-permute-start = (bf16[128,2048]{1,0:T(8,128)(2,1)}, bf16[128,2048]{1,0:T(8,128)(2,1)S(1)}, u32[]{:S(2)}, u32[]{:S(2)}) collective-permute-start(bf16[128,2048]{1,0:T(8,128)(2,1)} %constant_dynamic-slice_fusion), channel_id=1, source_target_pairs={{0,8},{4,12},{8,16},{12,20},{16,24},{20,28},{24,0},{28,4},{1,9},{5... | collective-permute-start | bytes 1572872 | tf_op jit(solution)/shard_map/ppermute | solution.py:510
  5.6 0.7 compare_select_fusion.1
  6.3 0.6 pad_add_fusion.scal
  6.9 1.0 copy.42
  7.9 0.9 pad.4.refs_2_.refs_9_.refs_6_
  8.8 0.7 select_convert_fusion.ids_ref.refs_3_.refs_9_
  9.5 4.4 %send_rows.1 = (bf16[512,512]{1,0:T(8,128)(2,1)}, bf16[512,640]{1,0:T(8,128)(2,1)}) custom-call(s32[3]{0:T(128)} %pad_add_fusion.scal, f32[8,512]{1,0:T(8,128)} %select_convert_fusion.ids_ref.refs_3_.refs_9_, bf16[512,2048]{1,0:T(8,128)(2,1)} %refs_0_.1), custom_call_target="tpu_custom_call" | custom-call | flops 3000000000 | bytes 1 | tf_op jit(solution)/shard_map/send_rows/pallas_call | solution.py:64
  13.9 5.9 %collective-permute-done.refs_0_ = bf16[128,2048]{1,0:T(8,128)(2,1)S(1)} collective-permute-done((bf16[128,2048]{1,0:T(8,128)(2,1)}, bf16[128,2048]{1,0:T(8,128)(2,1)S(1)}, u32[]{:S(2)}, u32[]{:S(2)}) %collective-permute-start) | collective-permute-done | bytes 524320 | tf_op jit(solution)/shard_map/ppermute | solution.py:510
  19.7 0.8 copy-done.10
  20.5 1.5 collective-permute-start.2
  22.0 11.8 %head_logits.1 = (bf16[512,2048]{1,0:T(8,128)(2,1)}, bf16[512,128]{1,0:T(8,128)(2,1)}, f32[512,128]{1,0:T(8,128)}, bf16[2,256,512]{2,1,0:T(8,128)(2,1)}, f32[8,512]{1,0:T(8,128)}) custom-call(s32[3]{0:T(128)} %pad_add_fusion.scal, bf16[512,2048]{1,0:T(8,128)(2,1)} %refs_0_.1, bf16[2048,2048]{1,0:T(8,128)(2,1)} %refs_5_.3, ...), custom_call_target="tpu_custom_call" | custom-call | flops 8999999488 | bytes 1 | tf_op jit(solution)/shard_map/head_logits/pallas_call | solution.py:64
  33.9 0.6 collective-permute-start.12
  34.5 1.3 collective-permute-start.11
  35.8 3.8 %collective-permute-start.10 = (f32[8,512]{1,0:T(8,128)S(1)}, f32[8,512]{1,0:T(8,128)S(1)}, u32[]{:S(2)}, u32[]{:S(2)}) collective-permute-start(f32[8,512]{1,0:T(8,128)S(1)} %copy-done.20), channel_id=1, source_target_pairs={{0,24},{4,28},{8,0},{12,4},{16,8},{20,12},{24,16},{28,20},{1,25},{... | collective-permute-start | bytes 49160 | tf_op jit(solution)/shard_map/ppermute | solution.py:497
  39.6 0.8 copy-done.12
  40.4 0.6 collective-permute-start.7
  41.0 2.7 %collective-permute-start.6 = (bf16[128,2048]{1,0:T(8,128)(2,1)}, bf16[128,2048]{1,0:T(8,128)(2,1)}, u32[]{:S(2)}, u32[]{:S(2)}) collective-permute-start(bf16[128,2048]{1,0:T(8,128)(2,1)} %get-tuple-element.61.refs_4_), channel_id=1, source_target_pairs={{0,8},{4,12},{8,16},{12,20},{16,24},{20,28},{24,0},{28,4},{1,9},{5... | collective-permute-start | bytes 1572872 | tf_op jit(solution)/shard_map/ppermute | solution.py:524
  43.7 12.0 %head_back.1 = (bf16[2,512,512]{2,1,0:T(8,128)(2,1)}, bf16[2,512,512]{2,1,0:T(8,128)(2,1)}) custom-call(s32[3]{0:T(128)} %pad_add_fusion.scal, bf16[512,2048]{1,0:T(8,128)(2,1)} %get-tuple-element.62.refs_0_.refs_3_, bf16[512,128]{1,0:T(8,128)(2,1)} %get-tuple-element.63.refs_1_.refs_7_, f32[512,128]{1,0:T(8,128)} %get-tuple-element.64.refs_2_.refs_6_, ...), custom_call_target="tpu_custom_call" | custom-call | flops 8999999488 | bytes 1 | tf_op jit(solution)/shard_map/head_back/pallas_call | solution.py:64
  56.4 0.5 copy-done.17
  57.1 4.4 %all-to-all-start = ((bf16[8,64,640]{2,1,0:T(8,128)(2,1)}), bf16[8,64,640]{2,1,0:T(8,128)(2,1)}, u32[]{:S(2)}, u32[]{:S(2)}) async-start(bf16[8,64,640]{2,1,0:T(8,128)(2,1)} %bitcast.4), calls=%async_computation | async-start | bytes 1310720 | tf_op jit(solution)/shard_map/all_to_all | solution.py:603
  61.9 0.8 copy-done.22
  62.7 1.5 collective-permute-start.18
  64.3 18.3 %line_logits.2 = (bf16[1024,2048]{1,0:T(8,128)(2,1)}, bf16[1024,128]{1,0:T(8,128)(2,1)}, f32[1024,128]{1,0:T(8,128)}, bf16[2,256,1024]{2,1,0:T(8,128)(2,1)}, f32[8,1024]{1,0:T(8,128)}) custom-call(s32[3]{0:T(128)} %pad_add_fusion.scal, bf16[128,2048]{1,0:T(8,128)(2,1)} %hold.10.refs_3_.refs_0_, bf16[128,2048]{1,0:T(8,128)(2,1)} %copy-done.22, ...), custom_call_target="tpu_custom_call" | custom-call | flops 20000000000 | bytes 1 | tf_op jit(solution)/shard_map/line_logits/pallas_call | solution.py:64
  82.6 1.1 copy.43
  83.8 0.8 slice.12.refs_0_
  84.7 0.8 copy-done.1
  85.9 0.5 collective-permute-start.16
  86.5 1.0 copy-done.2
  87.5 1.7 add.38.refs_7_
  89.2 0.8 copy-done.6
  90.0 12.2 %line_logits.3 = (bf16[512,2048]{1,0:T(8,128)(2,1)}, bf16[512,128]{1,0:T(8,128)(2,1)}, f32[512,128]{1,0:T(8,128)}, bf16[2,256,512]{2,1,0:T(8,128)(2,1)}, f32[8,1536]{1,0:T(8,128)}) custom-call(s32[3]{0:T(128)} %pad_add_fusion.scal, bf16[128,2048]{1,0:T(8,128)(2,1)} %get-tuple-element.69.refs_0_, bf16[128,2048]{1,0:T(8,128)(2,1)} %collective-permute-done.17.refs_1_, ...), custom_call_target="tpu_custom_call" | custom-call | flops 20000000000 | bytes 1 | tf_op jit(solution)/shard_map/line_logits/pallas_call | solution.py:64
  102.3 0.6 collective-permute-start.21
  102.9 1.5 collective-permute-start.25
  104.7 8.6 %tail_logits.1 = (bf16[128,1920]{1,0:T(8,128)(2,1)}, bf16[128,3840]{1,0:T(8,128)(2,1)}, f32[8,512]{1,0:T(8,128)}) custom-call(s32[3]{0:T(128)} %pad_add_fusion.scal, bf16[4,128,512]{2,1,0:T(8,128)(2,1)} %hold.15.refs_1_.refs_0_.refs_2_, bf16[4,128,512]{2,1,0:T(8,128)(2,1)} %collective-permute-done.15.refs_1_, bf16[4,128,512]{2,1,0:T(8,128)(2,1)} %hold.17.refs_2_.refs_12_, ...), custom_call_target="tpu_custom_call" | custom-call | flops 5000000000 | bytes 1 | tf_op jit(solution)/shard_map/tail_logits/pallas_call | solution.py:64
  113.3 1.6 collective-permute-start.24
  114.9 0.5 collective-permute-start.23
  115.4 1.6 collective-permute-done.25.refs_0_
  117.0 1.8 %collective-permute-done.23.refs_5_ = f32[8,512]{1,0:T(8,128)S(1)} collective-permute-done((f32[8,512]{1,0:T(8,128)}, f32[8,512]{1,0:T(8,128)S(1)}, u32[]{:S(2)}, u32[]{:S(2)}) %collective-permute-start.23) | collective-permute-done | bytes 16416 | tf_op jit(solution)/shard_map/ppermute | solution.py:21
  118.8 0.6 copy-done.30
  119.4 5.6 %tail_grads.1 = (bf16[1,1024,256]{2,1,0:T(8,128)(2,1)}, bf16[1,512,512]{2,1,0:T(8,128)(2,1)}, bf16[1,256,1024]{2,1,0:T(8,128)(2,1)}, bf16[1,128,2048]{2,1,0:T(8,128)(2,1)}, f32[128,1920]{1,0:T(8,128)}) custom-call(s32[3]{0:T(128)} %pad_add_fusion.scal, bf16[128,1920]{1,0:T(8,128)(2,1)} %get-tuple-element.72.refs_0_, ...), custom_call_target="tpu_custom_call" | custom-call | flops 3000000000 | bytes 1 | tf_op jit(solution)/shard_map/tail_grads/pallas_call | solution.py:64
  125.1 0.6 reverse_select_fusion
  125.7 0.6 collective-permute-start.30
  126.3 1.5 collective-permute-start.29
  127.8 1.2 copy-done.5
  129.0 0.6 add.39.refs_24_.refs_0_
  129.7 0.6 collective-permute-start.27
  130.3 0.5 collective-permute-done.29.refs_18_.refs_22_
  130.9 0.5 copy-done.24
  131.4 11.8 %head_weights.2 = (bf16[256,1536]{1,0:T(8,128)(2,1)}, bf16[256,1536]{1,0:T(8,128)(2,1)}, f32[2048,128]{1,0:T(8,128)}) custom-call(s32[3]{0:T(128)} %pad_add_fusion.scal, bf16[2,256,512]{2,1,0:T(8,128)(2,1)} %get-tuple-element.76.refs_0_, bf16[2,256,1024]{2,1,0:T(8,128)(2,1)} %get-tuple-element.77.refs_1_, bf16[2,256,512]{2,1,0:T(8,128)(2,1)} %get-tuple-element.78.refs_2_, ...), custom_call_target="tpu_custom_call" | custom-call | flops 8000000000 | bytes 1 | tf_op jit(solution)/shard_map/head_weights/pallas_call | solution.py:64
  143.2 1.5 collective-permute-start.31
  144.7 4.8 %tail_back.1 = (bf16[1,512,1024]{2,1,0:T(8,128)(2,1)}, bf16[1,512,512]{2,1,0:T(8,128)(2,1)}, bf16[1,512,256]{2,1,0:T(8,128)(2,1)}, bf16[1,512,128]{2,1,0:T(8,128)(2,1)}, bf16[4,128,512]{2,1,0:T(8,128)(2,1)}) custom-call(s32[3]{0:T(128)} %pad_add_fusion.scal, bf16[128,1920]{1,0:T(8,128)(2,1)} %copy-done.8, bf16[128,1920]{1,0:T(8,128)(2,1)} %collective-permute-done.27.refs_1_, ...), custom_call_target="tpu_custom_call" | custom-call | flops 3000000000 | bytes 1 | tf_op jit(solution)/shard_map/tail_back/pallas_call | solution.py:64
  149.5 1.9 %copy.44 = bf16[8,4,16,512]{3,2,1,0:T(8,128)(2,1)} copy(bf16[8,4,16,512]{3,2,0,1:T(8,128)(2,1)} %bitcast.22) | data formatting | bytes 1048576 | tf_op jit(solution)/shard_map/transpose | solution.py:667
  151.4 4.5 %all-to-all-start.1 = ((bf16[8,64,512]{2,1,0:T(8,128)(2,1)}), bf16[8,64,512]{2,1,0:T(8,128)(2,1)}, u32[]{:S(2)}, u32[]{:S(2)}) async-start(bf16[8,64,512]{2,1,0:T(8,128)(2,1)} %bitcast.15), calls=%async_computation.1 | async-start | bytes 1048576 | tf_op jit(solution)/shard_map/all_to_all | solution.py:668
  155.9 6.5 %head_weights.3 = (bf16[256,640]{1,0:T(8,128)(2,1)}, bf16[256,640]{1,0:T(8,128)(2,1)}) custom-call(s32[3]{0:T(128)} %pad_add_fusion.scal, bf16[2,256,512]{2,1,0:T(8,128)(2,1)} %get-tuple-element.76.refs_0_, bf16[2,256,1024]{2,1,0:T(8,128)(2,1)} %get-tuple-element.77.refs_1_, bf16[2,256,512]{2,1,0:T(8,128)(2,1)} %get-tuple-element.78.refs_2_, ...), custom_call_target="tpu_custom_call" | custom-call | flops 8000000000 | bytes 1 | tf_op jit(solution)/shard_map/head_weights/pallas_call | solution.py:64
  162.5 2.0 %collective-permute-start.32 = (bf16[256,640]{1,0:T(8,128)(2,1)}, bf16[256,640]{1,0:T(8,128)(2,1)}, u32[]{:S(2)}, u32[]{:S(2)}) collective-permute-start(bf16[256,640]{1,0:T(8,128)(2,1)} %get-tuple-element.89.refs_5_), channel_id=1, source_target_pairs={{0,4},{4,0},{8,12},{12,8},{16,20},{20,16},{24,28},{28,24},{1,5},{5... | collective-permute-start | bytes 983048 | tf_op jit(solution)/shard_map/ppermute | solution.py:764
  164.5 3.0 %collective-permute-done.31 = bf16[256,1536]{1,0:T(8,128)(2,1)} collective-permute-done((bf16[256,1536]{1,0:T(8,128)(2,1)}, bf16[256,1536]{1,0:T(8,128)(2,1)}, u32[]{:S(2)}, u32[]{:S(2)}) %collective-permute-start.31) | collective-permute-done | bytes 786464 | tf_op jit(solution)/shard_map/ppermute | solution.py:764
  167.5 1.6 add_convert_fusion
  169.1 1.1 all-to-all-done.1
  170.2 3.6 %grad_hidden.1.refs_2_ = bf16[512,512]{1,0:T(8,128)(2,1)} custom-call(s32[3]{0:T(128)} %pad_add_fusion.scal, bf16[512,512]{1,0:T(8,128)(2,1)} %get-tuple-element.57.refs_0_, bf16[512,512]{1,0:T(8,128)(2,1)} %bitcast.16.refs_1_, bf16[2,512,512]{2,1,0:T(8,128)(2,1)} %get-tuple-element.65.refs_3_.refs_0_.refs_2_, ...), custom_call_target="tpu_custom_call" | custom-call | flops 2000000000 | bytes 1 | tf_op jit(solution)/shard_map/grad_hidden/pallas_call | solution.py:64
  173.8 1.6 collective-permute-done.32.refs_1_
  175.4 1.2 add_convert_fusion.1
  176.6 0.7 copy.45
  177.3 1.1 pad_maximum_fusion
  (112 shorter events, 2.5 us)
Async XLA Ops:
  0.6 8.2 %copy-start.21 = (s32[512]{0:T(512)S(1)}, s32[512]{0:T(512)}, u32[]{:S(2)}) copy-start(s32[512]{0:T(512)} %param.15) | copy-start | bytes 6148
  2.5 17.2 %collective-permute-start = (bf16[128,2048]{1,0:T(8,128)(2,1)}, bf16[128,2048]{1,0:T(8,128)(2,1)S(1)}, u32[]{:S(2)}, u32[]{:S(2)}) collective-permute-start(bf16[128,2048]{1,0:T(8,128)(2,1)} %constant_dynamic-slice_fusion), channel_id=1, source_target_pairs={{0,8},{4,12},{8,16},{12,20},{16,24},{20,28},{24,0},{28,4},{1,9},{5... | collective-permute-start | bytes 1572872 | tf_op jit(solution)/shard_map/ppermute | solution.py:510
  19.7 0.8 copy-start.10
  20.5 15.3 %copy-start.20 = (f32[8,512]{1,0:T(8,128)S(1)}, f32[8,512]{1,0:T(8,128)}, u32[]{:S(2)}) copy-start(f32[8,512]{1,0:T(8,128)} %select_convert_fusion.ids_ref.refs_3_.refs_9_) | copy-start | bytes 49156
  20.5 15.2 %collective-permute-start.2 = (bf16[128,2048]{1,0:T(8,128)(2,1)}, bf16[128,2048]{1,0:T(8,128)(2,1)}, u32[]{:S(2)}, u32[]{:S(2)}) collective-permute-start(bf16[128,2048]{1,0:T(8,128)(2,1)} %hold.10.refs_3_.refs_0_), channel_id=1, source_target_pairs={{0,2},{1,3},{2,0},{3,1},{4,6},{5,7},{6,4},{7,5},{8,10},{9,11},{10,... | collective-permute-start | bytes 1572872 | tf_op jit(solution)/shard_map/ppermute | solution.py:21
  22.0 17.6 %collective-permute-start.1 = (bf16[128,2048]{1,0:T(8,128)(2,1)}, bf16[128,2048]{1,0:T(8,128)(2,1)S(1)}, u32[]{:S(2)}, u32[]{:S(2)}) collective-permute-start(bf16[128,2048]{1,0:T(8,128)(2,1)} %hold.10.refs_3_.refs_0_), channel_id=1, source_target_pairs={{0,8},{4,12},{8,16},{12,20},{16,24},{20,28},{24,0},{28,4},{1,9},{5... | collective-permute-start | bytes 1572872 | tf_op jit(solution)/shard_map/ppermute | solution.py:524
  33.9 6.5 %collective-permute-start.13 = (f32[8,512]{1,0:T(8,128)}, f32[8,512]{1,0:T(8,128)S(1)}, u32[]{:S(2)}, u32[]{:S(2)}) collective-permute-start(f32[8,512]{1,0:T(8,128)} %get-tuple-element.59.refs_2_.refs_4_.refs_12_), channel_id=1, source_target_pairs={{0,3},{1,2},{2,1},{3,0},{4,7},{5,6},{6,5},{7,4},{8,11},{9,10},{10,... | collective-permute-start | bytes 49160 | tf_op jit(solution)/shard_map/ppermute | solution.py:21
  33.9 6.5 %collective-permute-start.12 = (f32[8,512]{1,0:T(8,128)}, f32[8,512]{1,0:T(8,128)S(1)}, u32[]{:S(2)}, u32[]{:S(2)}) collective-permute-start(f32[8,512]{1,0:T(8,128)} %get-tuple-element.59.refs_2_.refs_4_.refs_12_), channel_id=1, source_target_pairs={{0,2},{1,3},{2,0},{3,1},{4,6},{5,7},{6,4},{7,5},{8,10},{9,11},{10,... | collective-permute-start | bytes 49160 | tf_op jit(solution)/shard_map/ppermute | solution.py:21
  34.5 6.5 %collective-permute-start.11 = (f32[8,512]{1,0:T(8,128)}, f32[8,512]{1,0:T(8,128)S(1)}, u32[]{:S(2)}, u32[]{:S(2)}) collective-permute-start(f32[8,512]{1,0:T(8,128)} %get-tuple-element.59.refs_2_.refs_4_.refs_12_), channel_id=1, source_target_pairs={{0,1},{1,0},{2,3},{3,2},{4,5},{5,4},{6,7},{7,6},{8,9},{9,8},{10,11... | collective-permute-start | bytes 49160 | tf_op jit(solution)/shard_map/ppermute | solution.py:21
  35.8 19.9 %collective-permute-start.10 = (f32[8,512]{1,0:T(8,128)S(1)}, f32[8,512]{1,0:T(8,128)S(1)}, u32[]{:S(2)}, u32[]{:S(2)}) collective-permute-start(f32[8,512]{1,0:T(8,128)S(1)} %copy-done.20), channel_id=1, source_target_pairs={{0,24},{4,28},{8,0},{12,4},{16,8},{20,12},{24,16},{28,20},{1,25},{... | collective-permute-start | bytes 49160 | tf_op jit(solution)/shard_map/ppermute | solution.py:497
  39.6 0.8 copy-start.12
  39.6 16.2 %collective-permute-start.9 = (f32[8,512]{1,0:T(8,128)S(1)}, f32[8,512]{1,0:T(8,128)S(1)}, u32[]{:S(2)}, u32[]{:S(2)}) collective-permute-start(f32[8,512]{1,0:T(8,128)S(1)} %copy-done.20), channel_id=1, source_target_pairs={{0,16},{4,20},{8,24},{12,28},{16,0},{20,4},{24,8},{28,12},{1,17},{... | collective-permute-start | bytes 49160 | tf_op jit(solution)/shard_map/ppermute | solution.py:497
  40.4 3.3 %copy-start.26 = (f32[8,512]{1,0:T(8,128)}, f32[8,512]{1,0:T(8,128)S(1)}, u32[]{:S(2)}) copy-start(f32[8,512]{1,0:T(8,128)S(1)} %collective-permute-done.13.refs_7_.refs_15_) | copy-start | bytes 49156
  40.4 15.9 %collective-permute-start.8 = (f32[8,512]{1,0:T(8,128)S(1)}, f32[8,512]{1,0:T(8,128)S(1)}, u32[]{:S(2)}, u32[]{:S(2)}) collective-permute-start(f32[8,512]{1,0:T(8,128)S(1)} %copy-done.20), channel_id=1, source_target_pairs={{0,8},{4,12},{8,16},{12,20},{16,24},{20,28},{24,0},{28,4},{1,9},{5... | collective-permute-start | bytes 49160 | tf_op jit(solution)/shard_map/ppermute | solution.py:497
  40.4 3.3 %copy-start.27 = (f32[8,512]{1,0:T(8,128)}, f32[8,512]{1,0:T(8,128)S(1)}, u32[]{:S(2)}) copy-start(f32[8,512]{1,0:T(8,128)S(1)} %collective-permute-done.12.refs_6_.refs_14_) | copy-start | bytes 49156
  40.4 16.5 %collective-permute-start.7 = (bf16[128,2048]{1,0:T(8,128)(2,1)}, bf16[128,2048]{1,0:T(8,128)(2,1)}, u32[]{:S(2)}, u32[]{:S(2)}) collective-permute-start(bf16[128,2048]{1,0:T(8,128)(2,1)} %get-tuple-element.61.refs_4_), channel_id=1, source_target_pairs={{0,2},{1,3},{2,0},{3,1},{4,6},{5,7},{6,4},{7,5},{8,10},{9,11},{10,... | collective-permute-start | bytes 1572872 | tf_op jit(solution)/shard_map/ppermute | solution.py:21
  41.0 2.7 %copy-start.28 = (f32[8,512]{1,0:T(8,128)}, f32[8,512]{1,0:T(8,128)S(1)}, u32[]{:S(2)}) copy-start(f32[8,512]{1,0:T(8,128)S(1)} %collective-permute-done.11.refs_5_.refs_13_) | copy-start | bytes 49156
  41.0 15.9 %collective-permute-start.6 = (bf16[128,2048]{1,0:T(8,128)(2,1)}, bf16[128,2048]{1,0:T(8,128)(2,1)}, u32[]{:S(2)}, u32[]{:S(2)}) collective-permute-start(bf16[128,2048]{1,0:T(8,128)(2,1)} %get-tuple-element.61.refs_4_), channel_id=1, source_target_pairs={{0,8},{4,12},{8,16},{12,20},{16,24},{20,28},{24,0},{28,4},{1,9},{5... | collective-permute-start | bytes 1572872 | tf_op jit(solution)/shard_map/ppermute | solution.py:524
  43.7 12.0 %copy-start.11 = (bf16[128,2048]{1,0:T(8,128)(2,1)S(1)}, bf16[128,2048]{1,0:T(8,128)(2,1)}, u32[]{:S(2)}) copy-start(bf16[128,2048]{1,0:T(8,128)(2,1)} %hold.10.refs_3_.refs_0_) | copy-start | bytes 1572868
  55.7 0.7 copy-start.13
  55.7 6.2 %collective-permute-start.3 = (bf16[128,2048]{1,0:T(8,128)(2,1)S(1)}, bf16[128,2048]{1,0:T(8,128)(2,1)S(1)}, u32[]{:S(2)}, u32[]{:S(2)}) collective-permute-start(bf16[128,2048]{1,0:T(8,128)(2,1)S(1)} %copy-done.11), channel_id=1, source_target_pairs={{0,1},{1,0},{2,3},{3,2},{4,5},{5,4},{6,7},{7,6},{8,9},{9,8},{10,11... | collective-permute-start | bytes 1572872 | tf_op jit(solution)/shard_map/ppermute | solution.py:21
  55.8 8.4 %collective-permute-start.4 = (bf16[128,2048]{1,0:T(8,128)(2,1)}, bf16[128,2048]{1,0:T(8,128)(2,1)}, u32[]{:S(2)}, u32[]{:S(2)}) collective-permute-start(bf16[128,2048]{1,0:T(8,128)(2,1)} %get-tuple-element.60.refs_1_.refs_2_), channel_id=1, source_target_pairs={{0,1},{1,0},{2,3},{3,2},{4,5},{5,4},{6,7},{7,6},{8,9},{9,8},{10,11... | collective-permute-start | bytes 1572872 | tf_op jit(solution)/shard_map/ppermute | solution.py:21
  56.3 8.0 %collective-permute-start.5 = (bf16[128,2048]{1,0:T(8,128)(2,1)}, bf16[128,2048]{1,0:T(8,128)(2,1)}, u32[]{:S(2)}, u32[]{:S(2)}) collective-permute-start(bf16[128,2048]{1,0:T(8,128)(2,1)} %get-tuple-element.61.refs_4_), channel_id=1, source_target_pairs={{0,1},{1,0},{2,3},{3,2},{4,5},{5,4},{6,7},{7,6},{8,9},{9,8},{10,11... | collective-permute-start | bytes 1572872 | tf_op jit(solution)/shard_map/ppermute | solution.py:21
  56.9 7.4 %collective-permute-start.14 = (bf16[128,2048]{1,0:T(8,128)(2,1)}, bf16[128,2048]{1,0:T(8,128)(2,1)}, u32[]{:S(2)}, u32[]{:S(2)}) collective-permute-start(bf16[128,2048]{1,0:T(8,128)(2,1)} %get-tuple-element.67.refs_6_.refs_10_), channel_id=1, source_target_pairs={{0,1},{1,0},{2,3},{3,2},{4,5},{5,4},{6,7},{7,6},{8,9},{9,8},{10,11... | collective-permute-start | bytes 1572872 | tf_op jit(solution)/shard_map/ppermute | solution.py:21
  57.1 25.6 %all-to-all-start = ((bf16[8,64,640]{2,1,0:T(8,128)(2,1)}), bf16[8,64,640]{2,1,0:T(8,128)(2,1)}, u32[]{:S(2)}, u32[]{:S(2)}) async-start(bf16[8,64,640]{2,1,0:T(8,128)(2,1)} %bitcast.4), calls=%async_computation | async-start | bytes 1310720 | tf_op jit(solution)/shard_map/all_to_all | solution.py:603
  61.5 25.0 %collective-permute-start.20 = (bf16[2,512,512]{2,1,0:T(8,128)(2,1)}, bf16[2,512,512]{2,1,0:T(8,128)(2,1)}, u32[]{:S(2)}, u32[]{:S(2)}) collective-permute-start(bf16[2,512,512]{2,1,0:T(8,128)(2,1)} %get-tuple-element.70), channel_id=1, source_target_pairs={{0,1},{1,0},{2,3},{3,2},{4,5},{5,4},{6,7},{7,6},{8,9},{9,8},{10,11... | collective-permute-start | bytes 3145736 | tf_op jit(solution)/shard_map/ppermute | solution.py:21
  61.9 0.8 copy-start.22
  62.7 21.9 %collective-permute-start.18 = (bf16[128,2048]{1,0:T(8,128)(2,1)}, bf16[128,2048]{1,0:T(8,128)(2,1)S(1)}, u32[]{:S(2)}, u32[]{:S(2)}) collective-permute-start(bf16[128,2048]{1,0:T(8,128)(2,1)} %get-tuple-element.69.refs_0_), channel_id=1, source_target_pairs={{0,2},{1,3},{2,0},{3,1},{4,6},{5,7},{6,4},{7,5},{8,10},{9,11},{10,... | collective-permute-start | bytes 1572872 | tf_op jit(solution)/shard_map/ppermute | solution.py:21
  64.3 25.8 %collective-permute-start.17 = (bf16[128,2048]{1,0:T(8,128)(2,1)}, bf16[128,2048]{1,0:T(8,128)(2,1)}, u32[]{:S(2)}, u32[]{:S(2)}) collective-permute-start(bf16[128,2048]{1,0:T(8,128)(2,1)} %get-tuple-element.69.refs_0_), channel_id=1, source_target_pairs={{0,1},{1,0},{2,3},{3,2},{4,5},{5,4},{6,7},{7,6},{8,9},{9,8},{10,11... | collective-permute-start | bytes 1572872 | tf_op jit(solution)/shard_map/ppermute | solution.py:21
  83.8 5.4 %copy-start.9 = (bf16[4,8,16,640]{3,2,1,0:T(8,128)(2,1)}, bf16[4,8,16,640]{3,2,1,0:T(8,128)(2,1)S(1)}, u32[]{:S(2)}) copy-start(bf16[4,8,16,640]{3,2,1,0:T(8,128)(2,1)S(1)} %copy.43) | copy-start | bytes 1966084
  83.8 2.7 %copy-start = (bf16[2,512,512]{2,1,0:T(8,128)(2,1)S(1)}, bf16[2,512,512]{2,1,0:T(8,128)(2,1)}, u32[]{:S(2)}) copy-start(bf16[2,512,512]{2,1,0:T(8,128)(2,1)} %get-tuple-element.65.refs_3_.refs_0_.refs_2_) | copy-start | bytes 3145732
  83.8 2.7 %copy-start.3 = (s32[3]{0:T(128)S(1)}, s32[3]{0:T(128)}, u32[]{:S(2)}) copy-start(s32[3]{0:T(128)} %pad_add_fusion.scal) | copy-start | bytes 40
  84.7 0.8 copy-start.1
  85.5 4.6 %collective-permute-start.19 = (bf16[128,2048]{1,0:T(8,128)(2,1)}, bf16[128,2048]{1,0:T(8,128)(2,1)}, u32[]{:S(2)}, u32[]{:S(2)}) collective-permute-start(bf16[128,2048]{1,0:T(8,128)(2,1)} %hold.16.refs_2_), channel_id=1, source_target_pairs={{0,1},{1,0},{2,3},{3,2},{4,5},{5,4},{6,7},{7,6},{8,9},{9,8},{10,11... | collective-permute-start | bytes 1572872 | tf_op jit(solution)/shard_map/ppermute | solution.py:21
  85.9 16.3 %collective-permute-start.16 = (bf16[4,128,512]{2,1,0:T(8,128)(2,1)}, bf16[4,128,512]{2,1,0:T(8,128)(2,1)}, u32[]{:S(2)}, u32[]{:S(2)}) collective-permute-start(bf16[4,128,512]{2,1,0:T(8,128)(2,1)} %hold.15.refs_1_.refs_0_.refs_2_), channel_id=1, source_target_pairs={{0,2},{1,3},{2,0},{3,1},{4,6},{5,7},{6,4},{7,5},{8,10},{9,11},{10,... | collective-permute-start | bytes 1572872 | tf_op jit(solution)/shard_map/ppermute | solution.py:21
  86.4 17.9 %collective-permute-start.15 = (bf16[4,128,512]{2,1,0:T(8,128)(2,1)}, bf16[4,128,512]{2,1,0:T(8,128)(2,1)}, u32[]{:S(2)}, u32[]{:S(2)}) collective-permute-start(bf16[4,128,512]{2,1,0:T(8,128)(2,1)} %hold.15.refs_1_.refs_0_.refs_2_), channel_id=1, source_target_pairs={{0,1},{1,0},{2,3},{3,2},{4,5},{5,4},{6,7},{7,6},{8,9},{9,8},{10,11... | collective-permute-start | bytes 1572872 | tf_op jit(solution)/shard_map/ppermute | solution.py:21
  86.5 1.0 copy-start.2
  89.2 0.8 copy-start.6
  90.0 12.8 %copy-start.7 = (bf16[512,512]{1,0:T(8,128)(2,1)S(1)}, bf16[512,512]{1,0:T(8,128)(2,1)}, u32[]{:S(2)}) copy-start(bf16[512,512]{1,0:T(8,128)(2,1)} %copy-done.6) | copy-start | bytes 1572868
  102.3 2.5 %collective-permute-start.21 = (bf16[4,128,512]{2,1,0:T(8,128)(2,1)}, bf16[4,128,512]{2,1,0:T(8,128)(2,1)}, u32[]{:S(2)}, u32[]{:S(2)}) collective-permute-start(bf16[4,128,512]{2,1,0:T(8,128)(2,1)} %hold.17.refs_2_.refs_12_), channel_id=1, source_target_pairs={{0,1},{1,0},{2,3},{3,2},{4,5},{5,4},{6,7},{7,6},{8,9},{9,8},{10,11... | collective-permute-start | bytes 1572872 | tf_op jit(solution)/shard_map/ppermute | solution.py:21
  102.9 14.1 %collective-permute-start.25 = (bf16[512,512]{1,0:T(8,128)(2,1)S(1)}, bf16[512,512]{1,0:T(8,128)(2,1)}, u32[]{:S(2)}, u32[]{:S(2)}) collective-permute-start(bf16[512,512]{1,0:T(8,128)(2,1)S(1)} %copy-done.7), channel_id=1, source_target_pairs={{0,2},{1,3},{2,0},{3,1},{4,6},{5,7},{6,4},{7,5},{8,10},{9,11},{10,... | collective-permute-start | bytes 1572872 | tf_op jit(solution)/shard_map/ppermute | solution.py:21
  113.3 3.7 %collective-permute-start.24 = (f32[8,512]{1,0:T(8,128)}, f32[8,512]{1,0:T(8,128)S(1)}, u32[]{:S(2)}, u32[]{:S(2)}) collective-permute-start(f32[8,512]{1,0:T(8,128)} %get-tuple-element.74.refs_1_.refs_3_), channel_id=1, source_target_pairs={{0,3},{1,2},{2,1},{3,0},{4,7},{5,6},{6,5},{7,4},{8,11},{9,10},{10,... | collective-permute-start | bytes 49160 | tf_op jit(solution)/shard_map/ppermute | solution.py:21
  114.9 3.9 %collective-permute-start.23 = (f32[8,512]{1,0:T(8,128)}, f32[8,512]{1,0:T(8,128)S(1)}, u32[]{:S(2)}, u32[]{:S(2)}) collective-permute-start(f32[8,512]{1,0:T(8,128)} %get-tuple-element.74.refs_1_.refs_3_), channel_id=1, source_target_pairs={{0,2},{1,3},{2,0},{3,1},{4,6},{5,7},{6,4},{7,5},{8,10},{9,11},{10,... | collective-permute-start | bytes 49160 | tf_op jit(solution)/shard_map/ppermute | solution.py:21
  115.4 3.4 %collective-permute-start.22 = (f32[8,512]{1,0:T(8,128)}, f32[8,512]{1,0:T(8,128)S(1)}, u32[]{:S(2)}, u32[]{:S(2)}) collective-permute-start(f32[8,512]{1,0:T(8,128)} %get-tuple-element.74.refs_1_.refs_3_), channel_id=1, source_target_pairs={{0,1},{1,0},{2,3},{3,2},{4,5},{5,4},{6,7},{7,6},{8,9},{9,8},{10,11... | collective-permute-start | bytes 49160 | tf_op jit(solution)/shard_map/ppermute | solution.py:21
  117.0 1.8 %copy-start.29 = (f32[8,512]{1,0:T(8,128)}, f32[8,512]{1,0:T(8,128)S(1)}, u32[]{:S(2)}) copy-start(f32[8,512]{1,0:T(8,128)S(1)} %collective-permute-done.24.refs_6_) | copy-start | bytes 49156
  118.8 0.6 copy-start.31
  119.4 5.6 %copy-start.14 = (f32[8,512]{1,0:T(8,128)S(1)}, f32[8,512]{1,0:T(8,128)}, u32[]{:S(2)}) copy-start(f32[8,512]{1,0:T(8,128)} %get-tuple-element.66.refs_2_) | copy-start | bytes 49156
  119.4 5.6 %copy-start.16 = (f32[8,512]{1,0:T(8,128)S(1)}, f32[8,512]{1,0:T(8,128)}, u32[]{:S(2)}) copy-start(f32[8,512]{1,0:T(8,128)} %get-tuple-element.84) | copy-start | bytes 49156
  119.4 5.6 %copy-start.18 = (f32[8,512]{1,0:T(8,128)S(1)}, f32[8,512]{1,0:T(8,128)}, u32[]{:S(2)}) copy-start(f32[8,512]{1,0:T(8,128)} %get-tuple-element.83) | copy-start | bytes 49156
  119.4 6.3 %copy-start.19 = (f32[8,1536]{1,0:T(8,128)S(1)}, f32[8,1536]{1,0:T(8,128)}, u32[]{:S(2)}) copy-start(f32[8,1536]{1,0:T(8,128)} %get-tuple-element.71.refs_1_.refs_16_.refs_20_) | copy-start | bytes 147460
  119.4 8.4 %copy-start.4 = (s32[3]{0:T(128)S(1)}, s32[3]{0:T(128)}, u32[]{:S(2)}) copy-start(s32[3]{0:T(128)} %pad_add_fusion.scal) | copy-start | bytes 40
  125.0 2.8 %collective-permute-start.26 = (f32[128,1920]{1,0:T(8,128)}, f32[128,1920]{1,0:T(8,128)S(1)}, u32[]{:S(2)}, u32[]{:S(2)}) collective-permute-start(f32[128,1920]{1,0:T(8,128)} %get-tuple-element.75.refs_0_.refs_2_), channel_id=1, source_target_pairs={{0,1},{1,0},{2,3},{3,2},{4,5},{5,4},{6,7},{7,6},{8,9},{9,8},{10,11... | collective-permute-start | bytes 2949128 | tf_op jit(solution)/shard_map/ppermute | solution.py:21
  125.7 4.6 %collective-permute-start.30 = (f32[8,1536]{1,0:T(8,128)S(1)}, f32[8,1536]{1,0:T(8,128)S(1)}, u32[]{:S(2)}, u32[]{:S(2)}) collective-permute-start(f32[8,1536]{1,0:T(8,128)S(1)} %copy-done.19), channel_id=1, source_target_pairs={{0,3},{1,2},{2,1},{3,0},{4,7},{5,6},{6,5},{7,4},{8,11},{9,10},{10,... | collective-permute-start | bytes 147464 | tf_op jit(solution)/shard_map/ppermute | solution.py:21
  126.3 4.5 %collective-permute-start.29 = (f32[8,1536]{1,0:T(8,128)S(1)}, f32[8,1536]{1,0:T(8,128)S(1)}, u32[]{:S(2)}, u32[]{:S(2)}) collective-permute-start(f32[8,1536]{1,0:T(8,128)S(1)} %copy-done.19), channel_id=1, source_target_pairs={{0,2},{1,3},{2,0},{3,1},{4,6},{5,7},{6,4},{7,5},{8,10},{9,11},{10,... | collective-permute-start | bytes 147464 | tf_op jit(solution)/shard_map/ppermute | solution.py:21
  127.8 3.0 %collective-permute-start.28 = (f32[8,1536]{1,0:T(8,128)S(1)}, f32[8,1536]{1,0:T(8,128)S(1)}, u32[]{:S(2)}, u32[]{:S(2)}) collective-permute-start(f32[8,1536]{1,0:T(8,128)S(1)} %copy-done.19), channel_id=1, source_target_pairs={{0,1},{1,0},{2,3},{3,2},{4,5},{5,4},{6,7},{7,6},{8,9},{9,8},{10,11... | collective-permute-start | bytes 147464 | tf_op jit(solution)/shard_map/ppermute | solution.py:21
  127.8 1.2 copy-start.5
  129.7 1.1 copy-start.8
  129.7 15.0 %collective-permute-start.27 = (bf16[128,1920]{1,0:T(8,128)(2,1)S(1)}, bf16[128,1920]{1,0:T(8,128)(2,1)}, u32[]{:S(2)}, u32[]{:S(2)}) collective-permute-start(bf16[128,1920]{1,0:T(8,128)(2,1)S(1)} %add.39.refs_24_.refs_0_), channel_id=1, source_target_pairs={{0,2},{1,3},{2,0},{3,1},{4,6},{5,7},{6,4},{7,5},{8,10},{9,11},{10,... | collective-permute-start | bytes 1474568 | tf_op jit(solution)/shard_map/ppermute | solution.py:21
  130.3 0.6 copy-start.23
  130.8 0.6 copy-start.24
  130.8 0.6 copy-start.25
  143.2 24.3 %collective-permute-start.31 = (bf16[256,1536]{1,0:T(8,128)(2,1)}, bf16[256,1536]{1,0:T(8,128)(2,1)}, u32[]{:S(2)}, u32[]{:S(2)}) collective-permute-start(bf16[256,1536]{1,0:T(8,128)(2,1)} %get-tuple-element.91), channel_id=1, source_target_pairs={{0,4},{4,0},{8,12},{12,8},{16,20},{20,16},{24,28},{28,24},{1,5},{5... | collective-permute-start | bytes 2359304 | tf_op jit(solution)/shard_map/ppermute | solution.py:764
  151.4 18.8 %all-to-all-start.1 = ((bf16[8,64,512]{2,1,0:T(8,128)(2,1)}), bf16[8,64,512]{2,1,0:T(8,128)(2,1)}, u32[]{:S(2)}, u32[]{:S(2)}) async-start(bf16[8,64,512]{2,1,0:T(8,128)(2,1)} %bitcast.15), calls=%async_computation.1 | async-start | bytes 1048576 | tf_op jit(solution)/shard_map/all_to_all | solution.py:668
  162.5 12.9 %collective-permute-start.32 = (bf16[256,640]{1,0:T(8,128)(2,1)}, bf16[256,640]{1,0:T(8,128)(2,1)}, u32[]{:S(2)}, u32[]{:S(2)}) collective-permute-start(bf16[256,640]{1,0:T(8,128)(2,1)} %get-tuple-element.89.refs_5_), channel_id=1, source_target_pairs={{0,4},{4,0},{8,12},{12,8},{16,20},{20,16},{24,28},{28,24},{1,5},{5... | collective-permute-start | bytes 983048 | tf_op jit(solution)/shard_map/ppermute | solution.py:764
  (3 other events, 1.8 us)

commit v3 on v2

--- a/solution.py
+++ b/solution.py
@@ -72,7 +72,7 @@
             out_specs=out_specs,
             scratch_shapes=list(scratch),
         ),
-        compiler_params=pltpu.CompilerParams(vmem_limit_bytes=(16 if name in SMALL else 63) << 20),
+        compiler_params=pltpu.CompilerParams(vmem_limit_bytes=(1023 * 64 if name not in SMALL else 16384) << 10),
         cost_estimate=pl.CostEstimate(
             flops=int(MICROSECONDS[name] * COST_SCALE * 1e9), bytes_accessed=1, transcendentals=0
         ),
@@ -424,13 +424,20 @@
         to += vcols
 
 
-def tail_back_kernel(cfg, scal, part, far, rows_ref, p1, p2, p3, p4, g1, g2, g3, g4, back_ref):
+def tail_back_kernel(in_place, scal, part, far, rows_ref, p1, p2, p3, p4, g1, g2, g3, g4, back_ref):
+    own = p1.shape[1]
     dred = (part[...].astype(F32) + far[...].astype(F32)).astype(BF16)
     at = 0
     for band, (proj, grad) in enumerate(zip((p1, p2, p3, p4), (g1, g2, g3, g4))):
         size = proj.shape[2]
         mine = dred[:, at : at + size]
-        back_ref[band] = dot_nt(mine, proj[0]).astype(BF16)
+        back = dot_nt(mine, proj[0]).astype(BF16)
+        if in_place:
+            groups = back_ref.shape[0]
+            rows = back.shape[0] // groups
+            back_ref[:, band * rows : (band + 1) * rows, :] = back.reshape(groups, rows, own)
+        else:
+            back_ref[band] = back
         grad[0] = dot_tn(rows_ref[band], mine).astype(BF16)
         at += size
 
@@ -651,10 +658,13 @@
 
     def tail_back():
         outs = [struct((1, own_width, p.shape[2]), BF16) for p in projections]
-        outs.append(struct((4, slots, own_width), BF16))
+        in_place = capacity % 16 == 0
+        outs.append(
+            struct((groups, 4 * capacity, own_width) if in_place else (4, slots, own_width), BF16)
+        )
         *grads_proj, back = order.call(
             tail_back_kernel,
-            None,
+            in_place,
             "tail_back",
             (part, far, rows, *projections),
             [whole(part), whole(far), whole(rows)] + proj_specs,
@@ -664,7 +674,8 @@
         return grads_proj, back
 
     def tail_return(back):
-        back = back.reshape(4, groups, capacity, own_width).transpose(1, 0, 2, 3)
+        if back.shape[0] != groups or capacity % 16:
+            back = back.reshape(4, groups, capacity, own_width).transpose(1, 0, 2, 3)
         returned = lax.all_to_all(
             back.reshape(groups, 4 * capacity, own_width),
             "vocab",
@@ -775,13 +786,13 @@
         return mine
 
     dispatch, send = tail_rows()
+    moved_ids = order.hold(*moved_ids)
     move_rows(1)
     early = head_group(0)
     early = [early] + shared(early)
     move_rows(2)
     rows, digits = tail_send(*order.hold(send))
     back_keep, back_beside = head_back()
-    moved_ids = order.hold(*moved_ids)
     move_rows(3)
     late = head_group(1, 2)
     (rows,) = order.hold(rows)

time: 180 us -> 177 us (0.983)
  local copies, waits for them, and re-layouts: 16.4 us -> 9.98 us
  other arithmetic: 6.45 us -> 8.79 us
    ppermute x1, waiting for transfers between devices: 5.87 us -> 0.01 us  [body(): from_line = {1: lax.ppermute(piece, 'vocab', ring)}]
    unnamed x66 -> x16, local copies, waits for them, and re-layouts: 9.69 us -> 5.19 us
    ppermute x2, waiting for transfers between devices: 0.01 us -> 3.67 us  [move_rows(): from_line[stage + 1] = lax.ppermute(held, 'vocab', ring)]
    ppermute x3, waiting for transfers between devices: 0.01 us -> 2.06 us  [body(): lax.ppermute(ids, 'vocab', [(i, (i + step * near) % groups) for i in rang...]
    transpose x1 -> x0, local copies, waits for them, and re-layouts: 1.87 us -> none  [tail_return(): back = back.reshape(4, groups, capacity, own_width).transpose(1, 0, 2, 3)]
  transfers between devices with their start and end apart: 35 -> 35, of which waited for: 8 -> 11; matrix products, arithmetic and copies ran while one was open for 6% -> 6% of each run, Pallas kernels for 54% -> 55%
where the time goes in v3:
time: 177 us; the launch traced here: 175 us
  Pallas kernels  102 us (58%)
  starting transfers between devices  36.1 us (20%)
  waiting for transfers between devices  17.5 us (10%)
  local copies, waits for them, and re-layouts  9.98 us (6%)
  other arithmetic  8.79 us (5%)
    pallas_call x13, Pallas kernels, kernel_call(): pl.pallas_call(kernel, name=name, out_shape=outs, grid_spec=pltpu.Prefetc...  102 us
    ppermute x25, starting transfers between devices, tp_swap(): return lax.ppermute(value, 'tp', xor_pairs(lax.axis_size('tp'), step))  13.9 us
    ppermute x2, waiting for transfers between devices, near_parts(): parts.append(lax.ppermute(part, 'vocab', xor_pairs(groups, step)))  6.32 us
    ppermute x25, waiting for transfers between devices, tp_swap(): return lax.ppermute(value, 'tp', xor_pairs(lax.axis_size('tp'), step))  5.43 us
    all_to_all x1, starting transfers between devices, tail_return(): lax.all_to_all(back.reshape(groups, 4 * capacity, own_width), 'vocab', sp...  5.36 us
    unnamed x16, local copies, waits for them, and re-layouts  5.19 us
    ppermute x3, starting transfers between devices, body(): lax.ppermute(ids, 'vocab', [(i, (i + step * near) % groups) for i in rang...  4.61 us
    all_to_all x1, starting transfers between devices, tail_send(): lax.all_to_all(send.reshape(groups, 4 * capacity, own_width + LANES), 'vo...  4.39 us
  transfers between devices with their start and end apart: 35, of which 11 were waited for; matrix products, arithmetic and copies ran while one was open for 6% of the time, Pallas kernels for 55%

profile of v3, /device:TPU:0, one launch (start us, length us, event | category | flops | bytes accessed | tf_op | source)
XLA Modules:
  0.0 175.4 jit_solution(10879237665670158726)
XLA Ops:
  0.6 1.9 %constant_dynamic-slice_fusion = bf16[128,2048]{1,0:T(8,128)(2,1)} fusion(bf16[512,2048]{1,0:T(8,128)(2,1)} %refs_0_.1, s32[]{:T(128)S(6)} %select_n.70), kind=kLoop, calls=%fused_computation.13 | loop fusion | bytes 1048580 | tf_op jit(solution)/shard_map/dynamic_slice | solution.py:516
  2.5 3.0 %collective-permute-start = (bf16[128,2048]{1,0:T(8,128)(2,1)}, bf16[128,2048]{1,0:T(8,128)(2,1)}, u32[]{:S(2)}, u32[]{:S(2)}) collective-permute-start(bf16[128,2048]{1,0:T(8,128)(2,1)} %constant_dynamic-slice_fusion), channel_id=1, source_target_pairs={{0,8},{4,12},{8,16},{12,20},{16,24},{20,28},{24,0},{28,4},{1,9},{5... | collective-permute-start | bytes 1572872 | tf_op jit(solution)/shard_map/ppermute | solution.py:517
  5.6 0.7 compare_select_fusion.1
  6.3 1.4 select_convert_fusion.ids_ref.refs_3_.refs_9_
  7.6 2.0 %collective-permute-start.3 = (f32[8,512]{1,0:T(8,128)}, f32[8,512]{1,0:T(8,128)}, u32[]{:S(2)}, u32[]{:S(2)}) collective-permute-start(f32[8,512]{1,0:T(8,128)} %select_convert_fusion.ids_ref.refs_3_.refs_9_), channel_id=1, source_target_pairs={{0,24},{4,28},{8,0},{12,4},{16,8},{20,12},{24,16},{28,20},{1,25},{... | collective-permute-start | bytes 49160 | tf_op jit(solution)/shard_map/ppermute | solution.py:504
  9.6 1.0 collective-permute-start.2
  10.7 1.6 collective-permute-start.1
  12.2 0.6 pad_add_fusion.scal
  12.9 4.3 %send_rows.1 = (bf16[512,512]{1,0:T(8,128)(2,1)}, bf16[512,640]{1,0:T(8,128)(2,1)}) custom-call(s32[3]{0:T(128)} %pad_add_fusion.scal, f32[8,512]{1,0:T(8,128)} %select_convert_fusion.ids_ref.refs_3_.refs_9_, bf16[512,2048]{1,0:T(8,128)(2,1)} %refs_0_.1), custom_call_target="tpu_custom_call" | custom-call | flops 3000000000 | bytes 1 | tf_op jit(solution)/shard_map/send_rows/pallas_call | solution.py:64
  17.2 1.0 copy.41
  18.3 0.9 pad.4.refs_2_.refs_9_.refs_6_
  19.2 0.5 collective-permute-done.3.refs_2_
  19.6 1.6 collective-permute-done.2.refs_1_
  21.2 1.6 collective-permute-start.5
  23.1 11.8 %head_logits.1 = (bf16[512,2048]{1,0:T(8,128)(2,1)}, bf16[512,128]{1,0:T(8,128)(2,1)}, f32[512,128]{1,0:T(8,128)}, bf16[2,256,512]{2,1,0:T(8,128)(2,1)}, f32[8,512]{1,0:T(8,128)}) custom-call(s32[3]{0:T(128)} %pad_add_fusion.scal, bf16[512,2048]{1,0:T(8,128)(2,1)} %refs_0_.1, bf16[2048,2048]{1,0:T(8,128)(2,1)} %refs_5_.3, ...), custom_call_target="tpu_custom_call" | custom-call | flops 8999999488 | bytes 1 | tf_op jit(solution)/shard_map/head_logits/pallas_call | solution.py:64
  35.0 1.0 collective-permute-start.12
  36.0 0.8 collective-permute-start.11
  36.9 1.6 collective-permute-done.4.refs_0_
  38.5 0.6 collective-permute-start.10
  39.1 0.9 collective-permute-start.9
  40.0 11.8 %head_back.1 = (bf16[2,512,512]{2,1,0:T(8,128)(2,1)}, bf16[2,512,512]{2,1,0:T(8,128)(2,1)}) custom-call(s32[3]{0:T(128)} %pad_add_fusion.scal, bf16[512,2048]{1,0:T(8,128)(2,1)} %get-tuple-element.63.refs_0_.refs_3_, bf16[512,128]{1,0:T(8,128)(2,1)} %get-tuple-element.64.refs_1_.refs_7_, f32[512,128]{1,0:T(8,128)} %get-tuple-element.65.refs_2_.refs_6_, ...), custom_call_target="tpu_custom_call" | custom-call | flops 8999999488 | bytes 1 | tf_op jit(solution)/shard_map/head_back/pallas_call | solution.py:64
  51.9 1.3 collective-permute-done.10.refs_1_
  53.2 2.0 %collective-permute-done.9.refs_0_ = bf16[128,2048]{1,0:T(8,128)(2,1)} collective-permute-done((bf16[128,2048]{1,0:T(8,128)(2,1)}, bf16[128,2048]{1,0:T(8,128)(2,1)}, u32[]{:S(2)}, u32[]{:S(2)}) %collective-permute-start.9) | collective-permute-done | bytes 524320 | tf_op jit(solution)/shard_map/ppermute | solution.py:531
  55.2 4.4 %all-to-all-start = ((bf16[8,64,640]{2,1,0:T(8,128)(2,1)}), bf16[8,64,640]{2,1,0:T(8,128)(2,1)}, u32[]{:S(2)}, u32[]{:S(2)}) async-start(bf16[8,64,640]{2,1,0:T(8,128)(2,1)} %bitcast.4), calls=%async_computation | async-start | bytes 1310720 | tf_op jit(solution)/shard_map/all_to_all | solution.py:610
  59.6 0.6 collective-permute-start.20
  60.2 1.5 collective-permute-start.18
  61.7 18.3 %line_logits.2 = (bf16[1024,2048]{1,0:T(8,128)(2,1)}, bf16[1024,128]{1,0:T(8,128)(2,1)}, f32[1024,128]{1,0:T(8,128)}, bf16[2,256,1024]{2,1,0:T(8,128)(2,1)}, f32[8,1024]{1,0:T(8,128)}) custom-call(s32[3]{0:T(128)} %pad_add_fusion.scal, bf16[128,2048]{1,0:T(8,128)(2,1)} %hold.11.refs_3_.refs_0_, bf16[128,2048]{1,0:T(8,128)(2,1)} %collective-permute-done.6.refs_1_, ...), custom_call_target="tpu_custom_call" | custom-call | flops 20000000000 | bytes 1 | tf_op jit(solution)/shard_map/line_logits/pallas_call | solution.py:64
  80.0 1.1 copy.42
  81.2 0.8 copy-done.6
  82.1 0.8 slice.12.refs_0_
  82.9 0.5 collective-permute-start.19
  83.4 0.5 collective-permute-start.16
  83.9 1.7 add.38.refs_7_
  85.6 0.8 copy-done.4
  86.4 12.1 %line_logits.3 = (bf16[512,2048]{1,0:T(8,128)(2,1)}, bf16[512,128]{1,0:T(8,128)(2,1)}, f32[512,128]{1,0:T(8,128)}, bf16[2,256,512]{2,1,0:T(8,128)(2,1)}, f32[8,1536]{1,0:T(8,128)}) custom-call(s32[3]{0:T(128)} %pad_add_fusion.scal, bf16[128,2048]{1,0:T(8,128)(2,1)} %get-tuple-element.69.refs_0_, bf16[128,2048]{1,0:T(8,128)(2,1)} %collective-permute-done.17.refs_1_, ...), custom_call_target="tpu_custom_call" | custom-call | flops 20000000000 | bytes 1 | tf_op jit(solution)/shard_map/line_logits/pallas_call | solution.py:64
  98.5 0.6 collective-permute-start.21
  99.1 1.5 collective-permute-start.25
  100.9 8.6 %tail_logits.1 = (bf16[128,1920]{1,0:T(8,128)(2,1)}, bf16[128,3840]{1,0:T(8,128)(2,1)}, f32[8,512]{1,0:T(8,128)}) custom-call(s32[3]{0:T(128)} %pad_add_fusion.scal, bf16[4,128,512]{2,1,0:T(8,128)(2,1)} %hold.15.refs_1_.refs_0_.refs_2_, bf16[4,128,512]{2,1,0:T(8,128)(2,1)} %collective-permute-done.15.refs_1_, bf16[4,128,512]{2,1,0:T(8,128)(2,1)} %hold.17.refs_2_.refs_12_, ...), custom_call_target="tpu_custom_call" | custom-call | flops 5000000000 | bytes 1 | tf_op jit(solution)/shard_map/tail_logits/pallas_call | solution.py:64
  109.5 1.6 collective-permute-start.24
  111.1 0.5 collective-permute-start.23
  111.6 1.9 %collective-permute-done.25.refs_0_ = bf16[512,512]{1,0:T(8,128)(2,1)} collective-permute-done((bf16[512,512]{1,0:T(8,128)(2,1)}, bf16[512,512]{1,0:T(8,128)(2,1)}, u32[]{:S(2)}, u32[]{:S(2)}) %collective-permute-start.25) | collective-permute-done | bytes 524320 | tf_op jit(solution)/shard_map/ppermute | solution.py:21
  113.5 1.7 collective-permute-done.23.refs_5_
  115.1 5.4 %tail_grads.1 = (bf16[1,1024,256]{2,1,0:T(8,128)(2,1)}, bf16[1,512,512]{2,1,0:T(8,128)(2,1)}, bf16[1,256,1024]{2,1,0:T(8,128)(2,1)}, bf16[1,128,2048]{2,1,0:T(8,128)(2,1)}, f32[128,1920]{1,0:T(8,128)}) custom-call(s32[3]{0:T(128)} %pad_add_fusion.scal, bf16[128,1920]{1,0:T(8,128)(2,1)} %get-tuple-element.72.refs_0_, ...), custom_call_target="tpu_custom_call" | custom-call | flops 3000000000 | bytes 1 | tf_op jit(solution)/shard_map/tail_grads/pallas_call | solution.py:64
  120.6 0.8 pad_maximum_fusion.1
  121.3 0.6 reverse_select_fusion
  122.0 0.6 collective-permute-start.30
  122.6 1.5 collective-permute-start.29
  124.1 0.7 copy-done.2
  124.8 1.2 copy-done.3
  126.0 1.4 add.39.refs_24_.refs_0_
  127.4 0.5 collective-permute-start.27
  127.9 11.8 %head_weights.2 = (bf16[256,1536]{1,0:T(8,128)(2,1)}, bf16[256,1536]{1,0:T(8,128)(2,1)}, f32[2048,128]{1,0:T(8,128)}) custom-call(s32[3]{0:T(128)} %pad_add_fusion.scal, bf16[2,256,512]{2,1,0:T(8,128)(2,1)} %get-tuple-element.76.refs_0_, bf16[2,256,1024]{2,1,0:T(8,128)(2,1)} %get-tuple-element.77.refs_1_, bf16[2,256,512]{2,1,0:T(8,128)(2,1)} %get-tuple-element.78.refs_2_, ...), custom_call_target="tpu_custom_call" | custom-call | flops 8000000000 | bytes 1 | tf_op jit(solution)/shard_map/head_weights/pallas_call | solution.py:64
  139.7 1.5 collective-permute-start.31
  141.3 4.8 %tail_back.1 = (bf16[1,512,1024]{2,1,0:T(8,128)(2,1)}, bf16[1,512,512]{2,1,0:T(8,128)(2,1)}, bf16[1,512,256]{2,1,0:T(8,128)(2,1)}, bf16[1,512,128]{2,1,0:T(8,128)(2,1)}, bf16[8,64,512]{2,1,0:T(8,128)(2,1)}) custom-call(s32[3]{0:T(128)} %pad_add_fusion.scal, bf16[128,1920]{1,0:T(8,128)(2,1)} %add.39.refs_24_.refs_0_, ...), custom_call_target="tpu_custom_call" | custom-call | flops 3000000000 | bytes 1 | tf_op jit(solution)/shard_map/tail_back/pallas_call | solution.py:64
  146.2 5.4 %all-to-all-start.1 = ((bf16[8,64,512]{2,1,0:T(8,128)(2,1)}), bf16[8,64,512]{2,1,0:T(8,128)(2,1)}, u32[]{:S(2)}, u32[]{:S(2)}) async-start(bf16[8,64,512]{2,1,0:T(8,128)(2,1)} %get-tuple-element.86.refs_10_), calls=%async_computation.1 | async-start | bytes 1048576 | tf_op jit(solution)/shard_map/all_to_all | solution.py:679
  151.5 6.5 %head_weights.3 = (bf16[256,640]{1,0:T(8,128)(2,1)}, bf16[256,640]{1,0:T(8,128)(2,1)}) custom-call(s32[3]{0:T(128)} %pad_add_fusion.scal, bf16[2,256,512]{2,1,0:T(8,128)(2,1)} %get-tuple-element.76.refs_0_, bf16[2,256,1024]{2,1,0:T(8,128)(2,1)} %get-tuple-element.77.refs_1_, bf16[2,256,512]{2,1,0:T(8,128)(2,1)} %get-tuple-element.78.refs_2_, ...), custom_call_target="tpu_custom_call" | custom-call | flops 8000000000 | bytes 1 | tf_op jit(solution)/shard_map/head_weights/pallas_call | solution.py:64
  158.0 2.0 %collective-permute-start.32 = (bf16[256,640]{1,0:T(8,128)(2,1)}, bf16[256,640]{1,0:T(8,128)(2,1)}, u32[]{:S(2)}, u32[]{:S(2)}) collective-permute-start(bf16[256,640]{1,0:T(8,128)(2,1)} %get-tuple-element.89.refs_5_), channel_id=1, source_target_pairs={{0,4},{4,0},{8,12},{12,8},{16,20},{20,16},{24,28},{28,24},{1,5},{5... | collective-permute-start | bytes 983048 | tf_op jit(solution)/shard_map/ppermute | solution.py:775
  160.1 4.6 %collective-permute-done.31 = bf16[256,1536]{1,0:T(8,128)(2,1)} collective-permute-done((bf16[256,1536]{1,0:T(8,128)(2,1)}, bf16[256,1536]{1,0:T(8,128)(2,1)}, u32[]{:S(2)}, u32[]{:S(2)}) %collective-permute-start.31) | collective-permute-done | bytes 786464 | tf_op jit(solution)/shard_map/ppermute | solution.py:775
  164.7 2.4 %add_convert_fusion = bf16[256,1536]{1,0:T(8,128)(2,1)} fusion(bf16[256,1536]{1,0:T(8,128)(2,1)} %collective-permute-done.31, bf16[256,1536]{1,0:T(8,128)(2,1)} %get-tuple-element.90), kind=kLoop, calls=%fused_computation | loop fusion | flops 1572864 | bytes 2359296 | tf_op jit(solution)/shard_map/convert_element_type | solution.py:779
  167.1 3.6 %grad_hidden.1.refs_2_ = bf16[512,512]{1,0:T(8,128)(2,1)} custom-call(s32[3]{0:T(128)} %pad_add_fusion.scal, bf16[512,512]{1,0:T(8,128)(2,1)} %get-tuple-element.57.refs_0_, bf16[512,512]{1,0:T(8,128)(2,1)} %bitcast.13.refs_1_, bf16[2,512,512]{2,1,0:T(8,128)(2,1)} %get-tuple-element.66.refs_2_.refs_0_, ...), custom_call_target="tpu_custom_call" | custom-call | flops 2000000000 | bytes 1 | tf_op jit(solution)/shard_map/grad_hidden/pallas_call | solution.py:64
  170.7 1.7 collective-permute-done.32.refs_1_
  172.4 1.2 add_convert_fusion.1
  173.6 0.7 copy.43
  174.3 1.1 pad_maximum_fusion
  (61 shorter events, 1.0 us)
Async XLA Ops:
  2.5 18.7 %collective-permute-start = (bf16[128,2048]{1,0:T(8,128)(2,1)}, bf16[128,2048]{1,0:T(8,128)(2,1)}, u32[]{:S(2)}, u32[]{:S(2)}) collective-permute-start(bf16[128,2048]{1,0:T(8,128)(2,1)} %constant_dynamic-slice_fusion), channel_id=1, source_target_pairs={{0,8},{4,12},{8,16},{12,20},{16,24},{20,28},{24,0},{28,4},{1,9},{5... | collective-permute-start | bytes 1572872 | tf_op jit(solution)/shard_map/ppermute | solution.py:517
  7.6 12.0 %collective-permute-start.3 = (f32[8,512]{1,0:T(8,128)}, f32[8,512]{1,0:T(8,128)}, u32[]{:S(2)}, u32[]{:S(2)}) collective-permute-start(f32[8,512]{1,0:T(8,128)} %select_convert_fusion.ids_ref.refs_3_.refs_9_), channel_id=1, source_target_pairs={{0,24},{4,28},{8,0},{12,4},{16,8},{20,12},{24,16},{28,20},{1,25},{... | collective-permute-start | bytes 49160 | tf_op jit(solution)/shard_map/ppermute | solution.py:504
  9.6 11.6 %collective-permute-start.2 = (f32[8,512]{1,0:T(8,128)}, f32[8,512]{1,0:T(8,128)}, u32[]{:S(2)}, u32[]{:S(2)}) collective-permute-start(f32[8,512]{1,0:T(8,128)} %select_convert_fusion.ids_ref.refs_3_.refs_9_), channel_id=1, source_target_pairs={{0,16},{4,20},{8,24},{12,28},{16,0},{20,4},{24,8},{28,12},{1,17},{... | collective-permute-start | bytes 49160 | tf_op jit(solution)/shard_map/ppermute | solution.py:504
  10.7 10.6 %collective-permute-start.1 = (f32[8,512]{1,0:T(8,128)}, f32[8,512]{1,0:T(8,128)}, u32[]{:S(2)}, u32[]{:S(2)}) collective-permute-start(f32[8,512]{1,0:T(8,128)} %select_convert_fusion.ids_ref.refs_3_.refs_9_), channel_id=1, source_target_pairs={{0,8},{4,12},{8,16},{12,20},{16,24},{20,28},{24,0},{28,4},{1,9},{5... | collective-permute-start | bytes 49160 | tf_op jit(solution)/shard_map/ppermute | solution.py:504
  21.2 15.6 %collective-permute-start.5 = (bf16[128,2048]{1,0:T(8,128)(2,1)}, bf16[128,2048]{1,0:T(8,128)(2,1)}, u32[]{:S(2)}, u32[]{:S(2)}) collective-permute-start(bf16[128,2048]{1,0:T(8,128)(2,1)} %hold.11.refs_3_.refs_0_), channel_id=1, source_target_pairs={{0,2},{1,3},{2,0},{3,1},{4,6},{5,7},{6,4},{7,5},{8,10},{9,11},{10,... | collective-permute-start | bytes 1572872 | tf_op jit(solution)/shard_map/ppermute | solution.py:21
  22.8 15.7 %collective-permute-start.4 = (bf16[128,2048]{1,0:T(8,128)(2,1)}, bf16[128,2048]{1,0:T(8,128)(2,1)}, u32[]{:S(2)}, u32[]{:S(2)}) collective-permute-start(bf16[128,2048]{1,0:T(8,128)(2,1)} %hold.11.refs_3_.refs_0_), channel_id=1, source_target_pairs={{0,8},{4,12},{8,16},{12,20},{16,24},{20,28},{24,0},{28,4},{1,9},{5... | collective-permute-start | bytes 1572872 | tf_op jit(solution)/shard_map/ppermute | solution.py:531
  35.0 3.5 %collective-permute-start.13 = (f32[8,512]{1,0:T(8,128)}, f32[8,512]{1,0:T(8,128)}, u32[]{:S(2)}, u32[]{:S(2)}) collective-permute-start(f32[8,512]{1,0:T(8,128)} %get-tuple-element.60.refs_2_.refs_4_.refs_12_), channel_id=1, source_target_pairs={{0,3},{1,2},{2,1},{3,0},{4,7},{5,6},{6,5},{7,4},{8,11},{9,10},{10,... | collective-permute-start | bytes 49160 | tf_op jit(solution)/shard_map/ppermute | solution.py:21
  35.0 4.1 %collective-permute-start.12 = (f32[8,512]{1,0:T(8,128)}, f32[8,512]{1,0:T(8,128)}, u32[]{:S(2)}, u32[]{:S(2)}) collective-permute-start(f32[8,512]{1,0:T(8,128)} %get-tuple-element.60.refs_2_.refs_4_.refs_12_), channel_id=1, source_target_pairs={{0,2},{1,3},{2,0},{3,1},{4,6},{5,7},{6,4},{7,5},{8,10},{9,11},{10,... | collective-permute-start | bytes 49160 | tf_op jit(solution)/shard_map/ppermute | solution.py:21
  36.0 4.0 %collective-permute-start.11 = (f32[8,512]{1,0:T(8,128)}, f32[8,512]{1,0:T(8,128)}, u32[]{:S(2)}, u32[]{:S(2)}) collective-permute-start(f32[8,512]{1,0:T(8,128)} %get-tuple-element.60.refs_2_.refs_4_.refs_12_), channel_id=1, source_target_pairs={{0,1},{1,0},{2,3},{3,2},{4,5},{5,4},{6,7},{7,6},{8,9},{9,8},{10,11... | collective-permute-start | bytes 49160 | tf_op jit(solution)/shard_map/ppermute | solution.py:21
  36.9 23.3 %collective-permute-start.6 = (bf16[128,2048]{1,0:T(8,128)(2,1)}, bf16[128,2048]{1,0:T(8,128)(2,1)}, u32[]{:S(2)}, u32[]{:S(2)}) collective-permute-start(bf16[128,2048]{1,0:T(8,128)(2,1)} %hold.11.refs_3_.refs_0_), channel_id=1, source_target_pairs={{0,1},{1,0},{2,3},{3,2},{4,5},{5,4},{6,7},{7,6},{8,9},{9,8},{10,11... | collective-permute-start | bytes 1572872 | tf_op jit(solution)/shard_map/ppermute | solution.py:21
  38.5 23.2 %collective-permute-start.7 = (bf16[128,2048]{1,0:T(8,128)(2,1)}, bf16[128,2048]{1,0:T(8,128)(2,1)}, u32[]{:S(2)}, u32[]{:S(2)}) collective-permute-start(bf16[128,2048]{1,0:T(8,128)(2,1)} %get-tuple-element.61.refs_1_.refs_2_), channel_id=1, source_target_pairs={{0,1},{1,0},{2,3},{3,2},{4,5},{5,4},{6,7},{7,6},{8,9},{9,8},{10,11... | collective-permute-start | bytes 1572872 | tf_op jit(solution)/shard_map/ppermute | solution.py:21
  38.5 14.7 %collective-permute-start.10 = (bf16[128,2048]{1,0:T(8,128)(2,1)}, bf16[128,2048]{1,0:T(8,128)(2,1)}, u32[]{:S(2)}, u32[]{:S(2)}) collective-permute-start(bf16[128,2048]{1,0:T(8,128)(2,1)} %get-tuple-element.62.refs_4_), channel_id=1, source_target_pairs={{0,2},{1,3},{2,0},{3,1},{4,6},{5,7},{6,4},{7,5},{8,10},{9,11},{10,... | collective-permute-start | bytes 1572872 | tf_op jit(solution)/shard_map/ppermute | solution.py:21
  39.1 16.1 %collective-permute-start.9 = (bf16[128,2048]{1,0:T(8,128)(2,1)}, bf16[128,2048]{1,0:T(8,128)(2,1)}, u32[]{:S(2)}, u32[]{:S(2)}) collective-permute-start(bf16[128,2048]{1,0:T(8,128)(2,1)} %get-tuple-element.62.refs_4_), channel_id=1, source_target_pairs={{0,8},{4,12},{8,16},{12,20},{16,24},{20,28},{24,0},{28,4},{1,9},{5... | collective-permute-start | bytes 1572872 | tf_op jit(solution)/shard_map/ppermute | solution.py:531
  40.0 21.7 %collective-permute-start.8 = (bf16[128,2048]{1,0:T(8,128)(2,1)}, bf16[128,2048]{1,0:T(8,128)(2,1)}, u32[]{:S(2)}, u32[]{:S(2)}) collective-permute-start(bf16[128,2048]{1,0:T(8,128)(2,1)} %get-tuple-element.62.refs_4_), channel_id=1, source_target_pairs={{0,1},{1,0},{2,3},{3,2},{4,5},{5,4},{6,7},{7,6},{8,9},{9,8},{10,11... | collective-permute-start | bytes 1572872 | tf_op jit(solution)/shard_map/ppermute | solution.py:21
  55.2 6.5 %collective-permute-start.14 = (bf16[128,2048]{1,0:T(8,128)(2,1)}, bf16[128,2048]{1,0:T(8,128)(2,1)}, u32[]{:S(2)}, u32[]{:S(2)}) collective-permute-start(bf16[128,2048]{1,0:T(8,128)(2,1)} %get-tuple-element.67.refs_6_.refs_10_), channel_id=1, source_target_pairs={{0,1},{1,0},{2,3},{3,2},{4,5},{5,4},{6,7},{7,6},{8,9},{9,8},{10,11... | collective-permute-start | bytes 1572872 | tf_op jit(solution)/shard_map/ppermute | solution.py:21
  55.2 24.8 %all-to-all-start = ((bf16[8,64,640]{2,1,0:T(8,128)(2,1)}), bf16[8,64,640]{2,1,0:T(8,128)(2,1)}, u32[]{:S(2)}, u32[]{:S(2)}) async-start(bf16[8,64,640]{2,1,0:T(8,128)(2,1)} %bitcast.4), calls=%async_computation | async-start | bytes 1310720 | tf_op jit(solution)/shard_map/all_to_all | solution.py:610
  59.6 24.3 %collective-permute-start.20 = (bf16[2,512,512]{2,1,0:T(8,128)(2,1)}, bf16[2,512,512]{2,1,0:T(8,128)(2,1)}, u32[]{:S(2)}, u32[]{:S(2)}) collective-permute-start(bf16[2,512,512]{2,1,0:T(8,128)(2,1)} %get-tuple-element.70), channel_id=1, source_target_pairs={{0,1},{1,0},{2,3},{3,2},{4,5},{5,4},{6,7},{7,6},{8,9},{9,8},{10,11... | collective-permute-start | bytes 3145736 | tf_op jit(solution)/shard_map/ppermute | solution.py:21
  60.2 22.7 %collective-permute-start.18 = (bf16[128,2048]{1,0:T(8,128)(2,1)}, bf16[128,2048]{1,0:T(8,128)(2,1)}, u32[]{:S(2)}, u32[]{:S(2)}) collective-permute-start(bf16[128,2048]{1,0:T(8,128)(2,1)} %get-tuple-element.69.refs_0_), channel_id=1, source_target_pairs={{0,2},{1,3},{2,0},{3,1},{4,6},{5,7},{6,4},{7,5},{8,10},{9,11},{10,... | collective-permute-start | bytes 1572872 | tf_op jit(solution)/shard_map/ppermute | solution.py:21
  61.7 24.7 %collective-permute-start.17 = (bf16[128,2048]{1,0:T(8,128)(2,1)}, bf16[128,2048]{1,0:T(8,128)(2,1)}, u32[]{:S(2)}, u32[]{:S(2)}) collective-permute-start(bf16[128,2048]{1,0:T(8,128)(2,1)} %get-tuple-element.69.refs_0_), channel_id=1, source_target_pairs={{0,1},{1,0},{2,3},{3,2},{4,5},{5,4},{6,7},{7,6},{8,9},{9,8},{10,11... | collective-permute-start | bytes 1572872 | tf_op jit(solution)/shard_map/ppermute | solution.py:21
  81.2 0.9 copy-start.6
  81.2 2.7 %copy-start = (bf16[2,512,512]{2,1,0:T(8,128)(2,1)S(1)}, bf16[2,512,512]{2,1,0:T(8,128)(2,1)}, u32[]{:S(2)}) copy-start(bf16[2,512,512]{2,1,0:T(8,128)(2,1)} %get-tuple-element.66.refs_2_.refs_0_) | copy-start | bytes 3145732
  81.2 2.7 %copy-start.1 = (s32[3]{0:T(128)S(1)}, s32[3]{0:T(128)}, u32[]{:S(2)}) copy-start(s32[3]{0:T(128)} %pad_add_fusion.scal) | copy-start | bytes 40
  82.9 3.5 %collective-permute-start.19 = (bf16[128,2048]{1,0:T(8,128)(2,1)}, bf16[128,2048]{1,0:T(8,128)(2,1)}, u32[]{:S(2)}, u32[]{:S(2)}) collective-permute-start(bf16[128,2048]{1,0:T(8,128)(2,1)} %hold.16.refs_2_), channel_id=1, source_target_pairs={{0,1},{1,0},{2,3},{3,2},{4,5},{5,4},{6,7},{7,6},{8,9},{9,8},{10,11... | collective-permute-start | bytes 1572872 | tf_op jit(solution)/shard_map/ppermute | solution.py:21
  83.4 15.1 %collective-permute-start.16 = (bf16[4,128,512]{2,1,0:T(8,128)(2,1)}, bf16[4,128,512]{2,1,0:T(8,128)(2,1)}, u32[]{:S(2)}, u32[]{:S(2)}) collective-permute-start(bf16[4,128,512]{2,1,0:T(8,128)(2,1)} %hold.15.refs_1_.refs_0_.refs_2_), channel_id=1, source_target_pairs={{0,2},{1,3},{2,0},{3,1},{4,6},{5,7},{6,4},{7,5},{8,10},{9,11},{10,... | collective-permute-start | bytes 1572872 | tf_op jit(solution)/shard_map/ppermute | solution.py:21
  83.9 16.7 %collective-permute-start.15 = (bf16[4,128,512]{2,1,0:T(8,128)(2,1)}, bf16[4,128,512]{2,1,0:T(8,128)(2,1)}, u32[]{:S(2)}, u32[]{:S(2)}) collective-permute-start(bf16[4,128,512]{2,1,0:T(8,128)(2,1)} %hold.15.refs_1_.refs_0_.refs_2_), channel_id=1, source_target_pairs={{0,1},{1,0},{2,3},{3,2},{4,5},{5,4},{6,7},{7,6},{8,9},{9,8},{10,11... | collective-permute-start | bytes 1572872 | tf_op jit(solution)/shard_map/ppermute | solution.py:21
  85.6 0.8 copy-start.4
  98.5 2.5 %collective-permute-start.21 = (bf16[4,128,512]{2,1,0:T(8,128)(2,1)}, bf16[4,128,512]{2,1,0:T(8,128)(2,1)}, u32[]{:S(2)}, u32[]{:S(2)}) collective-permute-start(bf16[4,128,512]{2,1,0:T(8,128)(2,1)} %hold.17.refs_2_.refs_12_), channel_id=1, source_target_pairs={{0,1},{1,0},{2,3},{3,2},{4,5},{5,4},{6,7},{7,6},{8,9},{9,8},{10,11... | collective-permute-start | bytes 1572872 | tf_op jit(solution)/shard_map/ppermute | solution.py:21
  99.1 14.4 %collective-permute-start.25 = (bf16[512,512]{1,0:T(8,128)(2,1)}, bf16[512,512]{1,0:T(8,128)(2,1)}, u32[]{:S(2)}, u32[]{:S(2)}) collective-permute-start(bf16[512,512]{1,0:T(8,128)(2,1)} %copy-done.4), channel_id=1, source_target_pairs={{0,2},{1,3},{2,0},{3,1},{4,6},{5,7},{6,4},{7,5},{8,10},{9,11},{10,... | collective-permute-start | bytes 1572872 | tf_op jit(solution)/shard_map/ppermute | solution.py:21
  109.5 4.0 %collective-permute-start.24 = (f32[8,512]{1,0:T(8,128)}, f32[8,512]{1,0:T(8,128)}, u32[]{:S(2)}, u32[]{:S(2)}) collective-permute-start(f32[8,512]{1,0:T(8,128)} %get-tuple-element.74.refs_1_.refs_3_), channel_id=1, source_target_pairs={{0,3},{1,2},{2,1},{3,0},{4,7},{5,6},{6,5},{7,4},{8,11},{9,10},{10,... | collective-permute-start | bytes 49160 | tf_op jit(solution)/shard_map/ppermute | solution.py:21
  111.1 4.1 %collective-permute-start.23 = (f32[8,512]{1,0:T(8,128)}, f32[8,512]{1,0:T(8,128)}, u32[]{:S(2)}, u32[]{:S(2)}) collective-permute-start(f32[8,512]{1,0:T(8,128)} %get-tuple-element.74.refs_1_.refs_3_), channel_id=1, source_target_pairs={{0,2},{1,3},{2,0},{3,1},{4,6},{5,7},{6,4},{7,5},{8,10},{9,11},{10,... | collective-permute-start | bytes 49160 | tf_op jit(solution)/shard_map/ppermute | solution.py:21
  111.6 3.6 %collective-permute-start.22 = (f32[8,512]{1,0:T(8,128)}, f32[8,512]{1,0:T(8,128)}, u32[]{:S(2)}, u32[]{:S(2)}) collective-permute-start(f32[8,512]{1,0:T(8,128)} %get-tuple-element.74.refs_1_.refs_3_), channel_id=1, source_target_pairs={{0,1},{1,0},{2,3},{3,2},{4,5},{5,4},{6,7},{7,6},{8,9},{9,8},{10,11... | collective-permute-start | bytes 49160 | tf_op jit(solution)/shard_map/ppermute | solution.py:21
  120.6 3.5 %collective-permute-start.26 = (f32[128,1920]{1,0:T(8,128)}, f32[128,1920]{1,0:T(8,128)S(1)}, u32[]{:S(2)}, u32[]{:S(2)}) collective-permute-start(f32[128,1920]{1,0:T(8,128)} %get-tuple-element.75.refs_0_.refs_2_), channel_id=1, source_target_pairs={{0,1},{1,0},{2,3},{3,2},{4,5},{5,4},{6,7},{7,6},{8,9},{9,8},{10,11... | collective-permute-start | bytes 2949128 | tf_op jit(solution)/shard_map/ppermute | solution.py:21
  122.0 5.9 %collective-permute-start.30 = (f32[8,1536]{1,0:T(8,128)}, f32[8,1536]{1,0:T(8,128)}, u32[]{:S(2)}, u32[]{:S(2)}) collective-permute-start(f32[8,1536]{1,0:T(8,128)} %get-tuple-element.71.refs_1_.refs_16_.refs_20_), channel_id=1, source_target_pairs={{0,3},{1,2},{2,1},{3,0},{4,7},{5,6},{6,5},{7,4},{8,11},{9,10},{10,... | collective-permute-start | bytes 147464 | tf_op jit(solution)/shard_map/ppermute | solution.py:21
  122.6 5.3 %collective-permute-start.29 = (f32[8,1536]{1,0:T(8,128)}, f32[8,1536]{1,0:T(8,128)}, u32[]{:S(2)}, u32[]{:S(2)}) collective-permute-start(f32[8,1536]{1,0:T(8,128)} %get-tuple-element.71.refs_1_.refs_16_.refs_20_), channel_id=1, source_target_pairs={{0,2},{1,3},{2,0},{3,1},{4,6},{5,7},{6,4},{7,5},{8,10},{9,11},{10,... | collective-permute-start | bytes 147464 | tf_op jit(solution)/shard_map/ppermute | solution.py:21
  124.1 3.8 %collective-permute-start.28 = (f32[8,1536]{1,0:T(8,128)}, f32[8,1536]{1,0:T(8,128)}, u32[]{:S(2)}, u32[]{:S(2)}) collective-permute-start(f32[8,1536]{1,0:T(8,128)} %get-tuple-element.71.refs_1_.refs_16_.refs_20_), channel_id=1, source_target_pairs={{0,1},{1,0},{2,3},{3,2},{4,5},{5,4},{6,7},{7,6},{8,9},{9,8},{10,11... | collective-permute-start | bytes 147464 | tf_op jit(solution)/shard_map/ppermute | solution.py:21
  124.1 0.7 copy-start.2
  124.8 1.2 copy-start.3
  127.4 13.9 %collective-permute-start.27 = (bf16[128,1920]{1,0:T(8,128)(2,1)}, bf16[128,1920]{1,0:T(8,128)(2,1)}, u32[]{:S(2)}, u32[]{:S(2)}) collective-permute-start(bf16[128,1920]{1,0:T(8,128)(2,1)} %add.39.refs_24_.refs_0_), channel_id=1, source_target_pairs={{0,2},{1,3},{2,0},{3,1},{4,6},{5,7},{6,4},{7,5},{8,10},{9,11},{10,... | collective-permute-start | bytes 1474568 | tf_op jit(solution)/shard_map/ppermute | solution.py:21
  139.7 25.0 %collective-permute-start.31 = (bf16[256,1536]{1,0:T(8,128)(2,1)}, bf16[256,1536]{1,0:T(8,128)(2,1)}, u32[]{:S(2)}, u32[]{:S(2)}) collective-permute-start(bf16[256,1536]{1,0:T(8,128)(2,1)} %get-tuple-element.91), channel_id=1, source_target_pairs={{0,4},{4,0},{8,12},{12,8},{16,20},{20,16},{24,28},{28,24},{1,5},{5... | collective-permute-start | bytes 2359304 | tf_op jit(solution)/shard_map/ppermute | solution.py:775
  146.2 21.0 %all-to-all-start.1 = ((bf16[8,64,512]{2,1,0:T(8,128)(2,1)}), bf16[8,64,512]{2,1,0:T(8,128)(2,1)}, u32[]{:S(2)}, u32[]{:S(2)}) async-start(bf16[8,64,512]{2,1,0:T(8,128)(2,1)} %get-tuple-element.86.refs_10_), calls=%async_computation.1 | async-start | bytes 1048576 | tf_op jit(solution)/shard_map/all_to_all | solution.py:679
  158.0 14.4 %collective-permute-start.32 = (bf16[256,640]{1,0:T(8,128)(2,1)}, bf16[256,640]{1,0:T(8,128)(2,1)}, u32[]{:S(2)}, u32[]{:S(2)}) collective-permute-start(bf16[256,640]{1,0:T(8,128)(2,1)} %get-tuple-element.89.refs_5_), channel_id=1, source_target_pairs={{0,4},{4,0},{8,12},{12,8},{16,20},{20,16},{24,28},{28,24},{1,5},{5... | collective-permute-start | bytes 983048 | tf_op jit(solution)/shard_map/ppermute | solution.py:775
  170.7 3.6 %copy-start.5 = (bf16[256,1536]{1,0:T(8,128)(2,1)S(1)}, bf16[256,1536]{1,0:T(8,128)(2,1)}, u32[]{:S(2)}) copy-start(bf16[256,1536]{1,0:T(8,128)(2,1)} %add_convert_fusion) | copy-start | bytes 2359300

commit v4 on v3

--- a/solution.py
+++ b/solution.py
@@ -741,7 +741,7 @@
         in_specs = [whole(t) for t in turned]
         in_specs += [pl.BlockSpec((size, block), lambda i, s: (0, i + first)) for size in sizes]
         if columns is None:
-            others = line_ids()
+            others = other_ids
             extra = [*stats, ids]
             in_specs += [whole(v) for v in extra]
             lanes = []
@@ -787,6 +787,7 @@
 
     dispatch, send = tail_rows()
     moved_ids = order.hold(*moved_ids)
+    (other_ids,) = order.hold(line_ids())
     move_rows(1)
     early = head_group(0)
     early = [early] + shared(early)

time: 177 us -> 180 us (1.017)
  waiting for transfers between devices: 17.5 us -> 20.3 us
    ppermute x1, waiting for transfers between devices: 0.01 us -> 4.2 us  [body(): from_line = {1: lax.ppermute(piece, 'vocab', ring)}]
    ppermute x3, waiting for transfers between devices: 2.06 us -> 0.01 us  [body(): lax.ppermute(ids, 'vocab', [(i, (i + step * near) % groups) for i in rang...]
  transfers between devices with their start and end apart: 35 -> 35, of which waited for: 11 -> 11; matrix products, arithmetic and copies ran while one was open for 6% -> 6% of each run, Pallas kernels for 55% -> 54%
where the time goes in v4:
time: 180 us; the launch traced here: 178 us
  Pallas kernels  102 us (57%)
  starting transfers between devices  36.5 us (20%)
  waiting for transfers between devices  20.3 us (11%)
  local copies, waits for them, and re-layouts  9.89 us (5%)
  other arithmetic  8.71 us (5%)
    pallas_call x13, Pallas kernels, kernel_call(): pl.pallas_call(kernel, name=name, out_shape=outs, grid_spec=pltpu.Prefetc...  102 us
    ppermute x25, starting transfers between devices, tp_swap(): return lax.ppermute(value, 'tp', xor_pairs(lax.axis_size('tp'), step))  14.4 us
    ppermute x2, waiting for transfers between devices, near_parts(): parts.append(lax.ppermute(part, 'vocab', xor_pairs(groups, step)))  6.7 us
    ppermute x25, waiting for transfers between devices, tp_swap(): return lax.ppermute(value, 'tp', xor_pairs(lax.axis_size('tp'), step))  6.11 us
    ppermute x3, starting transfers between devices, body(): lax.ppermute(ids, 'vocab', [(i, (i + step * near) % groups) for i in rang...  6.06 us
    unnamed x16, local copies, waits for them, and re-layouts  5.11 us
    all_to_all x1, starting transfers between devices, tail_return(): lax.all_to_all(back.reshape(groups, 4 * capacity, own_width), 'vocab', sp...  4.73 us
    all_to_all x1, starting transfers between devices, tail_send(): lax.all_to_all(send.reshape(groups, 4 * capacity, own_width + LANES), 'vo...  4.39 us
  transfers between devices with their start and end apart: 35, of which 11 were waited for; matrix products, arithmetic and copies ran while one was open for 6% of the time, Pallas kernels for 54%

profile of v4, /device:TPU:0, one launch (start us, length us, event | category | flops | bytes accessed | tf_op | source)
XLA Modules:
  0.0 178.5 jit_solution(4510131468673091825)
XLA Ops:
  0.7 0.7 compare_select_fusion.1
  1.4 1.4 select_convert_fusion.ids_ref.refs_3_.refs_9_
  2.7 5.0 %collective-permute-start.3 = (f32[8,512]{1,0:T(8,128)}, f32[8,512]{1,0:T(8,128)}, u32[]{:S(2)}, u32[]{:S(2)}) collective-permute-start(f32[8,512]{1,0:T(8,128)} %select_convert_fusion.ids_ref.refs_3_.refs_9_), channel_id=1, source_target_pairs={{0,24},{4,28},{8,0},{12,4},{16,8},{20,12},{24,16},{28,20},{1,25},{... | collective-permute-start | bytes 49160 | tf_op jit(solution)/shard_map/ppermute | solution.py:504
  7.8 1.0 collective-permute-start.1
  8.8 1.9 %constant_dynamic-slice_fusion = bf16[128,2048]{1,0:T(8,128)(2,1)} fusion(bf16[512,2048]{1,0:T(8,128)(2,1)} %refs_0_.1, s32[]{:T(128)S(6)} %select_n.70), kind=kLoop, calls=%fused_computation.13 | loop fusion | bytes 1048580 | tf_op jit(solution)/shard_map/dynamic_slice | solution.py:516
  10.7 2.5 %collective-permute-start = (bf16[128,2048]{1,0:T(8,128)(2,1)}, bf16[128,2048]{1,0:T(8,128)(2,1)}, u32[]{:S(2)}, u32[]{:S(2)}) collective-permute-start(bf16[128,2048]{1,0:T(8,128)(2,1)} %constant_dynamic-slice_fusion), channel_id=1, source_target_pairs={{0,8},{4,12},{8,16},{12,20},{16,24},{20,28},{24,0},{28,4},{1,9},{5... | collective-permute-start | bytes 1572872 | tf_op jit(solution)/shard_map/ppermute | solution.py:517
  13.1 0.6 pad_add_fusion.scal
  13.7 4.4 %send_rows.1 = (bf16[512,512]{1,0:T(8,128)(2,1)}, bf16[512,640]{1,0:T(8,128)(2,1)}) custom-call(s32[3]{0:T(128)} %pad_add_fusion.scal, f32[8,512]{1,0:T(8,128)} %select_convert_fusion.ids_ref.refs_3_.refs_9_, bf16[512,2048]{1,0:T(8,128)(2,1)} %refs_0_.1), custom_call_target="tpu_custom_call" | custom-call | flops 3000000000 | bytes 1 | tf_op jit(solution)/shard_map/send_rows/pallas_call | solution.py:64
  18.0 1.0 copy.42
  19.1 0.9 pad.4.refs_2_.refs_9_.refs_6_
  20.0 0.8 pad_maximum_fusion.1
  20.8 0.6 reverse_select_fusion
  21.4 4.2 %collective-permute-done.refs_0_ = bf16[128,2048]{1,0:T(8,128)(2,1)} collective-permute-done((bf16[128,2048]{1,0:T(8,128)(2,1)}, bf16[128,2048]{1,0:T(8,128)(2,1)}, u32[]{:S(2)}, u32[]{:S(2)}) %collective-permute-start) | collective-permute-done | bytes 524320 | tf_op jit(solution)/shard_map/ppermute | solution.py:517
  25.6 1.5 collective-permute-start.5
  27.1 0.7 collective-permute-start.4
  27.8 11.8 %head_logits.1 = (bf16[512,2048]{1,0:T(8,128)(2,1)}, bf16[512,128]{1,0:T(8,128)(2,1)}, f32[512,128]{1,0:T(8,128)}, bf16[2,256,512]{2,1,0:T(8,128)(2,1)}, f32[8,512]{1,0:T(8,128)}) custom-call(s32[3]{0:T(128)} %pad_add_fusion.scal, bf16[512,2048]{1,0:T(8,128)(2,1)} %refs_0_.1, bf16[2048,2048]{1,0:T(8,128)(2,1)} %refs_5_.3, ...), custom_call_target="tpu_custom_call" | custom-call | flops 8999999488 | bytes 1 | tf_op jit(solution)/shard_map/head_logits/pallas_call | solution.py:64
  39.7 0.6 collective-permute-start.12
  40.2 1.3 collective-permute-start.11
  41.5 0.5 collective-permute-start.7
  42.0 1.1 collective-permute-done.13.refs_7_.refs_15_
  43.1 0.6 collective-permute-start.10
  44.1 11.8 %head_back.1 = (bf16[2,512,512]{2,1,0:T(8,128)(2,1)}, bf16[2,512,512]{2,1,0:T(8,128)(2,1)}) custom-call(s32[3]{0:T(128)} %pad_add_fusion.scal, bf16[512,2048]{1,0:T(8,128)(2,1)} %get-tuple-element.65.refs_0_.refs_3_, bf16[512,128]{1,0:T(8,128)(2,1)} %get-tuple-element.66.refs_1_.refs_7_, f32[512,128]{1,0:T(8,128)} %get-tuple-element.67.refs_2_.refs_6_, ...), custom_call_target="tpu_custom_call" | custom-call | flops 8999999488 | bytes 1 | tf_op jit(solution)/shard_map/head_back/pallas_call | solution.py:64
  56.3 3.2 %collective-permute-done.9.refs_0_ = bf16[128,2048]{1,0:T(8,128)(2,1)} collective-permute-done((bf16[128,2048]{1,0:T(8,128)(2,1)}, bf16[128,2048]{1,0:T(8,128)(2,1)}, u32[]{:S(2)}, u32[]{:S(2)}) %collective-permute-start.9) | collective-permute-done | bytes 524320 | tf_op jit(solution)/shard_map/ppermute | solution.py:531
  59.5 4.4 %all-to-all-start = ((bf16[8,64,640]{2,1,0:T(8,128)(2,1)}), bf16[8,64,640]{2,1,0:T(8,128)(2,1)}, u32[]{:S(2)}, u32[]{:S(2)}) async-start(bf16[8,64,640]{2,1,0:T(8,128)(2,1)} %bitcast.9), calls=%async_computation | async-start | bytes 1310720 | tf_op jit(solution)/shard_map/all_to_all | solution.py:610
  63.9 0.6 collective-permute-start.20
  64.5 1.1 collective-permute-start.18
  65.6 18.3 %line_logits.2 = (bf16[1024,2048]{1,0:T(8,128)(2,1)}, bf16[1024,128]{1,0:T(8,128)(2,1)}, f32[1024,128]{1,0:T(8,128)}, bf16[2,256,1024]{2,1,0:T(8,128)(2,1)}, f32[8,1024]{1,0:T(8,128)}) custom-call(s32[3]{0:T(128)} %pad_add_fusion.scal, bf16[128,2048]{1,0:T(8,128)(2,1)} %hold.13.refs_3_.refs_0_, bf16[128,2048]{1,0:T(8,128)(2,1)} %collective-permute-done.6.refs_1_, ...), custom_call_target="tpu_custom_call" | custom-call | flops 20000000000 | bytes 1 | tf_op jit(solution)/shard_map/line_logits/pallas_call | solution.py:64
  84.0 1.1 copy.43
  85.1 0.8 copy-done.6
  86.0 0.8 slice.12.refs_0_
  86.8 0.5 collective-permute-start.19
  87.3 0.9 collective-permute-start.16
  88.2 1.7 add.38.refs_7_
  89.9 0.8 copy-done.4
  90.7 12.1 %line_logits.3 = (bf16[512,2048]{1,0:T(8,128)(2,1)}, bf16[512,128]{1,0:T(8,128)(2,1)}, f32[512,128]{1,0:T(8,128)}, bf16[2,256,512]{2,1,0:T(8,128)(2,1)}, f32[8,1536]{1,0:T(8,128)}) custom-call(s32[3]{0:T(128)} %pad_add_fusion.scal, bf16[128,2048]{1,0:T(8,128)(2,1)} %get-tuple-element.71.refs_0_, bf16[128,2048]{1,0:T(8,128)(2,1)} %collective-permute-done.17.refs_1_, ...), custom_call_target="tpu_custom_call" | custom-call | flops 20000000000 | bytes 1 | tf_op jit(solution)/shard_map/line_logits/pallas_call | solution.py:64
  102.8 0.6 collective-permute-start.21
  103.4 1.1 collective-permute-start.25
  104.5 0.8 collective-permute-done.21.refs_3_
  105.3 8.6 %tail_logits.1 = (bf16[128,1920]{1,0:T(8,128)(2,1)}, bf16[128,3840]{1,0:T(8,128)(2,1)}, f32[8,512]{1,0:T(8,128)}) custom-call(s32[3]{0:T(128)} %pad_add_fusion.scal, bf16[4,128,512]{2,1,0:T(8,128)(2,1)} %hold.17.refs_1_.refs_0_.refs_2_, bf16[4,128,512]{2,1,0:T(8,128)(2,1)} %collective-permute-done.15.refs_1_, bf16[4,128,512]{2,1,0:T(8,128)(2,1)} %hold.19.refs_2_.refs_12_, ...), custom_call_target="tpu_custom_call" | custom-call | flops 5000000000 | bytes 1 | tf_op jit(solution)/shard_map/tail_logits/pallas_call | solution.py:64
  113.8 1.2 collective-permute-start.24
  115.0 0.9 collective-permute-start.23
  115.9 1.9 %collective-permute-done.25.refs_0_ = bf16[512,512]{1,0:T(8,128)(2,1)} collective-permute-done((bf16[512,512]{1,0:T(8,128)(2,1)}, bf16[512,512]{1,0:T(8,128)(2,1)}, u32[]{:S(2)}, u32[]{:S(2)}) %collective-permute-start.25) | collective-permute-done | bytes 524320 | tf_op jit(solution)/shard_map/ppermute | solution.py:21
  117.8 1.3 collective-permute-done.23.refs_5_
  119.1 5.4 %tail_grads.1 = (bf16[1,1024,256]{2,1,0:T(8,128)(2,1)}, bf16[1,512,512]{2,1,0:T(8,128)(2,1)}, bf16[1,256,1024]{2,1,0:T(8,128)(2,1)}, bf16[1,128,2048]{2,1,0:T(8,128)(2,1)}, f32[128,1920]{1,0:T(8,128)}) custom-call(s32[3]{0:T(128)} %pad_add_fusion.scal, bf16[128,1920]{1,0:T(8,128)(2,1)} %get-tuple-element.74.refs_0_, ...), custom_call_target="tpu_custom_call" | custom-call | flops 3000000000 | bytes 1 | tf_op jit(solution)/shard_map/tail_grads/pallas_call | solution.py:64
  124.5 1.0 collective-permute-start.30
  125.5 1.1 collective-permute-start.29
  126.6 0.6 collective-permute-done.26.refs_1_
  127.3 0.6 copy-done.2
  127.8 1.2 copy-done.3
  129.0 1.4 add.39.refs_24_.refs_0_
  130.5 0.9 collective-permute-start.27
  131.4 11.8 %head_weights.2 = (bf16[256,1536]{1,0:T(8,128)(2,1)}, bf16[256,1536]{1,0:T(8,128)(2,1)}, f32[2048,128]{1,0:T(8,128)}) custom-call(s32[3]{0:T(128)} %pad_add_fusion.scal, bf16[2,256,512]{2,1,0:T(8,128)(2,1)} %get-tuple-element.78.refs_0_, bf16[2,256,1024]{2,1,0:T(8,128)(2,1)} %get-tuple-element.79.refs_1_, bf16[2,256,512]{2,1,0:T(8,128)(2,1)} %get-tuple-element.80.refs_2_, ...), custom_call_target="tpu_custom_call" | custom-call | flops 8000000000 | bytes 1 | tf_op jit(solution)/shard_map/head_weights/pallas_call | solution.py:64
  143.2 1.5 collective-permute-start.31
  144.7 4.8 %tail_back.1 = (bf16[1,512,1024]{2,1,0:T(8,128)(2,1)}, bf16[1,512,512]{2,1,0:T(8,128)(2,1)}, bf16[1,512,256]{2,1,0:T(8,128)(2,1)}, bf16[1,512,128]{2,1,0:T(8,128)(2,1)}, bf16[8,64,512]{2,1,0:T(8,128)(2,1)}) custom-call(s32[3]{0:T(128)} %pad_add_fusion.scal, bf16[128,1920]{1,0:T(8,128)(2,1)} %add.39.refs_24_.refs_0_, ...), custom_call_target="tpu_custom_call" | custom-call | flops 3000000000 | bytes 1 | tf_op jit(solution)/shard_map/tail_back/pallas_call | solution.py:64
  149.5 4.7 %all-to-all-start.1 = ((bf16[8,64,512]{2,1,0:T(8,128)(2,1)}), bf16[8,64,512]{2,1,0:T(8,128)(2,1)}, u32[]{:S(2)}, u32[]{:S(2)}) async-start(bf16[8,64,512]{2,1,0:T(8,128)(2,1)} %get-tuple-element.86.refs_10_), calls=%async_computation.1 | async-start | bytes 1048576 | tf_op jit(solution)/shard_map/all_to_all | solution.py:679
  154.2 6.5 %head_weights.3 = (bf16[256,640]{1,0:T(8,128)(2,1)}, bf16[256,640]{1,0:T(8,128)(2,1)}) custom-call(s32[3]{0:T(128)} %pad_add_fusion.scal, bf16[2,256,512]{2,1,0:T(8,128)(2,1)} %get-tuple-element.78.refs_0_, bf16[2,256,1024]{2,1,0:T(8,128)(2,1)} %get-tuple-element.79.refs_1_, bf16[2,256,512]{2,1,0:T(8,128)(2,1)} %get-tuple-element.80.refs_2_, ...), custom_call_target="tpu_custom_call" | custom-call | flops 8000000000 | bytes 1 | tf_op jit(solution)/shard_map/head_weights/pallas_call | solution.py:64
  160.7 2.0 %collective-permute-start.32 = (bf16[256,640]{1,0:T(8,128)(2,1)}, bf16[256,640]{1,0:T(8,128)(2,1)}, u32[]{:S(2)}, u32[]{:S(2)}) collective-permute-start(bf16[256,640]{1,0:T(8,128)(2,1)} %get-tuple-element.89.refs_5_), channel_id=1, source_target_pairs={{0,4},{4,0},{8,12},{12,8},{16,20},{20,16},{24,28},{28,24},{1,5},{5... | collective-permute-start | bytes 983048 | tf_op jit(solution)/shard_map/ppermute | solution.py:775
  162.8 5.4 %collective-permute-done.31 = bf16[256,1536]{1,0:T(8,128)(2,1)} collective-permute-done((bf16[256,1536]{1,0:T(8,128)(2,1)}, bf16[256,1536]{1,0:T(8,128)(2,1)}, u32[]{:S(2)}, u32[]{:S(2)}) %collective-permute-start.31) | collective-permute-done | bytes 786464 | tf_op jit(solution)/shard_map/ppermute | solution.py:775
  168.2 2.4 %add_convert_fusion = bf16[256,1536]{1,0:T(8,128)(2,1)} fusion(bf16[256,1536]{1,0:T(8,128)(2,1)} %collective-permute-done.31, bf16[256,1536]{1,0:T(8,128)(2,1)} %get-tuple-element.90), kind=kLoop, calls=%fused_computation | loop fusion | flops 1572864 | bytes 2359296 | tf_op jit(solution)/shard_map/convert_element_type | solution.py:779
  170.6 3.6 %grad_hidden.1.refs_2_ = bf16[512,512]{1,0:T(8,128)(2,1)} custom-call(s32[3]{0:T(128)} %pad_add_fusion.scal, bf16[512,512]{1,0:T(8,128)(2,1)} %get-tuple-element.57.refs_0_, bf16[512,512]{1,0:T(8,128)(2,1)} %bitcast.13.refs_1_, bf16[2,512,512]{2,1,0:T(8,128)(2,1)} %get-tuple-element.68.refs_2_.refs_0_, ...), custom_call_target="tpu_custom_call" | custom-call | flops 2000000000 | bytes 1 | tf_op jit(solution)/shard_map/grad_hidden/pallas_call | solution.py:64
  174.2 1.3 collective-permute-done.32.refs_1_
  175.5 1.2 add_convert_fusion.1
  176.7 0.7 copy.44
  177.4 1.1 pad_maximum_fusion
  (62 shorter events, 0.9 us)
Async XLA Ops:
  2.7 17.3 %collective-permute-start.3 = (f32[8,512]{1,0:T(8,128)}, f32[8,512]{1,0:T(8,128)}, u32[]{:S(2)}, u32[]{:S(2)}) collective-permute-start(f32[8,512]{1,0:T(8,128)} %select_convert_fusion.ids_ref.refs_3_.refs_9_), channel_id=1, source_target_pairs={{0,24},{4,28},{8,0},{12,4},{16,8},{20,12},{24,16},{28,20},{1,25},{... | collective-permute-start | bytes 49160 | tf_op jit(solution)/shard_map/ppermute | solution.py:504
  7.8 12.2 %collective-permute-start.2 = (f32[8,512]{1,0:T(8,128)}, f32[8,512]{1,0:T(8,128)}, u32[]{:S(2)}, u32[]{:S(2)}) collective-permute-start(f32[8,512]{1,0:T(8,128)} %select_convert_fusion.ids_ref.refs_3_.refs_9_), channel_id=1, source_target_pairs={{0,16},{4,20},{8,24},{12,28},{16,0},{20,4},{24,8},{28,12},{1,17},{... | collective-permute-start | bytes 49160 | tf_op jit(solution)/shard_map/ppermute | solution.py:504
  7.8 12.2 %collective-permute-start.1 = (f32[8,512]{1,0:T(8,128)}, f32[8,512]{1,0:T(8,128)}, u32[]{:S(2)}, u32[]{:S(2)}) collective-permute-start(f32[8,512]{1,0:T(8,128)} %select_convert_fusion.ids_ref.refs_3_.refs_9_), channel_id=1, source_target_pairs={{0,8},{4,12},{8,16},{12,20},{16,24},{20,28},{24,0},{28,4},{1,9},{5... | collective-permute-start | bytes 49160 | tf_op jit(solution)/shard_map/ppermute | solution.py:504
  10.7 14.9 %collective-permute-start = (bf16[128,2048]{1,0:T(8,128)(2,1)}, bf16[128,2048]{1,0:T(8,128)(2,1)}, u32[]{:S(2)}, u32[]{:S(2)}) collective-permute-start(bf16[128,2048]{1,0:T(8,128)(2,1)} %constant_dynamic-slice_fusion), channel_id=1, source_target_pairs={{0,8},{4,12},{8,16},{12,20},{16,24},{20,28},{24,0},{28,4},{1,9},{5... | collective-permute-start | bytes 1572872 | tf_op jit(solution)/shard_map/ppermute | solution.py:517
  25.6 15.9 %collective-permute-start.5 = (bf16[128,2048]{1,0:T(8,128)(2,1)}, bf16[128,2048]{1,0:T(8,128)(2,1)}, u32[]{:S(2)}, u32[]{:S(2)}) collective-permute-start(bf16[128,2048]{1,0:T(8,128)(2,1)} %hold.13.refs_3_.refs_0_), channel_id=1, source_target_pairs={{0,2},{1,3},{2,0},{3,1},{4,6},{5,7},{6,4},{7,5},{8,10},{9,11},{10,... | collective-permute-start | bytes 1572872 | tf_op jit(solution)/shard_map/ppermute | solution.py:21
  27.1 14.4 %collective-permute-start.4 = (bf16[128,2048]{1,0:T(8,128)(2,1)}, bf16[128,2048]{1,0:T(8,128)(2,1)}, u32[]{:S(2)}, u32[]{:S(2)}) collective-permute-start(bf16[128,2048]{1,0:T(8,128)(2,1)} %hold.13.refs_3_.refs_0_), channel_id=1, source_target_pairs={{0,8},{4,12},{8,16},{12,20},{16,24},{20,28},{24,0},{28,4},{1,9},{5... | collective-permute-start | bytes 1572872 | tf_op jit(solution)/shard_map/ppermute | solution.py:531
  39.6 3.5 %collective-permute-start.13 = (f32[8,512]{1,0:T(8,128)}, f32[8,512]{1,0:T(8,128)}, u32[]{:S(2)}, u32[]{:S(2)}) collective-permute-start(f32[8,512]{1,0:T(8,128)} %get-tuple-element.62.refs_2_.refs_4_.refs_12_), channel_id=1, source_target_pairs={{0,3},{1,2},{2,1},{3,0},{4,7},{5,6},{6,5},{7,4},{8,11},{9,10},{10,... | collective-permute-start | bytes 49160 | tf_op jit(solution)/shard_map/ppermute | solution.py:21
  39.7 4.1 %collective-permute-start.12 = (f32[8,512]{1,0:T(8,128)}, f32[8,512]{1,0:T(8,128)}, u32[]{:S(2)}, u32[]{:S(2)}) collective-permute-start(f32[8,512]{1,0:T(8,128)} %get-tuple-element.62.refs_2_.refs_4_.refs_12_), channel_id=1, source_target_pairs={{0,2},{1,3},{2,0},{3,1},{4,6},{5,7},{6,4},{7,5},{8,10},{9,11},{10,... | collective-permute-start | bytes 49160 | tf_op jit(solution)/shard_map/ppermute | solution.py:21
  40.2 3.8 %collective-permute-start.11 = (f32[8,512]{1,0:T(8,128)}, f32[8,512]{1,0:T(8,128)}, u32[]{:S(2)}, u32[]{:S(2)}) collective-permute-start(f32[8,512]{1,0:T(8,128)} %get-tuple-element.62.refs_2_.refs_4_.refs_12_), channel_id=1, source_target_pairs={{0,1},{1,0},{2,3},{3,2},{4,5},{5,4},{6,7},{7,6},{8,9},{9,8},{10,11... | collective-permute-start | bytes 49160 | tf_op jit(solution)/shard_map/ppermute | solution.py:21
  41.5 23.0 %collective-permute-start.6 = (bf16[128,2048]{1,0:T(8,128)(2,1)}, bf16[128,2048]{1,0:T(8,128)(2,1)}, u32[]{:S(2)}, u32[]{:S(2)}) collective-permute-start(bf16[128,2048]{1,0:T(8,128)(2,1)} %hold.13.refs_3_.refs_0_), channel_id=1, source_target_pairs={{0,1},{1,0},{2,3},{3,2},{4,5},{5,4},{6,7},{7,6},{8,9},{9,8},{10,11... | collective-permute-start | bytes 1572872 | tf_op jit(solution)/shard_map/ppermute | solution.py:21
  41.5 24.1 %collective-permute-start.7 = (bf16[128,2048]{1,0:T(8,128)(2,1)}, bf16[128,2048]{1,0:T(8,128)(2,1)}, u32[]{:S(2)}, u32[]{:S(2)}) collective-permute-start(bf16[128,2048]{1,0:T(8,128)(2,1)} %get-tuple-element.63.refs_1_.refs_2_), channel_id=1, source_target_pairs={{0,1},{1,0},{2,3},{3,2},{4,5},{5,4},{6,7},{7,6},{8,9},{9,8},{10,11... | collective-permute-start | bytes 1572872 | tf_op jit(solution)/shard_map/ppermute | solution.py:21
  43.1 13.1 %collective-permute-start.10 = (bf16[128,2048]{1,0:T(8,128)(2,1)}, bf16[128,2048]{1,0:T(8,128)(2,1)}, u32[]{:S(2)}, u32[]{:S(2)}) collective-permute-start(bf16[128,2048]{1,0:T(8,128)(2,1)} %get-tuple-element.64.refs_4_), channel_id=1, source_target_pairs={{0,2},{1,3},{2,0},{3,1},{4,6},{5,7},{6,4},{7,5},{8,10},{9,11},{10,... | collective-permute-start | bytes 1572872 | tf_op jit(solution)/shard_map/ppermute | solution.py:21
  43.8 15.7 %collective-permute-start.9 = (bf16[128,2048]{1,0:T(8,128)(2,1)}, bf16[128,2048]{1,0:T(8,128)(2,1)}, u32[]{:S(2)}, u32[]{:S(2)}) collective-permute-start(bf16[128,2048]{1,0:T(8,128)(2,1)} %get-tuple-element.64.refs_4_), channel_id=1, source_target_pairs={{0,8},{4,12},{8,16},{12,20},{16,24},{20,28},{24,0},{28,4},{1,9},{5... | collective-permute-start | bytes 1572872 | tf_op jit(solution)/shard_map/ppermute | solution.py:531
  44.1 21.6 %collective-permute-start.8 = (bf16[128,2048]{1,0:T(8,128)(2,1)}, bf16[128,2048]{1,0:T(8,128)(2,1)}, u32[]{:S(2)}, u32[]{:S(2)}) collective-permute-start(bf16[128,2048]{1,0:T(8,128)(2,1)} %get-tuple-element.64.refs_4_), channel_id=1, source_target_pairs={{0,1},{1,0},{2,3},{3,2},{4,5},{5,4},{6,7},{7,6},{8,9},{9,8},{10,11... | collective-permute-start | bytes 1572872 | tf_op jit(solution)/shard_map/ppermute | solution.py:21
  59.5 6.1 %collective-permute-start.14 = (bf16[128,2048]{1,0:T(8,128)(2,1)}, bf16[128,2048]{1,0:T(8,128)(2,1)}, u32[]{:S(2)}, u32[]{:S(2)}) collective-permute-start(bf16[128,2048]{1,0:T(8,128)(2,1)} %get-tuple-element.69.refs_6_.refs_10_), channel_id=1, source_target_pairs={{0,1},{1,0},{2,3},{3,2},{4,5},{5,4},{6,7},{7,6},{8,9},{9,8},{10,11... | collective-permute-start | bytes 1572872 | tf_op jit(solution)/shard_map/ppermute | solution.py:21
  59.5 24.4 %all-to-all-start = ((bf16[8,64,640]{2,1,0:T(8,128)(2,1)}), bf16[8,64,640]{2,1,0:T(8,128)(2,1)}, u32[]{:S(2)}, u32[]{:S(2)}) async-start(bf16[8,64,640]{2,1,0:T(8,128)(2,1)} %bitcast.9), calls=%async_computation | async-start | bytes 1310720 | tf_op jit(solution)/shard_map/all_to_all | solution.py:610
  63.9 24.3 %collective-permute-start.20 = (bf16[2,512,512]{2,1,0:T(8,128)(2,1)}, bf16[2,512,512]{2,1,0:T(8,128)(2,1)}, u32[]{:S(2)}, u32[]{:S(2)}) collective-permute-start(bf16[2,512,512]{2,1,0:T(8,128)(2,1)} %get-tuple-element.72), channel_id=1, source_target_pairs={{0,1},{1,0},{2,3},{3,2},{4,5},{5,4},{6,7},{7,6},{8,9},{9,8},{10,11... | collective-permute-start | bytes 3145736 | tf_op jit(solution)/shard_map/ppermute | solution.py:21
  64.5 22.3 %collective-permute-start.18 = (bf16[128,2048]{1,0:T(8,128)(2,1)}, bf16[128,2048]{1,0:T(8,128)(2,1)}, u32[]{:S(2)}, u32[]{:S(2)}) collective-permute-start(bf16[128,2048]{1,0:T(8,128)(2,1)} %get-tuple-element.71.refs_0_), channel_id=1, source_target_pairs={{0,2},{1,3},{2,0},{3,1},{4,6},{5,7},{6,4},{7,5},{8,10},{9,11},{10,... | collective-permute-start | bytes 1572872 | tf_op jit(solution)/shard_map/ppermute | solution.py:21
  65.6 25.1 %collective-permute-start.17 = (bf16[128,2048]{1,0:T(8,128)(2,1)}, bf16[128,2048]{1,0:T(8,128)(2,1)}, u32[]{:S(2)}, u32[]{:S(2)}) collective-permute-start(bf16[128,2048]{1,0:T(8,128)(2,1)} %get-tuple-element.71.refs_0_), channel_id=1, source_target_pairs={{0,1},{1,0},{2,3},{3,2},{4,5},{5,4},{6,7},{7,6},{8,9},{9,8},{10,11... | collective-permute-start | bytes 1572872 | tf_op jit(solution)/shard_map/ppermute | solution.py:21
  85.1 0.9 copy-start.6
  85.1 3.1 %copy-start = (bf16[2,512,512]{2,1,0:T(8,128)(2,1)S(1)}, bf16[2,512,512]{2,1,0:T(8,128)(2,1)}, u32[]{:S(2)}) copy-start(bf16[2,512,512]{2,1,0:T(8,128)(2,1)} %get-tuple-element.68.refs_2_.refs_0_) | copy-start | bytes 3145732
  85.1 3.1 %copy-start.1 = (s32[3]{0:T(128)S(1)}, s32[3]{0:T(128)}, u32[]{:S(2)}) copy-start(s32[3]{0:T(128)} %pad_add_fusion.scal) | copy-start | bytes 40
  86.8 3.9 %collective-permute-start.19 = (bf16[128,2048]{1,0:T(8,128)(2,1)}, bf16[128,2048]{1,0:T(8,128)(2,1)}, u32[]{:S(2)}, u32[]{:S(2)}) collective-permute-start(bf16[128,2048]{1,0:T(8,128)(2,1)} %hold.18.refs_2_), channel_id=1, source_target_pairs={{0,1},{1,0},{2,3},{3,2},{4,5},{5,4},{6,7},{7,6},{8,9},{9,8},{10,11... | collective-permute-start | bytes 1572872 | tf_op jit(solution)/shard_map/ppermute | solution.py:21
  87.3 15.5 %collective-permute-start.16 = (bf16[4,128,512]{2,1,0:T(8,128)(2,1)}, bf16[4,128,512]{2,1,0:T(8,128)(2,1)}, u32[]{:S(2)}, u32[]{:S(2)}) collective-permute-start(bf16[4,128,512]{2,1,0:T(8,128)(2,1)} %hold.17.refs_1_.refs_0_.refs_2_), channel_id=1, source_target_pairs={{0,2},{1,3},{2,0},{3,1},{4,6},{5,7},{6,4},{7,5},{8,10},{9,11},{10,... | collective-permute-start | bytes 1572872 | tf_op jit(solution)/shard_map/ppermute | solution.py:21
  88.2 16.3 %collective-permute-start.15 = (bf16[4,128,512]{2,1,0:T(8,128)(2,1)}, bf16[4,128,512]{2,1,0:T(8,128)(2,1)}, u32[]{:S(2)}, u32[]{:S(2)}) collective-permute-start(bf16[4,128,512]{2,1,0:T(8,128)(2,1)} %hold.17.refs_1_.refs_0_.refs_2_), channel_id=1, source_target_pairs={{0,1},{1,0},{2,3},{3,2},{4,5},{5,4},{6,7},{7,6},{8,9},{9,8},{10,11... | collective-permute-start | bytes 1572872 | tf_op jit(solution)/shard_map/ppermute | solution.py:21
  89.9 0.8 copy-start.4
  102.8 2.5 %collective-permute-start.21 = (bf16[4,128,512]{2,1,0:T(8,128)(2,1)}, bf16[4,128,512]{2,1,0:T(8,128)(2,1)}, u32[]{:S(2)}, u32[]{:S(2)}) collective-permute-start(bf16[4,128,512]{2,1,0:T(8,128)(2,1)} %hold.19.refs_2_.refs_12_), channel_id=1, source_target_pairs={{0,1},{1,0},{2,3},{3,2},{4,5},{5,4},{6,7},{7,6},{8,9},{9,8},{10,11... | collective-permute-start | bytes 1572872 | tf_op jit(solution)/shard_map/ppermute | solution.py:21
  103.4 14.4 %collective-permute-start.25 = (bf16[512,512]{1,0:T(8,128)(2,1)}, bf16[512,512]{1,0:T(8,128)(2,1)}, u32[]{:S(2)}, u32[]{:S(2)}) collective-permute-start(bf16[512,512]{1,0:T(8,128)(2,1)} %copy-done.4), channel_id=1, source_target_pairs={{0,2},{1,3},{2,0},{3,1},{4,6},{5,7},{6,4},{7,5},{8,10},{9,11},{10,... | collective-permute-start | bytes 1572872 | tf_op jit(solution)/shard_map/ppermute | solution.py:21
  113.8 4.0 %collective-permute-start.24 = (f32[8,512]{1,0:T(8,128)}, f32[8,512]{1,0:T(8,128)}, u32[]{:S(2)}, u32[]{:S(2)}) collective-permute-start(f32[8,512]{1,0:T(8,128)} %get-tuple-element.76.refs_1_.refs_3_), channel_id=1, source_target_pairs={{0,3},{1,2},{2,1},{3,0},{4,7},{5,6},{6,5},{7,4},{8,11},{9,10},{10,... | collective-permute-start | bytes 49160 | tf_op jit(solution)/shard_map/ppermute | solution.py:21
  115.0 4.1 %collective-permute-start.23 = (f32[8,512]{1,0:T(8,128)}, f32[8,512]{1,0:T(8,128)}, u32[]{:S(2)}, u32[]{:S(2)}) collective-permute-start(f32[8,512]{1,0:T(8,128)} %get-tuple-element.76.refs_1_.refs_3_), channel_id=1, source_target_pairs={{0,2},{1,3},{2,0},{3,1},{4,6},{5,7},{6,4},{7,5},{8,10},{9,11},{10,... | collective-permute-start | bytes 49160 | tf_op jit(solution)/shard_map/ppermute | solution.py:21
  115.9 3.2 %collective-permute-start.22 = (f32[8,512]{1,0:T(8,128)}, f32[8,512]{1,0:T(8,128)}, u32[]{:S(2)}, u32[]{:S(2)}) collective-permute-start(f32[8,512]{1,0:T(8,128)} %get-tuple-element.76.refs_1_.refs_3_), channel_id=1, source_target_pairs={{0,1},{1,0},{2,3},{3,2},{4,5},{5,4},{6,7},{7,6},{8,9},{9,8},{10,11... | collective-permute-start | bytes 49160 | tf_op jit(solution)/shard_map/ppermute | solution.py:21
  124.5 2.8 %collective-permute-start.26 = (f32[128,1920]{1,0:T(8,128)}, f32[128,1920]{1,0:T(8,128)S(1)}, u32[]{:S(2)}, u32[]{:S(2)}) collective-permute-start(f32[128,1920]{1,0:T(8,128)} %get-tuple-element.77.refs_0_.refs_2_), channel_id=1, source_target_pairs={{0,1},{1,0},{2,3},{3,2},{4,5},{5,4},{6,7},{7,6},{8,9},{9,8},{10,11... | collective-permute-start | bytes 2949128 | tf_op jit(solution)/shard_map/ppermute | solution.py:21
  124.5 6.9 %collective-permute-start.30 = (f32[8,1536]{1,0:T(8,128)}, f32[8,1536]{1,0:T(8,128)}, u32[]{:S(2)}, u32[]{:S(2)}) collective-permute-start(f32[8,1536]{1,0:T(8,128)} %get-tuple-element.73.refs_1_.refs_16_.refs_20_), channel_id=1, source_target_pairs={{0,3},{1,2},{2,1},{3,0},{4,7},{5,6},{6,5},{7,4},{8,11},{9,10},{10,... | collective-permute-start | bytes 147464 | tf_op jit(solution)/shard_map/ppermute | solution.py:21
  125.5 5.9 %collective-permute-start.29 = (f32[8,1536]{1,0:T(8,128)}, f32[8,1536]{1,0:T(8,128)}, u32[]{:S(2)}, u32[]{:S(2)}) collective-permute-start(f32[8,1536]{1,0:T(8,128)} %get-tuple-element.73.refs_1_.refs_16_.refs_20_), channel_id=1, source_target_pairs={{0,2},{1,3},{2,0},{3,1},{4,6},{5,7},{6,4},{7,5},{8,10},{9,11},{10,... | collective-permute-start | bytes 147464 | tf_op jit(solution)/shard_map/ppermute | solution.py:21
  126.6 4.7 %collective-permute-start.28 = (f32[8,1536]{1,0:T(8,128)}, f32[8,1536]{1,0:T(8,128)}, u32[]{:S(2)}, u32[]{:S(2)}) collective-permute-start(f32[8,1536]{1,0:T(8,128)} %get-tuple-element.73.refs_1_.refs_16_.refs_20_), channel_id=1, source_target_pairs={{0,1},{1,0},{2,3},{3,2},{4,5},{5,4},{6,7},{7,6},{8,9},{9,8},{10,11... | collective-permute-start | bytes 147464 | tf_op jit(solution)/shard_map/ppermute | solution.py:21
  127.3 0.6 copy-start.2
  127.8 1.2 copy-start.3
  130.5 14.2 %collective-permute-start.27 = (bf16[128,1920]{1,0:T(8,128)(2,1)}, bf16[128,1920]{1,0:T(8,128)(2,1)}, u32[]{:S(2)}, u32[]{:S(2)}) collective-permute-start(bf16[128,1920]{1,0:T(8,128)(2,1)} %add.39.refs_24_.refs_0_), channel_id=1, source_target_pairs={{0,2},{1,3},{2,0},{3,1},{4,6},{5,7},{6,4},{7,5},{8,10},{9,11},{10,... | collective-permute-start | bytes 1474568 | tf_op jit(solution)/shard_map/ppermute | solution.py:21
  143.2 25.0 %collective-permute-start.31 = (bf16[256,1536]{1,0:T(8,128)(2,1)}, bf16[256,1536]{1,0:T(8,128)(2,1)}, u32[]{:S(2)}, u32[]{:S(2)}) collective-permute-start(bf16[256,1536]{1,0:T(8,128)(2,1)} %get-tuple-element.91), channel_id=1, source_target_pairs={{0,4},{4,0},{8,12},{12,8},{16,20},{20,16},{24,28},{28,24},{1,5},{5... | collective-permute-start | bytes 2359304 | tf_op jit(solution)/shard_map/ppermute | solution.py:775
  149.5 21.1 %all-to-all-start.1 = ((bf16[8,64,512]{2,1,0:T(8,128)(2,1)}), bf16[8,64,512]{2,1,0:T(8,128)(2,1)}, u32[]{:S(2)}, u32[]{:S(2)}) async-start(bf16[8,64,512]{2,1,0:T(8,128)(2,1)} %get-tuple-element.86.refs_10_), calls=%async_computation.1 | async-start | bytes 1048576 | tf_op jit(solution)/shard_map/all_to_all | solution.py:679
  160.7 14.7 %collective-permute-start.32 = (bf16[256,640]{1,0:T(8,128)(2,1)}, bf16[256,640]{1,0:T(8,128)(2,1)}, u32[]{:S(2)}, u32[]{:S(2)}) collective-permute-start(bf16[256,640]{1,0:T(8,128)(2,1)} %get-tuple-element.89.refs_5_), channel_id=1, source_target_pairs={{0,4},{4,0},{8,12},{12,8},{16,20},{20,16},{24,28},{28,24},{1,5},{5... | collective-permute-start | bytes 983048 | tf_op jit(solution)/shard_map/ppermute | solution.py:775
  174.2 3.1 %copy-start.5 = (bf16[256,1536]{1,0:T(8,128)(2,1)S(1)}, bf16[256,1536]{1,0:T(8,128)(2,1)}, u32[]{:S(2)}) copy-start(bf16[256,1536]{1,0:T(8,128)(2,1)} %add_convert_fusion) | copy-start | bytes 2359300
